TPU v7x, 32 devices: a whole 2x2x4 slice. The times are simulated.
32 devices in a mesh: layer: 8 (over y, x, core), plane: 4 (over z).
Axes of the slice: x: 2, y: 2, z: 4, core: 2. Of those that a mesh axis runs over, the one named last changes fastest.
Arguments:
- sources: bfloat16 [8, 8, 2, 128, 128], P('layer', 'plane'), may hold values from -6 to 6
- operator_tiles: float32 [8, 96, 2, 128, 128], P('layer', 'plane'), may hold values from -0.109375 to 0.109375
- tile_rows: int32 [8, 96], P('layer', 'plane'), may hold values from 0 to 1, as said below
- tile_cols: int32 [8, 96], P('layer', 'plane'), may hold values from 0 to 5, as said below
- send_blocks: int32 [4, 2, 1], P('plane'), may hold values from 0 to 1
Outputs:
- traces: float32 [8, 8, 2, 128, 128], P('layer', 'plane')
Inputs may be any that keep to these rules, and one draw needn't show every extreme that they name: Entries of tile_rows lie in 0..1; in each layer and plane piece every row block has exactly 12 tiles, and among them at least one reads each of the four parts of the extended trace (arrived blocks, lower neighbour's, upper neighbour's, own trace). Entries of tile_cols index the extended trace of their piece.
All inputs are finite; a program needn't handle non-finite values.
Results may differ from a plain program's by a relative error of at most 0.0003.
Values sent between devices are 32-bit elements; how exact they have to be, the bound alone decides.
No kernel may reach another device: no remote copies, remote signals or barrier semaphores. Data moves between devices by JAX's collectives and lax.ppermute only.
A program may use at most 64 MiB of HBM per device.

v0:
```python
import jax
import jax.numpy as jnp
from jax import lax
from jax.sharding import PartitionSpec as P

TICKS = 3


def from_behind(block, axis, distance):
    devices = range(lax.axis_size(axis))
    route = [(i - distance, i) for i in devices if i - distance in devices]
    return lax.ppermute(block, axis, route)


def assemble_operator(mats, rows, cols, blocks_here, extended_count):
    highest = lax.Precision.HIGHEST
    width = mats.shape[-1]
    tile_count = mats.shape[0]
    slots = rows * extended_count + cols
    target = jnp.arange(blocks_here * extended_count, dtype=jnp.int32)
    selector = (slots[None, :] == target[:, None]).astype(jnp.float32)
    flat = mats.reshape(tile_count, 2 * width * width)
    summed = jnp.dot(selector, flat, precision=highest)
    summed = summed.reshape(blocks_here, extended_count, 2, width, width)
    real_part = summed[:, :, 0]
    imag_part = summed[:, :, 1]
    top_row = jnp.stack([real_part, -imag_part], axis=2)
    bottom_row = jnp.stack([imag_part, real_part], axis=2)
    dense = jnp.stack([top_row, bottom_row], axis=1)
    dense = jnp.transpose(dense, (0, 1, 4, 2, 3, 5))
    return dense.reshape(blocks_here * 2 * width, extended_count * 2 * width)


def per_device(sources, operator_tiles, tile_rows, tile_cols, send_blocks):
    highest = lax.Precision.HIGHEST
    source_now = sources[0].astype(jnp.float32)
    mats = operator_tiles[0]
    rows = tile_rows[0]
    cols = tile_cols[0]
    outgoing = send_blocks[0]
    blocks_here = source_now.shape[0]
    width = source_now.shape[2]
    shot_count = source_now.shape[3]
    listed = outgoing.shape[1]
    extended_count = 2 * blocks_here + 2 * listed
    dense = assemble_operator(mats, rows, cols, blocks_here, extended_count)
    planes = lax.axis_size("plane")
    plane_index = lax.axis_index("plane")
    traces = jnp.zeros_like(source_now)
    for repeat in range(TICKS):
        arrived = from_behind(traces, "layer", 1)
        to_lower = jnp.take(traces, outgoing[0], axis=0)
        to_upper = jnp.take(traces, outgoing[1], axis=0)
        from_lower = from_behind(to_upper, ("layer", "plane"), planes + 1)
        from_lower = jnp.where(plane_index > 0, from_lower, 0.0)
        from_upper = from_behind(to_lower, ("layer", "plane"), planes - 1)
        from_upper = jnp.where(plane_index < planes - 1, from_upper, 0.0)
        extended = jnp.concatenate([arrived, from_lower, from_upper, traces], axis=0)
        stacked = extended.reshape(extended_count * 2 * width, shot_count)
        fresh = jnp.dot(dense, stacked, precision=highest)
        traces = fresh.reshape(blocks_here, 2, width, shot_count) + source_now
    return traces[None]


def solution(mesh):
    placed = (
        P("layer", "plane", None, None, None),
        P("layer", "plane", None, None, None),
        P("layer", "plane"),
        P("layer", "plane"),
        P("plane", None, None),
    )
    return jax.shard_map(
        per_device,
        mesh=mesh,
        in_specs=placed,
        out_specs=P("layer", "plane", None, None, None),
        check_vma=False,
    )
```

profile of v0, /device:TPU:3, one launch (start us, length us, event | category | flops | bytes accessed | tf_op | source)
XLA Modules:
  0.0 68.8 jit_solution(3599448387616795104)
XLA Ops:
  0.0 1.3 %fusion.55 = (s32[1,1,1]{1,2,0:T(1,128)}, s32[1,1,1]{1,2,0:T(1,128)}) fusion(s32[1,2,1]{1,2,0:T(1,128)} %param.11), kind=kLoop, calls=%fused_computation.60 | loop fusion | bytes 16 | tf_op jit(solution)/shard_map/slice | solution.py:53
  3.3 5.2 %collective-permute-start.2 = (f32[1,2,128,128]{3,2,1,0:T(8,128)S(1)}, f32[1,2,128,128]{3,2,1,0:T(8,128)}, u32[]{:S(2)}, u32[]{:S(2)}) collective-permute-start(f32[1,2,128,128]{3,2,1,0:T(8,128)S(1)} %broadcast.66), channel_id=1, source_target_pairs={{0,3},{1,4},{2,5},{3,6},{4,7},{5,8},{6,9},{7,10},{8,11},{9,12},{10... | collective-permute-start | bytes 393224 | tf_op jit(solution)/shard_map/ppermute | solution.py:12
  10.4 0.7 broadcast.61
  11.1 1.9 %collective-permute-start.1 = (f32[1,2,128,128]{3,2,1,0:T(8,128)}, f32[1,2,128,128]{3,2,1,0:T(8,128)}, u32[]{:S(2)}, u32[]{:S(2)}) collective-permute-start(f32[1,2,128,128]{3,2,1,0:T(8,128)} %broadcast.61), channel_id=1, source_target_pairs={{0,5},{1,6},{2,7},{3,8},{4,9},{5,10},{6,11},{7,12},{8,13},{9,14},{... | collective-permute-start | bytes 393224 | tf_op jit(solution)/shard_map/ppermute | solution.py:12
  13.1 4.0 %collective-permute-start = (f32[2,2,128,128]{3,2,1,0:T(8,128)S(1)}, f32[2,2,128,128]{3,2,1,0:T(8,128)}, u32[]{:S(2)}, u32[]{:S(2)}) collective-permute-start(f32[2,2,128,128]{3,2,1,0:T(8,128)S(1)} %broadcast_in_dim.26), channel_id=1, source_target_pairs={{0,4},{4,8},{8,12},{12,16},{16,20},{20,24},{24,28},{1,5},{5,9},{9,... | collective-permute-start | bytes 786440 | tf_op jit(solution)/shard_map/ppermute | solution.py:12
  17.0 2.9 %reshape_squeeze.3 = f32[24,32768]{1,0:T(8,128)S(1)} reshape(f32[1,24,2,128,128]{4,3,2,1,0:T(8,128)} %param.8) | data formatting | bytes 6291456 | tf_op jit(solution)/shard_map/reshape;squeeze | solution.py:22
  19.9 0.0 copy-start.1
  19.9 0.0 copy-start.2
  20.0 0.5 copy.20
  20.5 0.1 copy-done.1
  20.6 0.0 copy-done.2
  20.6 3.4 %fusion = f32[2,6,2,128,128]{4,1,3,2,0:T(8,128)S(1)} fusion(f32[2,128,128,24]{2,1,0,3:T(8,128)S(1)} %bitcast.80, s32[2,6]{1,0:T(2,128)S(1)} %multiply_add_fusion, s32[24]{0:T(128)S(1)} %add_bitcast_fusion), kind=kOutput, calls=%fused_computation.1 | convolution fusion | flops 113246496 | bytes 4718736 | tf_op jit(solution)/shard_map/dot_general | solution.py:23
  24.0 0.2 slice_negate_fusion
  24.2 0.3 maximum_bitcast_fusion.1
  24.6 0.0 copy-start
  24.6 0.4 maximum_bitcast_fusion
  25.0 0.9 %broadcast_select_fusion.4 = f32[1,2,128,128]{3,2,1,0:T(8,128)S(1)} fusion(f32[1,2,128,128]{3,2,1,0:T(8,128)} %collective-permute-done.2, pred[]{:T(512)S(6)} %lt.8), kind=kLoop, calls=%fused_computation.48 | loop fusion | flops 32768 | bytes 262145 | tf_op jit(solution)/shard_map/jit(_where)/select_n | solution.py:57
  25.9 0.0 collective-permute-done.1
  25.9 0.0 collective-permute-done
  26.0 3.7 %fusion.18 = f32[2,2,128,128]{3,2,1,0:T(8,128)S(1)} fusion(f32[2,2,128,6,2,128]{5,3,2,4,0,1:T(8,128)S(1)} %maximum_bitcast_fusion, f32[2,2,128,128]{3,2,1,0:T(8,128)S(1)} %broadcast_in_dim.26, f32[1,2,128,128]{3,2,1,0:T(8,128)S(1)} %broadcast_select_fusion.4, f32[1,2,128,128]{3,2,1,0:T(8,128)S(1)} %broadcast_select_fusion.5, ...), kind=kOutput, calls=%fused_computation.15 | convolution fusion | flops 1208680448 | bytes 4325376 | tf_op jit(solution)/shard_map/dot_general | solution.py:60
  29.7 6.4 %collective-permute-start.5 = (f32[1,2,128,128]{3,2,1,0:T(8,128)S(1)}, f32[1,2,128,128]{3,2,1,0:T(8,128)S(1)}, u32[]{:S(2)}, u32[]{:S(2)}) collective-permute-start(f32[1,2,128,128]{3,2,1,0:T(8,128)S(1)} %get-tuple-element.25), channel_id=1, source_target_pairs={{0,3},{1,4},{2,5},{3,6},{4,7},{5,8},{6,9},{7,10},{8,11},{9,12},{10... | collective-permute-start | bytes 393224 | tf_op jit(solution)/shard_map/ppermute | solution.py:12
  36.1 2.2 %collective-permute-start.3 = (f32[2,2,128,128]{3,2,1,0:T(8,128)S(1)}, f32[2,2,128,128]{3,2,1,0:T(8,128)S(1)}, u32[]{:S(2)}, u32[]{:S(2)}) collective-permute-start(f32[2,2,128,128]{3,2,1,0:T(8,128)S(1)} %fusion.18), channel_id=1, source_target_pairs={{0,4},{4,8},{8,12},{12,16},{16,20},{20,24},{24,28},{1,5},{5,9},{9,... | collective-permute-start | bytes 786440 | tf_op jit(solution)/shard_map/ppermute | solution.py:12
  38.3 1.9 %collective-permute-start.4 = (f32[1,2,128,128]{3,2,1,0:T(8,128)S(1)}, f32[1,2,128,128]{3,2,1,0:T(8,128)S(1)}, u32[]{:S(2)}, u32[]{:S(2)}) collective-permute-start(f32[1,2,128,128]{3,2,1,0:T(8,128)S(1)} %get-tuple-element.24), channel_id=1, source_target_pairs={{0,5},{1,6},{2,7},{3,8},{4,9},{5,10},{6,11},{7,12},{8,13},{9,14},{... | collective-permute-start | bytes 393224 | tf_op jit(solution)/shard_map/ppermute | solution.py:12
  40.3 7.5 %collective-permute-done.4 = f32[1,2,128,128]{3,2,1,0:T(8,128)S(1)} collective-permute-done((f32[1,2,128,128]{3,2,1,0:T(8,128)S(1)}, f32[1,2,128,128]{3,2,1,0:T(8,128)S(1)}, u32[]{:S(2)}, u32[]{:S(2)}) %collective-permute-start.4) | collective-permute-done | bytes 131104 | tf_op jit(solution)/shard_map/ppermute | solution.py:12
  47.8 2.8 %fusion.21 = f32[2,2,128,128]{3,2,1,0:T(8,128)S(1)} fusion(f32[2,2,128,6,2,128]{5,3,2,4,0,1:T(8,128)S(1)} %maximum_bitcast_fusion, f32[2,2,128,128]{3,2,1,0:T(8,128)S(1)} %fusion.18, f32[1,2,128,128]{3,2,1,0:T(8,128)S(1)} %broadcast_select_fusion.2, f32[1,2,128,128]{3,2,1,0:T(8,128)S(1)} %broadcast_select_fusion.3, ...), kind=kOutput, calls=%fused_computation.16 | convolution fusion | flops 1208680448 | bytes 4325376 | tf_op jit(solution)/shard_map/dot_general | solution.py:60
  50.6 1.9 %collective-permute-start.8 = (f32[1,2,128,128]{3,2,1,0:T(8,128)S(1)}, f32[1,2,128,128]{3,2,1,0:T(8,128)S(1)}, u32[]{:S(2)}, u32[]{:S(2)}) collective-permute-start(f32[1,2,128,128]{3,2,1,0:T(8,128)S(1)} %get-tuple-element.23), channel_id=1, source_target_pairs={{0,3},{1,4},{2,5},{3,6},{4,7},{5,8},{6,9},{7,10},{8,11},{9,12},{10... | collective-permute-start | bytes 393224 | tf_op jit(solution)/shard_map/ppermute | solution.py:12
  52.5 3.1 %collective-permute-start.6 = (f32[2,2,128,128]{3,2,1,0:T(8,128)S(1)}, f32[2,2,128,128]{3,2,1,0:T(8,128)S(1)}, u32[]{:S(2)}, u32[]{:S(2)}) collective-permute-start(f32[2,2,128,128]{3,2,1,0:T(8,128)S(1)} %fusion.21), channel_id=1, source_target_pairs={{0,4},{4,8},{8,12},{12,16},{16,20},{20,24},{24,28},{1,5},{5,9},{9,... | collective-permute-start | bytes 786440 | tf_op jit(solution)/shard_map/ppermute | solution.py:12
  55.6 1.9 %collective-permute-start.7 = (f32[1,2,128,128]{3,2,1,0:T(8,128)S(1)}, f32[1,2,128,128]{3,2,1,0:T(8,128)S(1)}, u32[]{:S(2)}, u32[]{:S(2)}) collective-permute-start(f32[1,2,128,128]{3,2,1,0:T(8,128)S(1)} %get-tuple-element.22), channel_id=1, source_target_pairs={{0,5},{1,6},{2,7},{3,8},{4,9},{5,10},{6,11},{7,12},{8,13},{9,14},{... | collective-permute-start | bytes 393224 | tf_op jit(solution)/shard_map/ppermute | solution.py:12
  57.5 0.9 %collective-permute-done.8 = f32[1,2,128,128]{3,2,1,0:T(8,128)S(1)} collective-permute-done((f32[1,2,128,128]{3,2,1,0:T(8,128)S(1)}, f32[1,2,128,128]{3,2,1,0:T(8,128)S(1)}, u32[]{:S(2)}, u32[]{:S(2)}) %collective-permute-start.8) | collective-permute-done | bytes 131104 | tf_op jit(solution)/shard_map/ppermute | solution.py:12
  58.5 6.8 %collective-permute-done.7 = f32[1,2,128,128]{3,2,1,0:T(8,128)S(1)} collective-permute-done((f32[1,2,128,128]{3,2,1,0:T(8,128)S(1)}, f32[1,2,128,128]{3,2,1,0:T(8,128)S(1)}, u32[]{:S(2)}, u32[]{:S(2)}) %collective-permute-start.7) | collective-permute-done | bytes 131104 | tf_op jit(solution)/shard_map/ppermute | solution.py:12
  65.3 0.0 collective-permute-done.6
  65.3 3.5 %fusion.27 = f32[1,2,2,128,128]{4,3,2,1,0:T(8,128)} fusion(f32[2,2,128,6,2,128]{5,3,2,4,0,1:T(8,128)S(1)} %maximum_bitcast_fusion, f32[2,2,128,128]{3,2,1,0:T(8,128)S(1)} %fusion.21, f32[1,2,128,128]{3,2,1,0:T(8,128)S(1)} %broadcast_select_fusion, f32[1,2,128,128]{3,2,1,0:T(8,128)S(1)} %broadcast_select_fusion.1, ...), kind=kOutput, calls=%fused_computation.18 | convolution fusion | flops 1208680448 | bytes 4325376 | tf_op jit(solution)/shard_map/dot_general | solution.py:60
  (15 shorter events, 0.2 us)
Async XLA Ops:
  3.3 21.7 %collective-permute-start.2 = (f32[1,2,128,128]{3,2,1,0:T(8,128)S(1)}, f32[1,2,128,128]{3,2,1,0:T(8,128)}, u32[]{:S(2)}, u32[]{:S(2)}) collective-permute-start(f32[1,2,128,128]{3,2,1,0:T(8,128)S(1)} %broadcast.66), channel_id=1, source_target_pairs={{0,3},{1,4},{2,5},{3,6},{4,7},{5,8},{6,9},{7,10},{8,11},{9,12},{10... | collective-permute-start | bytes 393224 | tf_op jit(solution)/shard_map/ppermute | solution.py:12
  11.1 14.8 %collective-permute-start.1 = (f32[1,2,128,128]{3,2,1,0:T(8,128)}, f32[1,2,128,128]{3,2,1,0:T(8,128)}, u32[]{:S(2)}, u32[]{:S(2)}) collective-permute-start(f32[1,2,128,128]{3,2,1,0:T(8,128)} %broadcast.61), channel_id=1, source_target_pairs={{0,5},{1,6},{2,7},{3,8},{4,9},{5,10},{6,11},{7,12},{8,13},{9,14},{... | collective-permute-start | bytes 393224 | tf_op jit(solution)/shard_map/ppermute | solution.py:12
  13.1 12.9 %collective-permute-start = (f32[2,2,128,128]{3,2,1,0:T(8,128)S(1)}, f32[2,2,128,128]{3,2,1,0:T(8,128)}, u32[]{:S(2)}, u32[]{:S(2)}) collective-permute-start(f32[2,2,128,128]{3,2,1,0:T(8,128)S(1)} %broadcast_in_dim.26), channel_id=1, source_target_pairs={{0,4},{4,8},{8,12},{12,16},{16,20},{20,24},{24,28},{1,5},{5,9},{9,... | collective-permute-start | bytes 786440 | tf_op jit(solution)/shard_map/ppermute | solution.py:12
  19.9 0.7 copy-start.1
  19.9 0.7 copy-start.2
  24.6 1.4 %copy-start = (bf16[1,2,2,128,128]{4,3,2,1,0:T(8,128)(2,1)S(1)}, bf16[1,2,2,128,128]{4,3,2,1,0:T(8,128)(2,1)}, u32[]{:S(2)}) copy-start(bf16[1,2,2,128,128]{4,3,2,1,0:T(8,128)(2,1)} %param.7) | copy-start | bytes 393220
  29.7 10.5 %collective-permute-start.5 = (f32[1,2,128,128]{3,2,1,0:T(8,128)S(1)}, f32[1,2,128,128]{3,2,1,0:T(8,128)S(1)}, u32[]{:S(2)}, u32[]{:S(2)}) collective-permute-start(f32[1,2,128,128]{3,2,1,0:T(8,128)S(1)} %get-tuple-element.25), channel_id=1, source_target_pairs={{0,3},{1,4},{2,5},{3,6},{4,7},{5,8},{6,9},{7,10},{8,11},{9,12},{10... | collective-permute-start | bytes 393224 | tf_op jit(solution)/shard_map/ppermute | solution.py:12
  36.1 11.7 %collective-permute-start.3 = (f32[2,2,128,128]{3,2,1,0:T(8,128)S(1)}, f32[2,2,128,128]{3,2,1,0:T(8,128)S(1)}, u32[]{:S(2)}, u32[]{:S(2)}) collective-permute-start(f32[2,2,128,128]{3,2,1,0:T(8,128)S(1)} %fusion.18), channel_id=1, source_target_pairs={{0,4},{4,8},{8,12},{12,16},{16,20},{20,24},{24,28},{1,5},{5,9},{9,... | collective-permute-start | bytes 786440 | tf_op jit(solution)/shard_map/ppermute | solution.py:12
  38.3 9.5 %collective-permute-start.4 = (f32[1,2,128,128]{3,2,1,0:T(8,128)S(1)}, f32[1,2,128,128]{3,2,1,0:T(8,128)S(1)}, u32[]{:S(2)}, u32[]{:S(2)}) collective-permute-start(f32[1,2,128,128]{3,2,1,0:T(8,128)S(1)} %get-tuple-element.24), channel_id=1, source_target_pairs={{0,5},{1,6},{2,7},{3,8},{4,9},{5,10},{6,11},{7,12},{8,13},{9,14},{... | collective-permute-start | bytes 393224 | tf_op jit(solution)/shard_map/ppermute | solution.py:12
  50.6 7.8 %collective-permute-start.8 = (f32[1,2,128,128]{3,2,1,0:T(8,128)S(1)}, f32[1,2,128,128]{3,2,1,0:T(8,128)S(1)}, u32[]{:S(2)}, u32[]{:S(2)}) collective-permute-start(f32[1,2,128,128]{3,2,1,0:T(8,128)S(1)} %get-tuple-element.23), channel_id=1, source_target_pairs={{0,3},{1,4},{2,5},{3,6},{4,7},{5,8},{6,9},{7,10},{8,11},{9,12},{10... | collective-permute-start | bytes 393224 | tf_op jit(solution)/shard_map/ppermute | solution.py:12
  52.5 12.8 %collective-permute-start.6 = (f32[2,2,128,128]{3,2,1,0:T(8,128)S(1)}, f32[2,2,128,128]{3,2,1,0:T(8,128)S(1)}, u32[]{:S(2)}, u32[]{:S(2)}) collective-permute-start(f32[2,2,128,128]{3,2,1,0:T(8,128)S(1)} %fusion.21), channel_id=1, source_target_pairs={{0,4},{4,8},{8,12},{12,16},{16,20},{20,24},{24,28},{1,5},{5,9},{9,... | collective-permute-start | bytes 786440 | tf_op jit(solution)/shard_map/ppermute | solution.py:12
  55.6 9.7 %collective-permute-start.7 = (f32[1,2,128,128]{3,2,1,0:T(8,128)S(1)}, f32[1,2,128,128]{3,2,1,0:T(8,128)S(1)}, u32[]{:S(2)}, u32[]{:S(2)}) collective-permute-start(f32[1,2,128,128]{3,2,1,0:T(8,128)S(1)} %get-tuple-element.22), channel_id=1, source_target_pairs={{0,5},{1,6},{2,7},{3,8},{4,9},{5,10},{6,11},{7,12},{8,13},{9,14},{... | collective-permute-start | bytes 393224 | tf_op jit(solution)/shard_map/ppermute | solution.py:12
where the time goes:
time: 69.4 us; the launch traced here: 68.8 us
  starting transfers between devices  28.5 us (41%)
  waiting for transfers between devices  15.3 us (22%)
  matrix products  13.3 us (19%)
  local copies, waits for them, and re-layouts  5.55 us (8%)
  between operations  4.16 us (6%)
  other arithmetic  1.99 us (3%)
    ppermute x9, starting transfers between devices, from_behind(): return lax.ppermute(block, axis, route)  28.5 us
    ppermute x9, waiting for transfers between devices, from_behind(): return lax.ppermute(block, axis, route)  15.3 us
    dot_general x3, matrix products, per_device(): fresh = jnp.dot(dense, stacked, precision=highest)  9.91 us
    dot_general x1, matrix products, assemble_operator(): summed = jnp.dot(selector, flat, precision=highest)  3.37 us
    another operation x1, local copies, waits for them, and re-layouts, assemble_operator(): flat = mats.reshape(tile_count, 2 * width * width)  2.88 us
  transfers between devices with their start and end apart: 9, of which 3 were waited for; matrix products, arithmetic and copies ran while one was open for 14% of the time, Pallas kernels for 0%

commit v1 on v0

v1 whole, which is shorter than its diff:
```python
import jax
import jax.numpy as jnp
from jax import lax
from jax.experimental import pallas as pl
from jax.experimental.pallas import tpu as pltpu
from jax.sharding import PartitionSpec as P

F32 = jnp.float32
BF16 = jnp.bfloat16
LIMIT = 40 * 1024 * 1024


def even_pair(p, planes):
    q = p + 1 if p % 2 == 0 else p - 1
    return q if q < planes else p


def odd_pair(p, planes):
    q = p - 1 if p % 2 == 0 else p + 1
    return q if 0 <= q < planes else p


def same(p, planes):
    return p


def to_next_layer(block, partner):
    layers = lax.axis_size("layer")
    planes = lax.axis_size("plane")
    route = [
        (l * planes + p, (l + 1) % layers * planes + partner(p, planes))
        for l in range(layers)
        for p in range(planes)
    ]
    return lax.ppermute(block, ("layer", "plane"), route)


def choose(send_ref, blocks_ref, even_ref, odd_ref):
    is_odd = lax.axis_index("plane") % 2
    listed = even_ref.shape[0]
    for k in range(listed):
        even_ref[k] = blocks_ref[send_ref[(1 - is_odd) * listed + k]].astype(F32)
        odd_ref[k] = blocks_ref[send_ref[is_odd * listed + k]].astype(F32)


def split(value):
    high = value.astype(BF16)
    return high, (value - high.astype(F32)).astype(BF16)


def operand(blocks):
    rows = []
    for real, imag in blocks:
        rows.append(jnp.concatenate([real, imag], axis=1))
        rows.append(jnp.concatenate([-imag, real], axis=1))
    return jnp.concatenate(rows, axis=0)


def product(a, b):
    return jnp.dot(a, b, preferred_element_type=F32)


def widen_kernel(send_ref, source_ref, all_ref, even_ref, odd_ref):
    all_ref[...] = source_ref[...].astype(F32)
    choose(send_ref, source_ref, even_ref, odd_ref)


def prepare_kernel(rows_ref, cols_ref, tiles_ref, source_ref, high_ref, low_ref, own_ref, total):
    tile_count, _, width, _ = tiles_ref.shape
    blocks_here = source_ref.shape[0]
    extended = total.shape[0] // blocks_here
    listed = (extended - 2 * blocks_here) // 2
    layer = lax.axis_index("layer")
    plane = lax.axis_index("plane")
    planes = lax.axis_size("plane")
    is_odd = plane % 2
    total[...] = jnp.zeros_like(total)

    def add(t, carry):
        col = cols_ref[t]
        is_lower = (col >= blocks_here) & (col < blocks_here + listed)
        is_upper = (col >= blocks_here + listed) & (col < blocks_here + 2 * listed)
        place = jnp.where(is_lower & (is_odd == 0), col + listed, col)
        place = jnp.where(is_upper & (is_odd == 0), col - listed, place)
        slot = rows_ref[t] * extended + place
        total[slot, :, :width] += tiles_ref[t, 0]
        total[slot, :, width:] += tiles_ref[t, 1]
        return carry

    lax.fori_loop(0, tile_count, add, 0, unroll=4)
    has_layer = layer > 0
    has_next = plane + 1 < planes
    has_even = has_layer & ((is_odd == 1) | has_next)
    has_odd = has_layer & jnp.where(is_odd == 1, has_next, plane > 0)
    for c in range(extended):
        keep = None
        if c < blocks_here:
            keep = has_layer
        elif c < blocks_here + listed:
            keep = has_even
        elif c < blocks_here + 2 * listed:
            keep = has_odd
        for r in range(blocks_here):
            value = total[r * extended + c]
            if keep is not None:
                value = jnp.where(keep, value, 0.0)
            high, low = split(value)
            here = (slice(r * width, (r + 1) * width), slice(c * 2 * width, (c + 1) * 2 * width))
            high_ref[here] = high
            low_ref[here] = low
    first = (extended - blocks_here) * 2 * width
    own = operand([(source_ref[b, 0], source_ref[b, 1]) for b in range(blocks_here)])
    result = product(high_ref[:, first:], own) + product(low_ref[:, first:], own)
    shots = source_ref.shape[3]
    for b in range(blocks_here):
        for part in range(2):
            own_ref[b, part] = (
                result[b * width : (b + 1) * width, part * shots : (part + 1) * shots]
                + source_ref[b, part].astype(F32)
            )


def gather(all_ref, even_ref, odd_ref):
    return [
        (ref[b, 0], ref[b, 1])
        for ref in (all_ref, even_ref, odd_ref)
        for b in range(ref.shape[0])
    ]


def store(result, base_ref, out_ref):
    blocks, _, width, shots = base_ref.shape
    for b in range(blocks):
        for part in range(2):
            out_ref[b, part] = (
                result[b * width : (b + 1) * width, part * shots : (part + 1) * shots]
                + base_ref[b, part].astype(F32)
            )


def middle_kernel(send_ref, high_ref, low_ref, own_ref, all_ref, even_ref, odd_ref, new_ref, new_even_ref, new_odd_ref):
    blocks = [(x.astype(BF16), y.astype(BF16)) for x, y in gather(all_ref, even_ref, odd_ref)]
    stacked = operand(blocks)
    depth = stacked.shape[0]
    result = product(high_ref[:, :depth], stacked) + product(low_ref[:, :depth], stacked)
    store(result, own_ref, new_ref)
    choose(send_ref, new_ref, new_even_ref, new_odd_ref)


def three_products(high_ref, low_ref, columns, blocks):
    halves = [(split(x), split(y)) for x, y in blocks]
    high = operand([(x[0], y[0]) for x, y in halves])
    low = operand([(x[1], y[1]) for x, y in halves])
    left = high_ref[:, columns]
    return product(left, high) + product(low_ref[:, columns], high) + product(left, low)


def own_kernel(high_ref, low_ref, source_ref, trace_ref, own_ref):
    blocks = [(trace_ref[b, 0], trace_ref[b, 1]) for b in range(trace_ref.shape[0])]
    depth = 2 * trace_ref.shape[2] * len(blocks)
    result = three_products(high_ref, low_ref, slice(high_ref.shape[1] - depth, None), blocks)
    store(result, source_ref, own_ref)


def last_kernel(high_ref, low_ref, own_ref, all_ref, even_ref, odd_ref, out_ref):
    blocks = gather(all_ref, even_ref, odd_ref)
    depth = 2 * all_ref.shape[2] * len(blocks)
    result = three_products(high_ref, low_ref, slice(0, depth), blocks)
    store(result, own_ref, out_ref)


def call(kernel, ins, outs, flops, scratch=()):
    moved = sum(x.size * x.dtype.itemsize for x in (*ins, *outs))
    smem = pl.BlockSpec(memory_space=pltpu.SMEM)
    vmem = pl.BlockSpec(memory_space=pltpu.VMEM)
    return pl.pallas_call(
        kernel,
        out_shape=outs,
        in_specs=[smem if x.dtype == jnp.int32 else vmem for x in ins],
        out_specs=[vmem] * len(outs),
        scratch_shapes=scratch,
        compiler_params=pltpu.CompilerParams(vmem_limit_bytes=LIMIT),
        cost_estimate=pl.CostEstimate(flops=flops, bytes_accessed=moved, transcendentals=0),
    )(*ins)


def per_device(sources, operator_tiles, tile_rows, tile_cols, send_blocks):
    source = sources[0]
    tiles = operator_tiles[0]
    send = send_blocks.reshape(-1)
    blocks, _, width, shots = source.shape
    listed = send_blocks.shape[2]
    extended = 2 * blocks + 2 * listed
    shape = jax.ShapeDtypeStruct
    trace = shape(source.shape, F32)
    part = shape((listed, 2, width, shots), F32)
    half = shape((blocks * width, extended * 2 * width), BF16)
    flops = 2 * blocks * width * extended * 2 * width * 2 * shots

    def exchange(whole, even, odd):
        return (
            to_next_layer(whole, same),
            to_next_layer(even, even_pair),
            to_next_layer(odd, odd_pair),
        )

    arrived = exchange(*call(widen_kernel, (send, source), (trace, part, part), 0))
    high, low, own = call(
        prepare_kernel,
        (tile_rows[0], tile_cols[0], tiles, source),
        (half, half, trace),
        flops,
        [pltpu.VMEM((blocks * extended, width, 2 * width), F32)],
    )
    traces, even, odd = call(
        middle_kernel, (send, high, low, own, *arrived), (trace, part, part), 2 * flops
    )
    arrived = exchange(traces, even, odd)
    (own,) = call(own_kernel, (high, low, source, traces), (trace,), flops)
    (out,) = call(last_kernel, (high, low, own, *arrived), (trace,), 2 * flops)
    return out[None]


def solution(mesh):
    placed = (
        P("layer", "plane", None, None, None),
        P("layer", "plane", None, None, None),
        P("layer", "plane"),
        P("layer", "plane"),
        P("plane", None, None),
    )
    return jax.shard_map(
        per_device,
        mesh=mesh,
        in_specs=placed,
        out_specs=P("layer", "plane", None, None, None),
        check_vma=False,
    )
```

time: 69.4 us -> 24.5 us (0.35)
  the two profiles are of different devices: /device:TPU:3 before, /device:TPU:0 now
where the time goes in v1:
time: 24.5 us; the launch traced here: 24.3 us
  starting transfers between devices  9.12 us (37%)
  local copies, waits for them, and re-layouts  5.68 us (23%)
  waiting for transfers between devices  4.84 us (20%)
  Pallas kernels  4.58 us (19%)
    ppermute x6, starting transfers between devices, to_next_layer(): return lax.ppermute(block, ('layer', 'plane'), route)  9.12 us
    unnamed x14, local copies, waits for them, and re-layouts  5.68 us
    ppermute x6, waiting for transfers between devices, to_next_layer(): return lax.ppermute(block, ('layer', 'plane'), route)  4.84 us
    pallas_call x5, Pallas kernels, call(): pl.pallas_call(kernel, out_shape=outs, in_specs=[smem if x.dtype == jnp.i...  4.58 us
  transfers between devices with their start and end apart: 6, of which 3 were waited for; matrix products, arithmetic and copies ran while one was open for 0% of the time, Pallas kernels for 7%

profile of v1, /device:TPU:0, one launch (start us, length us, event | category | flops | bytes accessed | tf_op | source)
XLA Modules:
  0.0 24.3 jit_solution(13410739284319652947)
XLA Ops:
  0.0 0.0 copy-start.4
  0.0 0.0 copy-start.1
  0.0 0.9 %copy-done.1 = bf16[1,2,2,128,128]{4,3,2,1,0:T(8,128)(2,1)S(1)} copy-done((bf16[1,2,2,128,128]{4,3,2,1,0:T(8,128)(2,1)S(1)}, bf16[1,2,2,128,128]{4,3,2,1,0:T(8,128)(2,1)}, u32[]{:S(2)}) %copy-start.1) | copy-done | bytes 131096
  0.9 0.0 copy-start.3
  0.9 0.7 %copy-done.3 = s32[1,2,1]{1,2,0:T(1,128)S(1)} copy-done((s32[1,2,1]{1,2,0:T(1,128)S(1)}, s32[1,2,1]{1,2,0:T(1,128)}, u32[]{:S(2)}) %copy-start.3) | copy-done | bytes 32
  1.6 0.6 %shard_map.56 = (f32[2,2,128,128]{3,2,1,0:T(8,128)S(1)}, f32[1,2,128,128]{3,2,1,0:T(8,128)S(1)}, f32[1,2,128,128]{3,2,1,0:T(8,128)S(1)}) custom-call(s32[2]{0:T(128)S(1)} %bitcast.10, bf16[2,2,128,128]{3,2,1,0:T(8,128)(2,1)S(1)} %bitcast.7), custom_call_target="tpu_custom_call" | custom-call | bytes 655368 | tf_op jit(solution)/shard_map/pallas_call | solution.py:176
  2.2 0.5 %collective-permute-start = (f32[2,2,128,128]{3,2,1,0:T(8,128)S(1)}, f32[2,2,128,128]{3,2,1,0:T(8,128)S(1)}, u32[]{:S(2)}, u32[]{:S(2)}) collective-permute-start(f32[2,2,128,128]{3,2,1,0:T(8,128)S(1)} %get-tuple-element.17), channel_id=1, source_target_pairs={{0,4},{1,5},{2,6},{3,7},{4,8},{5,9},{6,10},{7,11},{8,12},{9,13},{1... | collective-permute-start | bytes 786440 | tf_op jit(solution)/shard_map/ppermute | solution.py:35
  2.7 3.8 %collective-permute-start.1 = (f32[1,2,128,128]{3,2,1,0:T(8,128)S(1)}, f32[1,2,128,128]{3,2,1,0:T(8,128)S(1)}, u32[]{:S(2)}, u32[]{:S(2)}) collective-permute-start(f32[1,2,128,128]{3,2,1,0:T(8,128)S(1)} %get-tuple-element.18), channel_id=1, source_target_pairs={{0,5},{1,4},{2,7},{3,6},{4,9},{5,8},{6,11},{7,10},{8,13},{9,12},{1... | collective-permute-start | bytes 393224 | tf_op jit(solution)/shard_map/ppermute | solution.py:35
  6.4 0.0 collective-permute-start.2
  6.5 0.0 copy-start
  6.5 1.9 %copy-done = f32[1,24,2,128,128]{4,3,2,1,0:T(8,128)S(1)} copy-done((f32[1,24,2,128,128]{4,3,2,1,0:T(8,128)S(1)}, f32[1,24,2,128,128]{4,3,2,1,0:T(8,128)}, u32[]{:S(2)}) %copy-start) | copy-done | bytes 3145752
  8.3 0.0 copy-start.2
  8.3 0.9 %copy-done.2 = bf16[1,2,2,128,128]{4,3,2,1,0:T(8,128)(2,1)S(1)} copy-done((bf16[1,2,2,128,128]{4,3,2,1,0:T(8,128)(2,1)S(1)}, bf16[1,2,2,128,128]{4,3,2,1,0:T(8,128)(2,1)}, u32[]{:S(2)}) %copy-start.2) | copy-done | bytes 131096
  9.2 0.0 copy-start.5
  9.2 0.7 %copy-done.5 = s32[1,24]{1,0:T(1,128)S(1)} copy-done((s32[1,24]{1,0:T(1,128)S(1)}, s32[1,24]{1,0:T(1,128)}, u32[]{:S(2)}) %copy-start.5) | copy-done | bytes 120
  9.9 0.0 copy-start.6
  9.9 0.7 %copy-done.6 = s32[1,24]{1,0:T(1,128)S(1)} copy-done((s32[1,24]{1,0:T(1,128)S(1)}, s32[1,24]{1,0:T(1,128)}, u32[]{:S(2)}) %copy-start.6) | copy-done | bytes 120
  10.6 1.4 %shard_map.55 = (bf16[256,1536]{1,0:T(8,128)(2,1)S(1)}, bf16[256,1536]{1,0:T(8,128)(2,1)S(1)}, f32[2,2,128,128]{3,2,1,0:T(8,128)S(1)}) custom-call(s32[24]{0:T(128)S(1)} %bitcast.12, s32[24]{0:T(128)S(1)} %bitcast.13, f32[24,2,128,128]{3,2,1,0:T(8,128)S(1)} %bitcast.6, bf16[2,2,128,128]{3,2,1,0:T(8,128)(2,1)S(1)} %bitcast.8), custom_call_target="tpu_custom_call" | custom-call | flops 201326592 | bytes 5112000 | tf_op jit(solution)/shard_map/pallas_call | solution.py:176
  11.9 0.0 collective-permute-done.1.even_ref
  11.9 0.5 %collective-permute-done.2.odd_ref = f32[1,2,128,128]{3,2,1,0:T(8,128)S(1)} collective-permute-done((f32[1,2,128,128]{3,2,1,0:T(8,128)S(1)}, f32[1,2,128,128]{3,2,1,0:T(8,128)S(1)}, u32[]{:S(2)}, u32[]{:S(2)}) %collective-permute-start.2) | collective-permute-done | bytes 131104 | tf_op jit(solution)/shard_map/ppermute | solution.py:35
  12.4 0.0 collective-permute-done.all_ref
  12.4 0.0 copy-done.4
  12.4 1.0 %shard_map.57 = (f32[2,2,128,128]{3,2,1,0:T(8,128)S(1)}, f32[1,2,128,128]{3,2,1,0:T(8,128)S(1)}, f32[1,2,128,128]{3,2,1,0:T(8,128)S(1)}) custom-call(s32[2]{0:T(128)S(1)} %bitcast.11, bf16[256,1536]{1,0:T(8,128)(2,1)S(1)} %get-tuple-element.14.high_ref, bf16[256,1536]{1,0:T(8,128)(2,1)S(1)} %get-tuple-element.15.low_ref, ...), custom_call_target="tpu_custom_call" | custom-call | flops 402653184 | bytes 2883592 | tf_op jit(solution)/shard_map/pallas_call | solution.py:176
  13.4 1.2 %collective-permute-start.3 = (f32[2,2,128,128]{3,2,1,0:T(8,128)S(1)}, f32[2,2,128,128]{3,2,1,0:T(8,128)S(1)}, u32[]{:S(2)}, u32[]{:S(2)}) collective-permute-start(f32[2,2,128,128]{3,2,1,0:T(8,128)S(1)} %get-tuple-element.20.trace_ref), channel_id=1, source_target_pairs={{0,4},{1,5},{2,6},{3,7},{4,8},{5,9},{6,10},{7,11},{8,12},{9,13},{1... | collective-permute-start | bytes 786440 | tf_op jit(solution)/shard_map/ppermute | solution.py:35
  14.6 2.3 %collective-permute-start.4 = (f32[1,2,128,128]{3,2,1,0:T(8,128)S(1)}, f32[1,2,128,128]{3,2,1,0:T(8,128)S(1)}, u32[]{:S(2)}, u32[]{:S(2)}) collective-permute-start(f32[1,2,128,128]{3,2,1,0:T(8,128)S(1)} %get-tuple-element.21), channel_id=1, source_target_pairs={{0,5},{1,4},{2,7},{3,6},{4,9},{5,8},{6,11},{7,10},{8,13},{9,12},{1... | collective-permute-start | bytes 393224 | tf_op jit(solution)/shard_map/ppermute | solution.py:35
  16.9 1.4 %collective-permute-start.5 = (f32[1,2,128,128]{3,2,1,0:T(8,128)S(1)}, f32[1,2,128,128]{3,2,1,0:T(8,128)S(1)}, u32[]{:S(2)}, u32[]{:S(2)}) collective-permute-start(f32[1,2,128,128]{3,2,1,0:T(8,128)S(1)} %get-tuple-element.22), channel_id=1, source_target_pairs={{0,4},{1,6},{2,5},{3,7},{4,8},{5,10},{6,9},{7,11},{8,12},{9,14},{1... | collective-permute-start | bytes 393224 | tf_op jit(solution)/shard_map/ppermute | solution.py:35
  18.3 0.4 %shard_map.58.own_ref = f32[2,2,128,128]{3,2,1,0:T(8,128)S(1)} custom-call(bf16[256,1536]{1,0:T(8,128)(2,1)S(1)} %get-tuple-element.14.high_ref, bf16[256,1536]{1,0:T(8,128)(2,1)S(1)} %get-tuple-element.15.low_ref, bf16[2,2,128,128]{3,2,1,0:T(8,128)(2,1)S(1)} %bitcast.9, f32[2,2,128,128]{3,2,1,0:T(8,128)S(1)} %get-tuple-element.20.trace_ref), custom_call_target="tpu_custom_call" | custom-call | flops 201326592 | bytes 2228224 | tf_op jit(solution)/shard_map/pallas_call | solution.py:176
  18.6 3.4 %collective-permute-done.4.even_ref = f32[1,2,128,128]{3,2,1,0:T(8,128)S(1)} collective-permute-done((f32[1,2,128,128]{3,2,1,0:T(8,128)S(1)}, f32[1,2,128,128]{3,2,1,0:T(8,128)S(1)}, u32[]{:S(2)}, u32[]{:S(2)}) %collective-permute-start.4) | collective-permute-done | bytes 131104 | tf_op jit(solution)/shard_map/ppermute | solution.py:35
  22.0 1.0 %collective-permute-done.5.odd_ref = f32[1,2,128,128]{3,2,1,0:T(8,128)S(1)} collective-permute-done((f32[1,2,128,128]{3,2,1,0:T(8,128)S(1)}, f32[1,2,128,128]{3,2,1,0:T(8,128)S(1)}, u32[]{:S(2)}, u32[]{:S(2)}) %collective-permute-start.5) | collective-permute-done | bytes 131104 | tf_op jit(solution)/shard_map/ppermute | solution.py:35
  23.0 0.0 collective-permute-done.3.all_ref
  23.0 1.3 %shard_map.59 = f32[2,2,128,128]{3,2,1,0:T(8,128)} custom-call(bf16[256,1536]{1,0:T(8,128)(2,1)S(1)} %get-tuple-element.14.high_ref, bf16[256,1536]{1,0:T(8,128)(2,1)S(1)} %get-tuple-element.15.low_ref, f32[2,2,128,128]{3,2,1,0:T(8,128)S(1)} %shard_map.58.own_ref, f32[2,2,128,128]{3,2,1,0:T(8,128)S(1)} %collective-permute-done.3.all_ref, ...), custom_call_target="tpu_custom_call" | custom-call | flops 402653184 | bytes 2621440 | tf_op jit(solution)/shard_map/pallas_call | solution.py:176
Async XLA Ops:
  0.0 12.4 %copy-start.4 = (s32[1,2,1]{1,2,0:T(1,128)S(1)}, s32[1,2,1]{1,2,0:T(1,128)}, u32[]{:S(2)}) copy-start(s32[1,2,1]{1,2,0:T(1,128)} %param.9) | copy-start | bytes 28
  0.0 0.9 %copy-start.1 = (bf16[1,2,2,128,128]{4,3,2,1,0:T(8,128)(2,1)S(1)}, bf16[1,2,2,128,128]{4,3,2,1,0:T(8,128)(2,1)}, u32[]{:S(2)}) copy-start(bf16[1,2,2,128,128]{4,3,2,1,0:T(8,128)(2,1)} %param.5) | copy-start | bytes 393220
  0.9 0.7 %copy-start.3 = (s32[1,2,1]{1,2,0:T(1,128)S(1)}, s32[1,2,1]{1,2,0:T(1,128)}, u32[]{:S(2)}) copy-start(s32[1,2,1]{1,2,0:T(1,128)} %param.9) | copy-start | bytes 28
  2.2 10.3 %collective-permute-start = (f32[2,2,128,128]{3,2,1,0:T(8,128)S(1)}, f32[2,2,128,128]{3,2,1,0:T(8,128)S(1)}, u32[]{:S(2)}, u32[]{:S(2)}) collective-permute-start(f32[2,2,128,128]{3,2,1,0:T(8,128)S(1)} %get-tuple-element.17), channel_id=1, source_target_pairs={{0,4},{1,5},{2,6},{3,7},{4,8},{5,9},{6,10},{7,11},{8,12},{9,13},{1... | collective-permute-start | bytes 786440 | tf_op jit(solution)/shard_map/ppermute | solution.py:35
  2.7 9.3 %collective-permute-start.1 = (f32[1,2,128,128]{3,2,1,0:T(8,128)S(1)}, f32[1,2,128,128]{3,2,1,0:T(8,128)S(1)}, u32[]{:S(2)}, u32[]{:S(2)}) collective-permute-start(f32[1,2,128,128]{3,2,1,0:T(8,128)S(1)} %get-tuple-element.18), channel_id=1, source_target_pairs={{0,5},{1,4},{2,7},{3,6},{4,9},{5,8},{6,11},{7,10},{8,13},{9,12},{1... | collective-permute-start | bytes 393224 | tf_op jit(solution)/shard_map/ppermute | solution.py:35
  6.4 6.0 %collective-permute-start.2 = (f32[1,2,128,128]{3,2,1,0:T(8,128)S(1)}, f32[1,2,128,128]{3,2,1,0:T(8,128)S(1)}, u32[]{:S(2)}, u32[]{:S(2)}) collective-permute-start(f32[1,2,128,128]{3,2,1,0:T(8,128)S(1)} %get-tuple-element.19), channel_id=1, source_target_pairs={{0,4},{1,6},{2,5},{3,7},{4,8},{5,10},{6,9},{7,11},{8,12},{9,14},{1... | collective-permute-start | bytes 393224 | tf_op jit(solution)/shard_map/ppermute | solution.py:35
  6.5 1.9 %copy-start = (f32[1,24,2,128,128]{4,3,2,1,0:T(8,128)S(1)}, f32[1,24,2,128,128]{4,3,2,1,0:T(8,128)}, u32[]{:S(2)}) copy-start(f32[1,24,2,128,128]{4,3,2,1,0:T(8,128)} %param.6) | copy-start | bytes 9437188
  8.3 0.9 %copy-start.2 = (bf16[1,2,2,128,128]{4,3,2,1,0:T(8,128)(2,1)S(1)}, bf16[1,2,2,128,128]{4,3,2,1,0:T(8,128)(2,1)}, u32[]{:S(2)}) copy-start(bf16[1,2,2,128,128]{4,3,2,1,0:T(8,128)(2,1)} %param.5) | copy-start | bytes 393220
  9.2 0.7 %copy-start.5 = (s32[1,24]{1,0:T(1,128)S(1)}, s32[1,24]{1,0:T(1,128)}, u32[]{:S(2)}) copy-start(s32[1,24]{1,0:T(1,128)} %param.7) | copy-start | bytes 292
  9.9 0.7 %copy-start.6 = (s32[1,24]{1,0:T(1,128)S(1)}, s32[1,24]{1,0:T(1,128)}, u32[]{:S(2)}) copy-start(s32[1,24]{1,0:T(1,128)} %param.8) | copy-start | bytes 292
  13.4 9.6 %collective-permute-start.3 = (f32[2,2,128,128]{3,2,1,0:T(8,128)S(1)}, f32[2,2,128,128]{3,2,1,0:T(8,128)S(1)}, u32[]{:S(2)}, u32[]{:S(2)}) collective-permute-start(f32[2,2,128,128]{3,2,1,0:T(8,128)S(1)} %get-tuple-element.20.trace_ref), channel_id=1, source_target_pairs={{0,4},{1,5},{2,6},{3,7},{4,8},{5,9},{6,10},{7,11},{8,12},{9,13},{1... | collective-permute-start | bytes 786440 | tf_op jit(solution)/shard_map/ppermute | solution.py:35
  14.6 7.4 %collective-permute-start.4 = (f32[1,2,128,128]{3,2,1,0:T(8,128)S(1)}, f32[1,2,128,128]{3,2,1,0:T(8,128)S(1)}, u32[]{:S(2)}, u32[]{:S(2)}) collective-permute-start(f32[1,2,128,128]{3,2,1,0:T(8,128)S(1)} %get-tuple-element.21), channel_id=1, source_target_pairs={{0,5},{1,4},{2,7},{3,6},{4,9},{5,8},{6,11},{7,10},{8,13},{9,12},{1... | collective-permute-start | bytes 393224 | tf_op jit(solution)/shard_map/ppermute | solution.py:35
  16.9 6.1 %collective-permute-start.5 = (f32[1,2,128,128]{3,2,1,0:T(8,128)S(1)}, f32[1,2,128,128]{3,2,1,0:T(8,128)S(1)}, u32[]{:S(2)}, u32[]{:S(2)}) collective-permute-start(f32[1,2,128,128]{3,2,1,0:T(8,128)S(1)} %get-tuple-element.22), channel_id=1, source_target_pairs={{0,4},{1,6},{2,5},{3,7},{4,8},{5,10},{6,9},{7,11},{8,12},{9,14},{1... | collective-permute-start | bytes 393224 | tf_op jit(solution)/shard_map/ppermute | solution.py:35

commit v2 on v1

v2 whole, which is shorter than its diff:
```python
import jax
import jax.numpy as jnp
from jax import lax
from jax.experimental import pallas as pl
from jax.experimental.pallas import tpu as pltpu
from jax.sharding import PartitionSpec as P

F32 = jnp.float32
BF16 = jnp.bfloat16
LIMIT = 40 * 1024 * 1024
CHUNKS = 6


def even_pair(p, planes):
    q = p + 1 if p % 2 == 0 else p - 1
    return q if q < planes else p


def odd_pair(p, planes):
    q = p - 1 if p % 2 == 0 else p + 1
    return q if 0 <= q < planes else p


def same(p, planes):
    return p


def to_next_layer(block, partner):
    layers = lax.axis_size("layer")
    planes = lax.axis_size("plane")
    route = [
        (l * planes + p, (l + 1) % layers * planes + partner(p, planes))
        for l in range(layers)
        for p in range(planes)
    ]
    return lax.ppermute(block, ("layer", "plane"), route)


def split(value):
    high = value.astype(BF16)
    return high, (value - high.astype(F32)).astype(BF16)


def operand(blocks):
    rows = []
    for real, imag in blocks:
        rows.append(jnp.concatenate([real, imag], axis=1))
        rows.append(jnp.concatenate([-imag, real], axis=1))
    return jnp.concatenate(rows, axis=0)


def product(a, b):
    return jnp.dot(a, b, preferred_element_type=F32)


def two_products(matrix_ref, columns, operand_value):
    both = product(matrix_ref[:, columns], operand_value)
    half = both.shape[0] // 2
    return both[:half] + both[half:]


def three_products(matrix_ref, columns, blocks):
    halves = [(split(x), split(y)) for x, y in blocks]
    high = operand([(x[0], y[0]) for x, y in halves])
    low = operand([(x[1], y[1]) for x, y in halves])
    half = matrix_ref.shape[0] // 2
    return two_products(matrix_ref, columns, high) + product(matrix_ref[:half, columns], low)


def store(result, base_ref, out_ref):
    blocks, _, width, shots = base_ref.shape
    for b in range(blocks):
        for part in range(2):
            out_ref[b, part] = (
                result[b * width : (b + 1) * width, part * shots : (part + 1) * shots]
                + base_ref[b, part].astype(F32)
            )


def fetch(pairs, sems):
    copies = [pltpu.make_async_copy(a, b, sems.at[i]) for i, (a, b) in enumerate(pairs)]
    for copy in copies:
        copy.start()
    return copies


def widen_kernel(send_hbm, source_hbm, all_ref, even_ref, odd_ref, send_ref, source_ref, sems):
    copies = fetch([(source_hbm, source_ref), (send_hbm, send_ref)], sems)
    is_odd = lax.axis_index("plane") % 2
    listed = even_ref.shape[0]
    copies[0].wait()
    all_ref[...] = source_ref[...].astype(F32)
    copies[1].wait()
    for k in range(listed):
        even_ref[k] = source_ref[send_ref[(1 - is_odd) * listed + k]].astype(F32)
        odd_ref[k] = source_ref[send_ref[is_odd * listed + k]].astype(F32)


def prepare_kernel(
    rows_hbm, cols_hbm, send_hbm, source_hbm, tiles_hbm,
    matrix_ref, own_ref, mask_ref,
    rows_ref, cols_ref, send_ref, source_ref, tiles_ref, total, sems,
):
    tile_count, _, width, _ = tiles_ref.shape
    blocks_here = source_ref.shape[0]
    extended = total.shape[0] // blocks_here
    listed = (extended - 2 * blocks_here) // 2
    small = [(rows_hbm, rows_ref), (cols_hbm, cols_ref), (send_hbm, send_ref)]
    chunk = tile_count // CHUNKS if tile_count % CHUNKS == 0 else tile_count
    parts = [pl.ds(first, chunk) for first in range(0, tile_count, chunk)]
    large = [(tiles_hbm.at[part], tiles_ref.at[part]) for part in parts]
    copies = fetch(small + large + [(source_hbm, source_ref)], sems)
    layer = lax.axis_index("layer")
    plane = lax.axis_index("plane")
    planes = lax.axis_size("plane")
    is_odd = plane % 2
    total[...] = jnp.zeros_like(total)

    def add(t, carry):
        col = cols_ref[t]
        is_lower = (col >= blocks_here) & (col < blocks_here + listed)
        is_upper = (col >= blocks_here + listed) & (col < blocks_here + 2 * listed)
        place = jnp.where(is_lower & (is_odd == 0), col + listed, col)
        place = jnp.where(is_upper & (is_odd == 0), col - listed, place)
        slot = rows_ref[t] * extended + place
        total[slot, :, :width] += tiles_ref[t, 0]
        total[slot, :, width:] += tiles_ref[t, 1]
        return carry

    for copy in copies[:3]:
        copy.wait()
    for k in range(listed):
        to_even = send_ref[(1 - is_odd) * listed + k]
        to_odd = send_ref[is_odd * listed + k]
        for b in range(blocks_here):
            for kind, chosen in enumerate((to_even, to_odd)):
                mask_ref[kind, k, b] = jnp.full(mask_ref.shape[3:], jnp.where(chosen == b, 1.0, 0.0), F32)
    for i, copy in enumerate(copies[3:-1]):
        copy.wait()
        lax.fori_loop(i * chunk, (i + 1) * chunk, add, 0, unroll=True)
    has_layer = layer > 0
    has_next = plane + 1 < planes
    has_even = has_layer & ((is_odd == 1) | has_next)
    has_odd = has_layer & jnp.where(is_odd == 1, has_next, plane > 0)
    height = blocks_here * width
    for c in range(extended):
        keep = None
        if c < blocks_here:
            keep = has_layer
        elif c < blocks_here + listed:
            keep = has_even
        elif c < blocks_here + 2 * listed:
            keep = has_odd
        for r in range(blocks_here):
            value = total[r * extended + c]
            if keep is not None:
                value = jnp.where(keep, value, 0.0)
            high, low = split(value)
            here = slice(c * 2 * width, (c + 1) * 2 * width)
            matrix_ref[r * width : (r + 1) * width, here] = high
            matrix_ref[height + r * width : height + (r + 1) * width, here] = low
    copies[-1].wait()
    own = operand([(source_ref[b, 0], source_ref[b, 1]) for b in range(blocks_here)])
    columns = slice((extended - blocks_here) * 2 * width, None)
    store(two_products(matrix_ref, columns, own), source_ref, own_ref)


def gather(*refs):
    return [(ref[b, 0], ref[b, 1]) for ref in refs for b in range(ref.shape[0])]


def middle_kernel(mask_ref, matrix_ref, own_ref, all_ref, even_ref, odd_ref, new_ref, new_even_ref, new_odd_ref):
    blocks = [(x.astype(BF16), y.astype(BF16)) for x, y in gather(all_ref, even_ref, odd_ref)]
    stacked = operand(blocks)
    store(two_products(matrix_ref, slice(0, stacked.shape[0]), stacked), own_ref, new_ref)
    count, _, width, shots = new_ref.shape
    rows = mask_ref.shape[3]
    for kind, out_ref in enumerate((new_even_ref, new_odd_ref)):
        for k in range(out_ref.shape[0]):
            chosen = jnp.zeros((2, width // rows, rows, shots), F32)
            for b in range(count):
                block = new_ref[b].reshape(chosen.shape)
                chosen = jnp.where(mask_ref[kind, k, b][None, None] > 0.5, block, chosen)
            out_ref[k] = chosen.reshape(2, width, shots)


def own_kernel(matrix_ref, source_ref, trace_ref, own_ref):
    blocks = gather(trace_ref)
    depth = 2 * trace_ref.shape[2] * len(blocks)
    store(three_products(matrix_ref, slice(matrix_ref.shape[1] - depth, None), blocks), source_ref, own_ref)


def last_kernel(matrix_ref, own_ref, all_ref, even_ref, odd_ref, out_ref):
    blocks = gather(all_ref, even_ref, odd_ref)
    depth = 2 * all_ref.shape[2] * len(blocks)
    store(three_products(matrix_ref, slice(0, depth), blocks), own_ref, out_ref)


def call(kernel, ins, outs, flops, scratch=(), in_hbm=False):
    moved = sum(x.size * x.dtype.itemsize for x in (*ins, *outs))
    if in_hbm:
        ins = [pltpu.with_memory_space_constraint(x, pltpu.HBM) for x in ins]
    vmem = pl.BlockSpec(memory_space=pltpu.VMEM)
    hbm = pl.BlockSpec(memory_space=pltpu.HBM)
    return pl.pallas_call(
        kernel,
        out_shape=outs,
        in_specs=[hbm if in_hbm else vmem] * len(ins),
        out_specs=[vmem] * len(outs),
        scratch_shapes=scratch,
        compiler_params=pltpu.CompilerParams(vmem_limit_bytes=LIMIT),
        cost_estimate=pl.CostEstimate(flops=flops, bytes_accessed=moved, transcendentals=0),
    )(*ins)


def per_device(sources, operator_tiles, tile_rows, tile_cols, send_blocks):
    source = sources[0]
    tiles = operator_tiles[0]
    rows = tile_rows.reshape(-1)
    cols = tile_cols.reshape(-1)
    send = send_blocks.reshape(-1)
    blocks, _, width, shots = source.shape
    listed = send_blocks.shape[2]
    extended = 2 * blocks + 2 * listed
    shape = jax.ShapeDtypeStruct
    trace = shape(source.shape, F32)
    part = shape((listed, 2, width, shots), F32)
    matrix = shape((2 * blocks * width, extended * 2 * width), BF16)
    mask = shape((2, listed, blocks, 8, shots), F32)
    flops = 2 * blocks * width * extended * 2 * width * 2 * shots

    def exchange(whole, even, odd):
        return (
            to_next_layer(whole, same),
            to_next_layer(even, even_pair),
            to_next_layer(odd, odd_pair),
        )

    send_copy = pltpu.SMEM(send.shape, send.dtype)
    source_copy = pltpu.VMEM(source.shape, source.dtype)
    arrived = exchange(
        *call(
            widen_kernel,
            (send, source),
            (trace, part, part),
            0,
            [send_copy, source_copy, pltpu.SemaphoreType.DMA((2,))],
            in_hbm=True,
        )
    )
    matrix, own, mask = call(
        prepare_kernel,
        (rows, cols, send, source, tiles),
        (matrix, trace, mask),
        flops,
        [
            pltpu.SMEM(rows.shape, rows.dtype),
            pltpu.SMEM(cols.shape, cols.dtype),
            send_copy,
            source_copy,
            pltpu.VMEM(tiles.shape, F32),
            pltpu.VMEM((blocks * extended, width, 2 * width), F32),
            pltpu.SemaphoreType.DMA((CHUNKS + 4,)),
        ],
        in_hbm=True,
    )
    traces, even, odd = call(middle_kernel, (mask, matrix, own, *arrived), (trace, part, part), 2 * flops)
    arrived = exchange(traces, even, odd)
    (own,) = call(own_kernel, (matrix, source, traces), (trace,), flops)
    (out,) = call(last_kernel, (matrix, own, *arrived), (trace,), 2 * flops)
    return out[None]


def solution(mesh):
    placed = (
        P("layer", "plane", None, None, None),
        P("layer", "plane", None, None, None),
        P("layer", "plane"),
        P("layer", "plane"),
        P("plane", None, None),
    )
    return jax.shard_map(
        per_device,
        mesh=mesh,
        in_specs=placed,
        out_specs=P("layer", "plane", None, None, None),
        check_vma=False,
    )
```

time: 24.5 us -> 22.8 us (0.931)
  local copies, waits for them, and re-layouts: 5.68 us -> 0.01 us
  waiting for transfers between devices: 4.84 us -> 9.96 us
  starting transfers between devices: 9.12 us -> 6.97 us
  Pallas kernels: 4.58 us -> 5.62 us
    unnamed x14 -> x2, local copies, waits for them, and re-layouts: 5.68 us -> 0.01 us
    ppermute x6, waiting for transfers between devices: 4.84 us -> 9.96 us  [to_next_layer(): return lax.ppermute(block, ('layer', 'plane'), route)]
    ppermute x6, starting transfers between devices: 9.12 us -> 6.97 us  [to_next_layer(): return lax.ppermute(block, ('layer', 'plane'), route)]
    pallas_call x5, Pallas kernels: 4.58 us -> 5.62 us  [call(): pl.pallas_call(kernel, out_shape=outs, in_specs=[hbm if in_hbm else vmem]...]
  transfers between devices with their start and end apart: 6 -> 6, of which waited for: 3 -> 4; matrix products, arithmetic and copies ran while one was open for 0% -> 0% of each run, Pallas kernels for 7% -> 13%
where the time goes in v2:
time: 22.8 us; the launch traced here: 22.6 us
  waiting for transfers between devices  9.96 us (44%)
  starting transfers between devices  6.97 us (31%)
  Pallas kernels  5.62 us (25%)
    ppermute x6, waiting for transfers between devices, to_next_layer(): return lax.ppermute(block, ('layer', 'plane'), route)  9.96 us
    ppermute x6, starting transfers between devices, to_next_layer(): return lax.ppermute(block, ('layer', 'plane'), route)  6.97 us
    pallas_call x5, Pallas kernels, call(): pl.pallas_call(kernel, out_shape=outs, in_specs=[hbm if in_hbm else vmem]...  5.62 us
  transfers between devices with their start and end apart: 6, of which 4 were waited for; matrix products, arithmetic and copies ran while one was open for 0% of the time, Pallas kernels for 13%

profile of v2, /device:TPU:0, one launch (start us, length us, event | category | flops | bytes accessed | tf_op | source)
XLA Modules:
  0.0 22.6 jit_solution(7614504368848947797)
XLA Ops:
  0.0 0.0 copy-start
  0.0 1.0 %shard_map.56 = (f32[2,2,128,128]{3,2,1,0:T(8,128)S(1)}, f32[1,2,128,128]{3,2,1,0:T(8,128)S(1)}, f32[1,2,128,128]{3,2,1,0:T(8,128)S(1)}) custom-call(s32[2]{0:T(128)} %bitcast.10, bf16[2,2,128,128]{3,2,1,0:T(8,128)(2,1)} %bitcast.6), custom_call_target="tpu_custom_call" | custom-call | bytes 655368 | tf_op jit(solution)/shard_map/pallas_call | solution.py:205
  1.1 0.5 %collective-permute-start = (f32[2,2,128,128]{3,2,1,0:T(8,128)S(1)}, f32[2,2,128,128]{3,2,1,0:T(8,128)S(1)}, u32[]{:S(2)}, u32[]{:S(2)}) collective-permute-start(f32[2,2,128,128]{3,2,1,0:T(8,128)S(1)} %get-tuple-element.17), channel_id=1, source_target_pairs={{0,4},{1,5},{2,6},{3,7},{4,8},{5,9},{6,10},{7,11},{8,12},{9,13},{1... | collective-permute-start | bytes 786440 | tf_op jit(solution)/shard_map/ppermute | solution.py:36
  1.6 3.8 %collective-permute-start.1 = (f32[1,2,128,128]{3,2,1,0:T(8,128)S(1)}, f32[1,2,128,128]{3,2,1,0:T(8,128)S(1)}, u32[]{:S(2)}, u32[]{:S(2)}) collective-permute-start(f32[1,2,128,128]{3,2,1,0:T(8,128)S(1)} %get-tuple-element.18), channel_id=1, source_target_pairs={{0,5},{1,4},{2,7},{3,6},{4,9},{5,8},{6,11},{7,10},{8,13},{9,12},{1... | collective-permute-start | bytes 393224 | tf_op jit(solution)/shard_map/ppermute | solution.py:36
  5.3 0.0 collective-permute-start.2
  5.3 2.5 %shard_map.55 = (bf16[512,1536]{1,0:T(8,128)(2,1)S(1)}, f32[2,2,128,128]{3,2,1,0:T(8,128)S(1)}, f32[2,1,2,8,128]{4,3,2,1,0:T(8,128)S(1)}) custom-call(s32[24]{0:T(128)} %bitcast.12, s32[24]{0:T(128)} %bitcast.13, s32[2]{0:T(128)} %bitcast.11, bf16[2,2,128,128]{3,2,1,0:T(8,128)(2,1)} %bitcast.7, f32[24,2,128,128]{3,2,1,0:T(8,128)} %bitcast.9), custom_call_target="tpu_custom_call" | custom-call | flops 201326592 | bytes 5128392 | tf_op jit(solution)/shard_map/pallas_call | solution.py:205
  7.8 2.3 %collective-permute-done.1.even_ref = f32[1,2,128,128]{3,2,1,0:T(8,128)S(1)} collective-permute-done((f32[1,2,128,128]{3,2,1,0:T(8,128)S(1)}, f32[1,2,128,128]{3,2,1,0:T(8,128)S(1)}, u32[]{:S(2)}, u32[]{:S(2)}) %collective-permute-start.1) | collective-permute-done | bytes 131104 | tf_op jit(solution)/shard_map/ppermute | solution.py:36
  10.1 1.2 %collective-permute-done.2.odd_ref = f32[1,2,128,128]{3,2,1,0:T(8,128)S(1)} collective-permute-done((f32[1,2,128,128]{3,2,1,0:T(8,128)S(1)}, f32[1,2,128,128]{3,2,1,0:T(8,128)S(1)}, u32[]{:S(2)}, u32[]{:S(2)}) %collective-permute-start.2) | collective-permute-done | bytes 131104 | tf_op jit(solution)/shard_map/ppermute | solution.py:36
  11.3 0.0 collective-permute-done.all_ref
  11.3 0.4 %shard_map.57 = (f32[2,2,128,128]{3,2,1,0:T(8,128)S(1)}, f32[1,2,128,128]{3,2,1,0:T(8,128)S(1)}, f32[1,2,128,128]{3,2,1,0:T(8,128)S(1)}) custom-call(f32[2,1,2,8,128]{4,3,2,1,0:T(8,128)S(1)} %get-tuple-element.15.mask_ref, bf16[512,1536]{1,0:T(8,128)(2,1)S(1)} %get-tuple-element.14.matrix_ref, f32[2,2,128,128]{3,2,1,0:T(8,128)S(1)} %get-tuple-element.16.own_ref, ...), custom_call_target="tpu_custom_call" | custom-call | flops 402653184 | bytes 2899968 | tf_op jit(solution)/shard_map/pallas_call | solution.py:205
  11.8 0.1 collective-permute-start.3
  11.8 2.6 %collective-permute-start.4 = (f32[1,2,128,128]{3,2,1,0:T(8,128)S(1)}, f32[1,2,128,128]{3,2,1,0:T(8,128)S(1)}, u32[]{:S(2)}, u32[]{:S(2)}) collective-permute-start(f32[1,2,128,128]{3,2,1,0:T(8,128)S(1)} %get-tuple-element.21), channel_id=1, source_target_pairs={{0,5},{1,4},{2,7},{3,6},{4,9},{5,8},{6,11},{7,10},{8,13},{9,12},{1... | collective-permute-start | bytes 393224 | tf_op jit(solution)/shard_map/ppermute | solution.py:36
  14.4 0.0 collective-permute-start.5
  14.5 0.0 copy-done
  14.5 0.4 %shard_map.58.own_ref = f32[2,2,128,128]{3,2,1,0:T(8,128)S(1)} custom-call(bf16[512,1536]{1,0:T(8,128)(2,1)S(1)} %get-tuple-element.14.matrix_ref, bf16[2,2,128,128]{3,2,1,0:T(8,128)(2,1)S(1)} %bitcast.8, f32[2,2,128,128]{3,2,1,0:T(8,128)S(1)} %get-tuple-element.20.trace_ref), custom_call_target="tpu_custom_call" | custom-call | flops 201326592 | bytes 2228224 | tf_op jit(solution)/shard_map/pallas_call | solution.py:205
  14.8 5.4 %collective-permute-done.4.even_ref = f32[1,2,128,128]{3,2,1,0:T(8,128)S(1)} collective-permute-done((f32[1,2,128,128]{3,2,1,0:T(8,128)S(1)}, f32[1,2,128,128]{3,2,1,0:T(8,128)S(1)}, u32[]{:S(2)}, u32[]{:S(2)}) %collective-permute-start.4) | collective-permute-done | bytes 131104 | tf_op jit(solution)/shard_map/ppermute | solution.py:36
  20.3 1.0 %collective-permute-done.5.odd_ref = f32[1,2,128,128]{3,2,1,0:T(8,128)S(1)} collective-permute-done((f32[1,2,128,128]{3,2,1,0:T(8,128)S(1)}, f32[1,2,128,128]{3,2,1,0:T(8,128)S(1)}, u32[]{:S(2)}, u32[]{:S(2)}) %collective-permute-start.5) | collective-permute-done | bytes 131104 | tf_op jit(solution)/shard_map/ppermute | solution.py:36
  21.3 0.0 collective-permute-done.3.all_ref
  21.3 1.3 %shard_map.59 = f32[2,2,128,128]{3,2,1,0:T(8,128)} custom-call(bf16[512,1536]{1,0:T(8,128)(2,1)S(1)} %get-tuple-element.14.matrix_ref, f32[2,2,128,128]{3,2,1,0:T(8,128)S(1)} %shard_map.58.own_ref, f32[2,2,128,128]{3,2,1,0:T(8,128)S(1)} %collective-permute-done.3.all_ref, f32[1,2,128,128]{3,2,1,0:T(8,128)S(1)} %collective-permute-done.4.even_ref, ...), custom_call_target="tpu_custom_call" | custom-call | flops 402653184 | bytes 2621440 | tf_op jit(solution)/shard_map/pallas_call | solution.py:205
Async XLA Ops:
  0.0 14.5 %copy-start = (bf16[1,2,2,128,128]{4,3,2,1,0:T(8,128)(2,1)S(1)}, bf16[1,2,2,128,128]{4,3,2,1,0:T(8,128)(2,1)}, u32[]{:S(2)}) copy-start(bf16[1,2,2,128,128]{4,3,2,1,0:T(8,128)(2,1)} %param.5) | copy-start | bytes 393220
  1.1 10.3 %collective-permute-start = (f32[2,2,128,128]{3,2,1,0:T(8,128)S(1)}, f32[2,2,128,128]{3,2,1,0:T(8,128)S(1)}, u32[]{:S(2)}, u32[]{:S(2)}) collective-permute-start(f32[2,2,128,128]{3,2,1,0:T(8,128)S(1)} %get-tuple-element.17), channel_id=1, source_target_pairs={{0,4},{1,5},{2,6},{3,7},{4,8},{5,9},{6,10},{7,11},{8,12},{9,13},{1... | collective-permute-start | bytes 786440 | tf_op jit(solution)/shard_map/ppermute | solution.py:36
  1.6 8.5 %collective-permute-start.1 = (f32[1,2,128,128]{3,2,1,0:T(8,128)S(1)}, f32[1,2,128,128]{3,2,1,0:T(8,128)S(1)}, u32[]{:S(2)}, u32[]{:S(2)}) collective-permute-start(f32[1,2,128,128]{3,2,1,0:T(8,128)S(1)} %get-tuple-element.18), channel_id=1, source_target_pairs={{0,5},{1,4},{2,7},{3,6},{4,9},{5,8},{6,11},{7,10},{8,13},{9,12},{1... | collective-permute-start | bytes 393224 | tf_op jit(solution)/shard_map/ppermute | solution.py:36
  5.3 6.0 %collective-permute-start.2 = (f32[1,2,128,128]{3,2,1,0:T(8,128)S(1)}, f32[1,2,128,128]{3,2,1,0:T(8,128)S(1)}, u32[]{:S(2)}, u32[]{:S(2)}) collective-permute-start(f32[1,2,128,128]{3,2,1,0:T(8,128)S(1)} %get-tuple-element.19), channel_id=1, source_target_pairs={{0,4},{1,6},{2,5},{3,7},{4,8},{5,10},{6,9},{7,11},{8,12},{9,14},{1... | collective-permute-start | bytes 393224 | tf_op jit(solution)/shard_map/ppermute | solution.py:36
  11.8 9.6 %collective-permute-start.3 = (f32[2,2,128,128]{3,2,1,0:T(8,128)S(1)}, f32[2,2,128,128]{3,2,1,0:T(8,128)S(1)}, u32[]{:S(2)}, u32[]{:S(2)}) collective-permute-start(f32[2,2,128,128]{3,2,1,0:T(8,128)S(1)} %get-tuple-element.20.trace_ref), channel_id=1, source_target_pairs={{0,4},{1,5},{2,6},{3,7},{4,8},{5,9},{6,10},{7,11},{8,12},{9,13},{1... | collective-permute-start | bytes 786440 | tf_op jit(solution)/shard_map/ppermute | solution.py:36
  11.8 8.4 %collective-permute-start.4 = (f32[1,2,128,128]{3,2,1,0:T(8,128)S(1)}, f32[1,2,128,128]{3,2,1,0:T(8,128)S(1)}, u32[]{:S(2)}, u32[]{:S(2)}) collective-permute-start(f32[1,2,128,128]{3,2,1,0:T(8,128)S(1)} %get-tuple-element.21), channel_id=1, source_target_pairs={{0,5},{1,4},{2,7},{3,6},{4,9},{5,8},{6,11},{7,10},{8,13},{9,12},{1... | collective-permute-start | bytes 393224 | tf_op jit(solution)/shard_map/ppermute | solution.py:36
  14.4 6.9 %collective-permute-start.5 = (f32[1,2,128,128]{3,2,1,0:T(8,128)S(1)}, f32[1,2,128,128]{3,2,1,0:T(8,128)S(1)}, u32[]{:S(2)}, u32[]{:S(2)}) collective-permute-start(f32[1,2,128,128]{3,2,1,0:T(8,128)S(1)} %get-tuple-element.22), channel_id=1, source_target_pairs={{0,4},{1,6},{2,5},{3,7},{4,8},{5,10},{6,9},{7,11},{8,12},{9,14},{1... | collective-permute-start | bytes 393224 | tf_op jit(solution)/shard_map/ppermute | solution.py:36

commit v3 on v2

--- a/solution.py
+++ b/solution.py
@@ -25,15 +25,29 @@
     return p
 
 
-def to_next_layer(block, partner):
+def outward(l, p, layers, planes, partner):
+    return (l + 1) % layers, partner(p, planes) if l % 2 == 1 and l + 1 < layers else p
+
+
+def inward(l, p, layers, planes, partner):
+    if l % 2 == 1:
+        return l - 1, p
+    return (l + 1, partner(p, planes)) if l + 1 < layers else (l, p)
+
+
+def permute(block, way, partner):
     layers = lax.axis_size("layer")
     planes = lax.axis_size("plane")
-    route = [
-        (l * planes + p, (l + 1) % layers * planes + partner(p, planes))
-        for l in range(layers)
-        for p in range(planes)
-    ]
+    route = []
+    for l in range(layers):
+        for p in range(planes):
+            to_layer, to_plane = way(l, p, layers, planes, partner)
+            route.append((l * planes + p, to_layer * planes + to_plane))
     return lax.ppermute(block, ("layer", "plane"), route)
+
+
+def onward(l, p, layers, planes, partner):
+    return (l + 1) % layers, partner(p, planes) if l + 1 < layers else p
 
 
 def split(value):
@@ -169,13 +183,10 @@
     return [(ref[b, 0], ref[b, 1]) for ref in refs for b in range(ref.shape[0])]
 
 
-def middle_kernel(mask_ref, matrix_ref, own_ref, all_ref, even_ref, odd_ref, new_ref, new_even_ref, new_odd_ref):
-    blocks = [(x.astype(BF16), y.astype(BF16)) for x, y in gather(all_ref, even_ref, odd_ref)]
-    stacked = operand(blocks)
-    store(two_products(matrix_ref, slice(0, stacked.shape[0]), stacked), own_ref, new_ref)
+def choose(mask_ref, new_ref, even_ref, odd_ref):
     count, _, width, shots = new_ref.shape
     rows = mask_ref.shape[3]
-    for kind, out_ref in enumerate((new_even_ref, new_odd_ref)):
+    for kind, out_ref in enumerate((even_ref, odd_ref)):
         for k in range(out_ref.shape[0]):
             chosen = jnp.zeros((2, width // rows, rows, shots), F32)
             for b in range(count):
@@ -184,20 +195,78 @@
             out_ref[k] = chosen.reshape(2, width, shots)
 
 
+def second_tick(matrix_ref, own_ref, arrived_refs, new_ref):
+    blocks = [(x.astype(BF16), y.astype(BF16)) for x, y in gather(*arrived_refs)]
+    stacked = operand(blocks)
+    store(two_products(matrix_ref, slice(0, stacked.shape[0]), stacked), own_ref, new_ref)
+
+
+def on_odd_layer():
+    return lax.axis_index("layer") % 2 == 1
+
+
+def odd_kernel(matrix_ref, own_ref, all_ref, even_ref, odd_ref, new_ref):
+    @pl.when(on_odd_layer())
+    def _():
+        second_tick(matrix_ref, own_ref, (all_ref, even_ref, odd_ref), new_ref)
+
+    @pl.when(jnp.logical_not(on_odd_layer()))
+    def _():
+        new_ref[...] = own_ref[...]
+
+
+def even_kernel(mask_ref, matrix_ref, own_ref, known_ref, all_ref, even_ref, odd_ref, new_ref, new_even_ref, new_odd_ref):
+    @pl.when(on_odd_layer())
+    def _():
+        new_ref[...] = known_ref[...]
+
+    @pl.when(jnp.logical_not(on_odd_layer()))
+    def _():
+        second_tick(matrix_ref, own_ref, (all_ref, even_ref, odd_ref), new_ref)
+
+    choose(mask_ref, new_ref, new_even_ref, new_odd_ref)
+
+
 def own_kernel(matrix_ref, source_ref, trace_ref, own_ref):
     blocks = gather(trace_ref)
     depth = 2 * trace_ref.shape[2] * len(blocks)
     store(three_products(matrix_ref, slice(matrix_ref.shape[1] - depth, None), blocks), source_ref, own_ref)
 
 
-def last_kernel(matrix_ref, own_ref, all_ref, even_ref, odd_ref, out_ref):
-    blocks = gather(all_ref, even_ref, odd_ref)
-    depth = 2 * all_ref.shape[2] * len(blocks)
-    store(three_products(matrix_ref, slice(0, depth), blocks), own_ref, out_ref)
-
-
-def call(kernel, ins, outs, flops, scratch=(), in_hbm=False):
-    moved = sum(x.size * x.dtype.itemsize for x in (*ins, *outs))
+def third_tick(matrix_ref, first, base_ref, refs, out_ref):
+    blocks = gather(*refs)
+    unit = 2 * base_ref.shape[2]
+    columns = slice(first * unit, (first + len(blocks)) * unit)
+    store(three_products(matrix_ref, columns, blocks), base_ref, out_ref)
+
+
+def even_whole_kernel(matrix_ref, base_ref, all_ref, out_ref):
+    @pl.when(on_odd_layer())
+    def _():
+        out_ref[...] = base_ref[...]
+
+    @pl.when(jnp.logical_not(on_odd_layer()))
+    def _():
+        third_tick(matrix_ref, 0, base_ref, (all_ref,), out_ref)
+
+
+def odd_whole_kernel(matrix_ref, base_ref, all_ref, out_ref):
+    @pl.when(on_odd_layer())
+    def _():
+        third_tick(matrix_ref, 0, base_ref, (all_ref,), out_ref)
+
+    @pl.when(jnp.logical_not(on_odd_layer()))
+    def _():
+        out_ref[...] = base_ref[...]
+
+
+def last_kernel(matrix_ref, base_ref, even_ref, odd_ref, out_ref):
+    third_tick(matrix_ref, base_ref.shape[0], base_ref, (even_ref, odd_ref), out_ref)
+
+
+def call(kernel, ins, outs, flops, scratch=(), in_hbm=False, moved=None):
+    if moved is None:
+        moved = sum(x.size * x.dtype.itemsize for x in (*ins, *outs))
     if in_hbm:
         ins = [pltpu.with_memory_space_constraint(x, pltpu.HBM) for x in ins]
     vmem = pl.BlockSpec(memory_space=pltpu.VMEM)
@@ -229,25 +298,19 @@
     mask = shape((2, listed, blocks, 8, shots), F32)
     flops = 2 * blocks * width * extended * 2 * width * 2 * shots
 
-    def exchange(whole, even, odd):
-        return (
-            to_next_layer(whole, same),
-            to_next_layer(even, even_pair),
-            to_next_layer(odd, odd_pair),
-        )
-
     send_copy = pltpu.SMEM(send.shape, send.dtype)
     source_copy = pltpu.VMEM(source.shape, source.dtype)
-    arrived = exchange(
-        *call(
-            widen_kernel,
-            (send, source),
-            (trace, part, part),
-            0,
-            [send_copy, source_copy, pltpu.SemaphoreType.DMA((2,))],
-            in_hbm=True,
-        )
-    )
+    whole, even, odd = call(
+        widen_kernel,
+        (send, source),
+        (trace, part, part),
+        0,
+        [send_copy, source_copy, pltpu.SemaphoreType.DMA((2,))],
+        in_hbm=True,
+    )
+    whole = permute(whole, onward, same)
+    from_even = permute(even, inward, even_pair), permute(odd, inward, odd_pair)
+    from_odd = permute(even, outward, even_pair), permute(odd, outward, odd_pair)
     matrix, own, mask = call(
         prepare_kernel,
         (rows, cols, send, source, tiles),
@@ -264,10 +327,18 @@
         ],
         in_hbm=True,
     )
-    traces, even, odd = call(middle_kernel, (mask, matrix, own, *arrived), (trace, part, part), 2 * flops)
-    arrived = exchange(traces, even, odd)
+    (second,) = call(odd_kernel, (matrix, own, whole, *from_even), (trace,), flops)
+    early = permute(second, outward, same)
+    traces, even, odd = call(
+        even_kernel, (mask, matrix, own, second, whole, *from_odd), (trace, part, part), 10**11, moved=10**9
+    )
+    late = permute(traces, inward, same)
+    even = permute(even, onward, even_pair)
+    odd = permute(odd, onward, odd_pair)
     (own,) = call(own_kernel, (matrix, source, traces), (trace,), flops)
-    (out,) = call(last_kernel, (matrix, own, *arrived), (trace,), 2 * flops)
+    (own,) = call(even_whole_kernel, (matrix, own, early), (trace,), 10**11, moved=10**9)
+    (own,) = call(odd_whole_kernel, (matrix, own, late), (trace,), flops)
+    (out,) = call(last_kernel, (matrix, own, even, odd), (trace,), flops)
     return out[None]
 
 

time: 22.8 us -> 21.2 us (0.930)
  waiting for transfers between devices: 9.96 us -> 5.12 us
  starting transfers between devices: 6.97 us -> 10.1 us
    ppermute x6 -> x9, waiting for transfers between devices: 9.96 us -> 5.12 us  [permute(): return lax.ppermute(block, ('layer', 'plane'), route)]
    ppermute x6 -> x9, starting transfers between devices: 6.97 us -> 10.1 us  [permute(): return lax.ppermute(block, ('layer', 'plane'), route)]
    pallas_call x5 -> x8, Pallas kernels: 5.62 us -> 5.82 us  [call(): pl.pallas_call(kernel, out_shape=outs, in_specs=[hbm if in_hbm else vmem]...]
  transfers between devices with their start and end apart: 6 -> 9, of which waited for: 4 -> 4; matrix products, arithmetic and copies ran while one was open for 0% -> 0% of each run, Pallas kernels for 13% -> 18%
where the time goes in v3:
time: 21.2 us; the launch traced here: 21.1 us
  starting transfers between devices  10.1 us (48%)
  Pallas kernels  5.82 us (27%)
  waiting for transfers between devices  5.12 us (24%)
    ppermute x9, starting transfers between devices, permute(): return lax.ppermute(block, ('layer', 'plane'), route)  10.1 us
    pallas_call x8, Pallas kernels, call(): pl.pallas_call(kernel, out_shape=outs, in_specs=[hbm if in_hbm else vmem]...  5.82 us
    ppermute x9, waiting for transfers between devices, permute(): return lax.ppermute(block, ('layer', 'plane'), route)  5.12 us
  transfers between devices with their start and end apart: 9, of which 4 were waited for; matrix products, arithmetic and copies ran while one was open for 0% of the time, Pallas kernels for 18%

profile of v3, /device:TPU:0, one launch (start us, length us, event | category | flops | bytes accessed | tf_op | source)
XLA Modules:
  0.0 21.1 jit_solution(11353841836056380402)
XLA Ops:
  0.0 1.0 %shard_map.56 = (f32[2,2,128,128]{3,2,1,0:T(8,128)S(1)}, f32[1,2,128,128]{3,2,1,0:T(8,128)S(1)}, f32[1,2,128,128]{3,2,1,0:T(8,128)S(1)}) custom-call(s32[2]{0:T(128)} %bitcast.10, bf16[2,2,128,128]{3,2,1,0:T(8,128)(2,1)} %bitcast.6), custom_call_target="tpu_custom_call" | custom-call | bytes 655368 | tf_op jit(solution)/shard_map/pallas_call | solution.py:274
  1.0 0.5 %collective-permute-start = (f32[2,2,128,128]{3,2,1,0:T(8,128)S(1)}, f32[2,2,128,128]{3,2,1,0:T(8,128)S(1)}, u32[]{:S(2)}, u32[]{:S(2)}) collective-permute-start(f32[2,2,128,128]{3,2,1,0:T(8,128)S(1)} %get-tuple-element.17), channel_id=1, source_target_pairs={{0,4},{1,5},{2,6},{3,7},{4,8},{5,9},{6,10},{7,11},{8,12},{9,13},{1... | collective-permute-start | bytes 786440 | tf_op jit(solution)/shard_map/ppermute | solution.py:46
  1.5 3.8 %collective-permute-start.1 = (f32[1,2,128,128]{3,2,1,0:T(8,128)S(1)}, f32[1,2,128,128]{3,2,1,0:T(8,128)S(1)}, u32[]{:S(2)}, u32[]{:S(2)}) collective-permute-start(f32[1,2,128,128]{3,2,1,0:T(8,128)S(1)} %get-tuple-element.18), channel_id=1, source_target_pairs={{0,5},{1,4},{2,7},{3,6},{4,0},{5,1},{6,2},{7,3},{8,13},{9,12},{10,... | collective-permute-start | bytes 393224 | tf_op jit(solution)/shard_map/ppermute | solution.py:46
  5.3 0.0 collective-permute-start.2
  5.3 0.5 %collective-permute-start.3 = (f32[1,2,128,128]{3,2,1,0:T(8,128)S(1)}, f32[1,2,128,128]{3,2,1,0:T(8,128)S(1)}, u32[]{:S(2)}, u32[]{:S(2)}) collective-permute-start(f32[1,2,128,128]{3,2,1,0:T(8,128)S(1)} %get-tuple-element.18), channel_id=1, source_target_pairs={{0,4},{1,5},{2,6},{3,7},{4,9},{5,8},{6,11},{7,10},{8,12},{9,13},{1... | collective-permute-start | bytes 393224 | tf_op jit(solution)/shard_map/ppermute | solution.py:46
  5.8 2.1 %collective-permute-start.4 = (f32[1,2,128,128]{3,2,1,0:T(8,128)S(1)}, f32[1,2,128,128]{3,2,1,0:T(8,128)S(1)}, u32[]{:S(2)}, u32[]{:S(2)}) collective-permute-start(f32[1,2,128,128]{3,2,1,0:T(8,128)S(1)} %get-tuple-element.19), channel_id=1, source_target_pairs={{0,4},{1,5},{2,6},{3,7},{4,8},{5,10},{6,9},{7,11},{8,12},{9,13},{1... | collective-permute-start | bytes 393224 | tf_op jit(solution)/shard_map/ppermute | solution.py:46
  7.9 2.5 %shard_map.55 = (bf16[512,1536]{1,0:T(8,128)(2,1)S(1)}, f32[2,2,128,128]{3,2,1,0:T(8,128)S(1)}, f32[2,1,2,8,128]{4,3,2,1,0:T(8,128)S(1)}) custom-call(s32[24]{0:T(128)} %bitcast.12, s32[24]{0:T(128)} %bitcast.13, s32[2]{0:T(128)} %bitcast.11, bf16[2,2,128,128]{3,2,1,0:T(8,128)(2,1)} %bitcast.7, f32[24,2,128,128]{3,2,1,0:T(8,128)} %bitcast.9), custom_call_target="tpu_custom_call" | custom-call | flops 201326592 | bytes 5128392 | tf_op jit(solution)/shard_map/pallas_call | solution.py:274
  10.4 0.0 collective-permute-done.1.even_ref
  10.4 0.0 collective-permute-done.2.odd_ref
  10.4 0.0 collective-permute-done.all_ref
  10.5 0.5 %collective-permute-start.5 = (f32[2,2,128,128]{3,2,1,0:T(8,128)S(1)}, f32[2,2,128,128]{3,2,1,0:T(8,128)S(1)}, u32[]{:S(2)}, u32[]{:S(2)}) collective-permute-start(f32[2,2,128,128]{3,2,1,0:T(8,128)S(1)} %shard_map.57.known_ref), channel_id=1, source_target_pairs={{0,4},{1,5},{2,6},{3,7},{4,8},{5,9},{6,10},{7,11},{8,12},{9,13},{1... | collective-permute-start | bytes 786440 | tf_op jit(solution)/shard_map/ppermute | solution.py:46
  10.9 0.0 collective-permute-done.3.even_ref
  10.9 1.0 %collective-permute-done.4.odd_ref = f32[1,2,128,128]{3,2,1,0:T(8,128)S(1)} collective-permute-done((f32[1,2,128,128]{3,2,1,0:T(8,128)S(1)}, f32[1,2,128,128]{3,2,1,0:T(8,128)S(1)}, u32[]{:S(2)}, u32[]{:S(2)}) %collective-permute-start.4) | collective-permute-done | bytes 131104 | tf_op jit(solution)/shard_map/ppermute | solution.py:46
  12.0 0.0 copy-start
  12.0 0.5 %shard_map.58 = (f32[2,2,128,128]{3,2,1,0:T(8,128)S(1)}, f32[1,2,128,128]{3,2,1,0:T(8,128)S(1)}, f32[1,2,128,128]{3,2,1,0:T(8,128)S(1)}) custom-call(f32[2,1,2,8,128]{4,3,2,1,0:T(8,128)S(1)} %get-tuple-element.15.mask_ref, bf16[512,1536]{1,0:T(8,128)(2,1)S(1)} %get-tuple-element.14.matrix_ref, f32[2,2,128,128]{3,2,1,0:T(8,128)S(1)} %get-tuple-element.16.own_ref, ...), custom_call_target="tpu_custom_call" | custom-call | flops 99999997952 | bytes 1000000000 | tf_op jit(solution)/shard_map/pallas_call | solution.py:274
  12.4 0.4 %collective-permute-start.7 = (f32[1,2,128,128]{3,2,1,0:T(8,128)S(1)}, f32[1,2,128,128]{3,2,1,0:T(8,128)S(1)}, u32[]{:S(2)}, u32[]{:S(2)}) collective-permute-start(f32[1,2,128,128]{3,2,1,0:T(8,128)S(1)} %get-tuple-element.21), channel_id=1, source_target_pairs={{0,5},{1,4},{2,7},{3,6},{4,9},{5,8},{6,11},{7,10},{8,13},{9,12},{1... | collective-permute-start | bytes 393224 | tf_op jit(solution)/shard_map/ppermute | solution.py:46
  12.8 2.3 %collective-permute-start.8 = (f32[1,2,128,128]{3,2,1,0:T(8,128)S(1)}, f32[1,2,128,128]{3,2,1,0:T(8,128)S(1)}, u32[]{:S(2)}, u32[]{:S(2)}) collective-permute-start(f32[1,2,128,128]{3,2,1,0:T(8,128)S(1)} %get-tuple-element.22), channel_id=1, source_target_pairs={{0,4},{1,6},{2,5},{3,7},{4,8},{5,10},{6,9},{7,11},{8,12},{9,14},{1... | collective-permute-start | bytes 393224 | tf_op jit(solution)/shard_map/ppermute | solution.py:46
  15.1 0.0 collective-permute-start.6
  15.1 0.0 copy-done
  15.1 0.4 %shard_map.59.base_ref = f32[2,2,128,128]{3,2,1,0:T(8,128)S(1)} custom-call(bf16[512,1536]{1,0:T(8,128)(2,1)S(1)} %get-tuple-element.14.matrix_ref, bf16[2,2,128,128]{3,2,1,0:T(8,128)(2,1)S(1)} %bitcast.8, f32[2,2,128,128]{3,2,1,0:T(8,128)S(1)} %get-tuple-element.20.trace_ref), custom_call_target="tpu_custom_call" | custom-call | flops 201326592 | bytes 2228224 | tf_op jit(solution)/shard_map/pallas_call | solution.py:274
  15.5 1.7 %collective-permute-done.5.all_ref = f32[2,2,128,128]{3,2,1,0:T(8,128)S(1)} collective-permute-done((f32[2,2,128,128]{3,2,1,0:T(8,128)S(1)}, f32[2,2,128,128]{3,2,1,0:T(8,128)S(1)}, u32[]{:S(2)}, u32[]{:S(2)}) %collective-permute-start.5) | collective-permute-done | bytes 262176 | tf_op jit(solution)/shard_map/ppermute | solution.py:46
  17.2 0.4 %shard_map.60.base_ref = f32[2,2,128,128]{3,2,1,0:T(8,128)S(1)} custom-call(bf16[512,1536]{1,0:T(8,128)(2,1)S(1)} %get-tuple-element.14.matrix_ref, f32[2,2,128,128]{3,2,1,0:T(8,128)S(1)} %shard_map.59.base_ref, f32[2,2,128,128]{3,2,1,0:T(8,128)S(1)} %collective-permute-done.5.all_ref), custom_call_target="tpu_custom_call" | custom-call | flops 99999997952 | bytes 1000000000 | tf_op jit(solution)/shard_map/pallas_call | solution.py:274
  17.6 0.0 collective-permute-done.6.all_ref
  17.6 1.0 %collective-permute-done.7.even_ref = f32[1,2,128,128]{3,2,1,0:T(8,128)S(1)} collective-permute-done((f32[1,2,128,128]{3,2,1,0:T(8,128)S(1)}, f32[1,2,128,128]{3,2,1,0:T(8,128)S(1)}, u32[]{:S(2)}, u32[]{:S(2)}) %collective-permute-start.7) | collective-permute-done | bytes 131104 | tf_op jit(solution)/shard_map/ppermute | solution.py:46
  18.6 1.4 %collective-permute-done.8.odd_ref = f32[1,2,128,128]{3,2,1,0:T(8,128)S(1)} collective-permute-done((f32[1,2,128,128]{3,2,1,0:T(8,128)S(1)}, f32[1,2,128,128]{3,2,1,0:T(8,128)S(1)}, u32[]{:S(2)}, u32[]{:S(2)}) %collective-permute-start.8) | collective-permute-done | bytes 131104 | tf_op jit(solution)/shard_map/ppermute | solution.py:46
  20.0 1.1 %shard_map.62 = f32[2,2,128,128]{3,2,1,0:T(8,128)} custom-call(bf16[512,1536]{1,0:T(8,128)(2,1)S(1)} %get-tuple-element.14.matrix_ref, f32[2,2,128,128]{3,2,1,0:T(8,128)S(1)} %shard_map.61.base_ref, f32[1,2,128,128]{3,2,1,0:T(8,128)S(1)} %collective-permute-done.7.even_ref, f32[1,2,128,128]{3,2,1,0:T(8,128)S(1)} %collective-permute-done.8.odd_ref), custom_call_target="tpu_custom_call" | custom-call | flops 201326592 | bytes 2359296 | tf_op jit(solution)/shard_map/pallas_call | solution.py:274
  (2 shorter events, 0.1 us)
Async XLA Ops:
  1.0 9.4 %collective-permute-start = (f32[2,2,128,128]{3,2,1,0:T(8,128)S(1)}, f32[2,2,128,128]{3,2,1,0:T(8,128)S(1)}, u32[]{:S(2)}, u32[]{:S(2)}) collective-permute-start(f32[2,2,128,128]{3,2,1,0:T(8,128)S(1)} %get-tuple-element.17), channel_id=1, source_target_pairs={{0,4},{1,5},{2,6},{3,7},{4,8},{5,9},{6,10},{7,11},{8,12},{9,13},{1... | collective-permute-start | bytes 786440 | tf_op jit(solution)/shard_map/ppermute | solution.py:46
  1.5 8.9 %collective-permute-start.1 = (f32[1,2,128,128]{3,2,1,0:T(8,128)S(1)}, f32[1,2,128,128]{3,2,1,0:T(8,128)S(1)}, u32[]{:S(2)}, u32[]{:S(2)}) collective-permute-start(f32[1,2,128,128]{3,2,1,0:T(8,128)S(1)} %get-tuple-element.18), channel_id=1, source_target_pairs={{0,5},{1,4},{2,7},{3,6},{4,0},{5,1},{6,2},{7,3},{8,13},{9,12},{10,... | collective-permute-start | bytes 393224 | tf_op jit(solution)/shard_map/ppermute | solution.py:46
  5.3 5.1 %collective-permute-start.2 = (f32[1,2,128,128]{3,2,1,0:T(8,128)S(1)}, f32[1,2,128,128]{3,2,1,0:T(8,128)S(1)}, u32[]{:S(2)}, u32[]{:S(2)}) collective-permute-start(f32[1,2,128,128]{3,2,1,0:T(8,128)S(1)} %get-tuple-element.19), channel_id=1, source_target_pairs={{0,4},{1,6},{2,5},{3,7},{4,0},{5,1},{6,2},{7,3},{8,12},{9,14},{10,... | collective-permute-start | bytes 393224 | tf_op jit(solution)/shard_map/ppermute | solution.py:46
  5.3 5.7 %collective-permute-start.3 = (f32[1,2,128,128]{3,2,1,0:T(8,128)S(1)}, f32[1,2,128,128]{3,2,1,0:T(8,128)S(1)}, u32[]{:S(2)}, u32[]{:S(2)}) collective-permute-start(f32[1,2,128,128]{3,2,1,0:T(8,128)S(1)} %get-tuple-element.18), channel_id=1, source_target_pairs={{0,4},{1,5},{2,6},{3,7},{4,9},{5,8},{6,11},{7,10},{8,12},{9,13},{1... | collective-permute-start | bytes 393224 | tf_op jit(solution)/shard_map/ppermute | solution.py:46
  5.8 6.2 %collective-permute-start.4 = (f32[1,2,128,128]{3,2,1,0:T(8,128)S(1)}, f32[1,2,128,128]{3,2,1,0:T(8,128)S(1)}, u32[]{:S(2)}, u32[]{:S(2)}) collective-permute-start(f32[1,2,128,128]{3,2,1,0:T(8,128)S(1)} %get-tuple-element.19), channel_id=1, source_target_pairs={{0,4},{1,5},{2,6},{3,7},{4,8},{5,10},{6,9},{7,11},{8,12},{9,13},{1... | collective-permute-start | bytes 393224 | tf_op jit(solution)/shard_map/ppermute | solution.py:46
  10.5 6.7 %collective-permute-start.5 = (f32[2,2,128,128]{3,2,1,0:T(8,128)S(1)}, f32[2,2,128,128]{3,2,1,0:T(8,128)S(1)}, u32[]{:S(2)}, u32[]{:S(2)}) collective-permute-start(f32[2,2,128,128]{3,2,1,0:T(8,128)S(1)} %shard_map.57.known_ref), channel_id=1, source_target_pairs={{0,4},{1,5},{2,6},{3,7},{4,8},{5,9},{6,10},{7,11},{8,12},{9,13},{1... | collective-permute-start | bytes 786440 | tf_op jit(solution)/shard_map/ppermute | solution.py:46
  12.0 3.2 %copy-start = (bf16[1,2,2,128,128]{4,3,2,1,0:T(8,128)(2,1)S(1)}, bf16[1,2,2,128,128]{4,3,2,1,0:T(8,128)(2,1)}, u32[]{:S(2)}) copy-start(bf16[1,2,2,128,128]{4,3,2,1,0:T(8,128)(2,1)} %param.5) | copy-start | bytes 393220
  12.4 6.2 %collective-permute-start.7 = (f32[1,2,128,128]{3,2,1,0:T(8,128)S(1)}, f32[1,2,128,128]{3,2,1,0:T(8,128)S(1)}, u32[]{:S(2)}, u32[]{:S(2)}) collective-permute-start(f32[1,2,128,128]{3,2,1,0:T(8,128)S(1)} %get-tuple-element.21), channel_id=1, source_target_pairs={{0,5},{1,4},{2,7},{3,6},{4,9},{5,8},{6,11},{7,10},{8,13},{9,12},{1... | collective-permute-start | bytes 393224 | tf_op jit(solution)/shard_map/ppermute | solution.py:46
  12.8 7.2 %collective-permute-start.8 = (f32[1,2,128,128]{3,2,1,0:T(8,128)S(1)}, f32[1,2,128,128]{3,2,1,0:T(8,128)S(1)}, u32[]{:S(2)}, u32[]{:S(2)}) collective-permute-start(f32[1,2,128,128]{3,2,1,0:T(8,128)S(1)} %get-tuple-element.22), channel_id=1, source_target_pairs={{0,4},{1,6},{2,5},{3,7},{4,8},{5,10},{6,9},{7,11},{8,12},{9,14},{1... | collective-permute-start | bytes 393224 | tf_op jit(solution)/shard_map/ppermute | solution.py:46
  15.1 2.5 %collective-permute-start.6 = (f32[2,2,128,128]{3,2,1,0:T(8,128)S(1)}, f32[2,2,128,128]{3,2,1,0:T(8,128)S(1)}, u32[]{:S(2)}, u32[]{:S(2)}) collective-permute-start(f32[2,2,128,128]{3,2,1,0:T(8,128)S(1)} %get-tuple-element.20.trace_ref), channel_id=1, source_target_pairs={{0,4},{1,5},{2,6},{3,7},{4,0},{5,1},{6,2},{7,3},{8,12},{9,13},{10,... | collective-permute-start | bytes 786440 | tf_op jit(solution)/shard_map/ppermute | solution.py:46

commit v4 on v3

--- a/solution.py
+++ b/solution.py
@@ -8,7 +8,6 @@
 F32 = jnp.float32
 BF16 = jnp.bfloat16
 LIMIT = 40 * 1024 * 1024
-CHUNKS = 6
 
 
 def even_pair(p, planes):
@@ -46,8 +45,14 @@
     return lax.ppermute(block, ("layer", "plane"), route)
 
 
+def mixed(l, p, layers, planes, partner):
+    if l + 1 == layers:
+        return 0, p
+    return l + 1, partner[l % 2](p, planes)
+
+
 def onward(l, p, layers, planes, partner):
-    return (l + 1) % layers, partner(p, planes) if l + 1 < layers else p
+    return (l + 1) % layers, p
 
 
 def split(value):
@@ -111,19 +116,16 @@
 
 
 def prepare_kernel(
-    rows_hbm, cols_hbm, send_hbm, source_hbm, tiles_hbm,
+    rows_hbm, cols_hbm, send_hbm, source_hbm, tiles_ref,
     matrix_ref, own_ref, mask_ref,
-    rows_ref, cols_ref, send_ref, source_ref, tiles_ref, total, sems,
+    rows_ref, cols_ref, send_ref, source_ref, total, sems,
 ):
     tile_count, _, width, _ = tiles_ref.shape
     blocks_here = source_ref.shape[0]
     extended = total.shape[0] // blocks_here
     listed = (extended - 2 * blocks_here) // 2
     small = [(rows_hbm, rows_ref), (cols_hbm, cols_ref), (send_hbm, send_ref)]
-    chunk = tile_count // CHUNKS if tile_count % CHUNKS == 0 else tile_count
-    parts = [pl.ds(first, chunk) for first in range(0, tile_count, chunk)]
-    large = [(tiles_hbm.at[part], tiles_ref.at[part]) for part in parts]
-    copies = fetch(small + large + [(source_hbm, source_ref)], sems)
+    copies = fetch(small + [(source_hbm, source_ref)], sems)
     layer = lax.axis_index("layer")
     plane = lax.axis_index("plane")
     planes = lax.axis_size("plane")
@@ -149,9 +151,7 @@
         for b in range(blocks_here):
             for kind, chosen in enumerate((to_even, to_odd)):
                 mask_ref[kind, k, b] = jnp.full(mask_ref.shape[3:], jnp.where(chosen == b, 1.0, 0.0), F32)
-    for i, copy in enumerate(copies[3:-1]):
-        copy.wait()
-        lax.fori_loop(i * chunk, (i + 1) * chunk, add, 0, unroll=True)
+    lax.fori_loop(0, tile_count, add, 0, unroll=8)
     has_layer = layer > 0
     has_next = plane + 1 < planes
     has_even = has_layer & ((is_odd == 1) | has_next)
@@ -183,16 +183,15 @@
     return [(ref[b, 0], ref[b, 1]) for ref in refs for b in range(ref.shape[0])]
 
 
-def choose(mask_ref, new_ref, even_ref, odd_ref):
+def choose(mask_ref, kind, new_ref, out_ref):
     count, _, width, shots = new_ref.shape
     rows = mask_ref.shape[3]
-    for kind, out_ref in enumerate((even_ref, odd_ref)):
-        for k in range(out_ref.shape[0]):
-            chosen = jnp.zeros((2, width // rows, rows, shots), F32)
-            for b in range(count):
-                block = new_ref[b].reshape(chosen.shape)
-                chosen = jnp.where(mask_ref[kind, k, b][None, None] > 0.5, block, chosen)
-            out_ref[k] = chosen.reshape(2, width, shots)
+    for k in range(out_ref.shape[0]):
+        chosen = jnp.zeros((2, width // rows, rows, shots), F32)
+        for b in range(count):
+            block = new_ref[b].reshape(chosen.shape)
+            chosen = jnp.where(mask_ref[kind, k, b][None, None] > 0.5, block, chosen)
+        out_ref[k] = chosen.reshape(2, width, shots)
 
 
 def second_tick(matrix_ref, own_ref, arrived_refs, new_ref):
@@ -205,7 +204,7 @@
     return lax.axis_index("layer") % 2 == 1
 
 
-def odd_kernel(matrix_ref, own_ref, all_ref, even_ref, odd_ref, new_ref):
+def odd_kernel(mask_ref, matrix_ref, own_ref, all_ref, even_ref, odd_ref, new_ref, new_even_ref):
     @pl.when(on_odd_layer())
     def _():
         second_tick(matrix_ref, own_ref, (all_ref, even_ref, odd_ref), new_ref)
@@ -214,17 +213,32 @@
     def _():
         new_ref[...] = own_ref[...]
 
-
-def even_kernel(mask_ref, matrix_ref, own_ref, known_ref, all_ref, even_ref, odd_ref, new_ref, new_even_ref, new_odd_ref):
+    choose(mask_ref, 0, new_ref, new_even_ref)
+
+
+def on_even_layer():
+    layer = lax.axis_index("layer")
+    return (layer % 2 == 0) & (layer > 0)
+
+
+def even_kernel(mask_ref, matrix_ref, own_ref, known_ref, all_ref, even_ref, odd_ref, new_ref, mixed_ref, new_odd_ref):
+    @pl.when(jnp.logical_not(on_even_layer()))
+    def _():
+        new_ref[...] = known_ref[...]
+
+    @pl.when(on_even_layer())
+    def _():
+        second_tick(matrix_ref, own_ref, (all_ref, even_ref, odd_ref), new_ref)
+
+    choose(mask_ref, 1, new_ref, new_odd_ref)
+
     @pl.when(on_odd_layer())
     def _():
-        new_ref[...] = known_ref[...]
+        mixed_ref[...] = new_odd_ref[...]
 
     @pl.when(jnp.logical_not(on_odd_layer()))
     def _():
-        second_tick(matrix_ref, own_ref, (all_ref, even_ref, odd_ref), new_ref)
-
-    choose(mask_ref, new_ref, new_even_ref, new_odd_ref)
+        choose(mask_ref, 0, new_ref, mixed_ref)
 
 
 def own_kernel(matrix_ref, source_ref, trace_ref, own_ref):
@@ -240,14 +254,14 @@
     store(three_products(matrix_ref, columns, blocks), base_ref, out_ref)
 
 
-def even_whole_kernel(matrix_ref, base_ref, all_ref, out_ref):
-    @pl.when(on_odd_layer())
+def even_last_kernel(matrix_ref, base_ref, all_ref, even_ref, out_ref):
+    @pl.when(jnp.logical_not(on_even_layer()))
     def _():
         out_ref[...] = base_ref[...]
 
-    @pl.when(jnp.logical_not(on_odd_layer()))
-    def _():
-        third_tick(matrix_ref, 0, base_ref, (all_ref,), out_ref)
+    @pl.when(on_even_layer())
+    def _():
+        third_tick(matrix_ref, 0, base_ref, (all_ref, even_ref), out_ref)
 
 
 def odd_whole_kernel(matrix_ref, base_ref, all_ref, out_ref):
@@ -260,21 +274,33 @@
         out_ref[...] = base_ref[...]
 
 
-def last_kernel(matrix_ref, base_ref, even_ref, odd_ref, out_ref):
-    third_tick(matrix_ref, base_ref.shape[0], base_ref, (even_ref, odd_ref), out_ref)
+def last_kernel(matrix_ref, base_ref, mixed_ref, odd_ref, out_ref):
+    blocks = base_ref.shape[0]
+
+    @pl.when(on_odd_layer())
+    def _():
+        third_tick(matrix_ref, blocks, base_ref, (mixed_ref, odd_ref), out_ref)
+
+    @pl.when(on_even_layer())
+    def _():
+        third_tick(matrix_ref, blocks + mixed_ref.shape[0], base_ref, (mixed_ref,), out_ref)
+
+    @pl.when(lax.axis_index("layer") == 0)
+    def _():
+        out_ref[...] = base_ref[...]
 
 
 def call(kernel, ins, outs, flops, scratch=(), in_hbm=False, moved=None):
     if moved is None:
         moved = sum(x.size * x.dtype.itemsize for x in (*ins, *outs))
     if in_hbm:
-        ins = [pltpu.with_memory_space_constraint(x, pltpu.HBM) for x in ins]
+        ins = [x if x.size > 10**6 // 2 else pltpu.with_memory_space_constraint(x, pltpu.HBM) for x in ins]
     vmem = pl.BlockSpec(memory_space=pltpu.VMEM)
     hbm = pl.BlockSpec(memory_space=pltpu.HBM)
     return pl.pallas_call(
         kernel,
         out_shape=outs,
-        in_specs=[hbm if in_hbm else vmem] * len(ins),
+        in_specs=[hbm if in_hbm and x.size <= 10**6 // 2 else vmem for x in ins],
         out_specs=[vmem] * len(outs),
         scratch_shapes=scratch,
         compiler_params=pltpu.CompilerParams(vmem_limit_bytes=LIMIT),
@@ -304,13 +330,14 @@
         widen_kernel,
         (send, source),
         (trace, part, part),
-        0,
+        10**11,
         [send_copy, source_copy, pltpu.SemaphoreType.DMA((2,))],
         in_hbm=True,
+        moved=10**8,
     )
     whole = permute(whole, onward, same)
+    from_odd = permute(even, outward, even_pair), permute(odd, outward, odd_pair)
     from_even = permute(even, inward, even_pair), permute(odd, inward, odd_pair)
-    from_odd = permute(even, outward, even_pair), permute(odd, outward, odd_pair)
     matrix, own, mask = call(
         prepare_kernel,
         (rows, cols, send, source, tiles),
@@ -321,24 +348,24 @@
             pltpu.SMEM(cols.shape, cols.dtype),
             send_copy,
             source_copy,
-            pltpu.VMEM(tiles.shape, F32),
             pltpu.VMEM((blocks * extended, width, 2 * width), F32),
-            pltpu.SemaphoreType.DMA((CHUNKS + 4,)),
+            pltpu.SemaphoreType.DMA((4,)),
         ],
         in_hbm=True,
     )
-    (second,) = call(odd_kernel, (matrix, own, whole, *from_even), (trace,), flops)
+    second, even = call(odd_kernel, (mask, matrix, own, whole, *from_even), (trace, part), flops)
     early = permute(second, outward, same)
+    early_even = permute(even, outward, even_pair)
     traces, even, odd = call(
-        even_kernel, (mask, matrix, own, second, whole, *from_odd), (trace, part, part), 10**11, moved=10**9
-    )
+        even_kernel, (mask, matrix, own, second, whole, *from_odd), (trace, part, part), 2000000000, moved=0
+    )
+    late_mixed = permute(even, mixed, (even_pair, odd_pair))
+    late_odd = permute(odd, inward, odd_pair)
     late = permute(traces, inward, same)
-    even = permute(even, onward, even_pair)
-    odd = permute(odd, onward, odd_pair)
     (own,) = call(own_kernel, (matrix, source, traces), (trace,), flops)
-    (own,) = call(even_whole_kernel, (matrix, own, early), (trace,), 10**11, moved=10**9)
+    (own,) = call(even_last_kernel, (matrix, own, early, early_even), (trace,), 10**11, moved=10**9)
     (own,) = call(odd_whole_kernel, (matrix, own, late), (trace,), flops)
-    (out,) = call(last_kernel, (matrix, own, even, odd), (trace,), flops)
+    (out,) = call(last_kernel, (matrix, own, late_mixed, late_odd), (trace,), flops)
     return out[None]
 
 

time: 21.2 us -> 20.5 us (0.967)
  the two profiles are of different devices: /device:TPU:0 before, /device:TPU:11 now
where the time goes in v4:
time: 20.5 us; the launch traced here: 20.4 us
  starting transfers between devices  11.6 us (57%)
  Pallas kernels  5.07 us (25%)
  waiting for transfers between devices  3.55 us (17%)
    ppermute x10, starting transfers between devices, permute(): return lax.ppermute(block, ('layer', 'plane'), route)  11.6 us
    pallas_call x8, Pallas kernels, call(): pl.pallas_call(kernel, out_shape=outs, in_specs=[hbm if in_hbm and x.size...  5.07 us
    ppermute x10, waiting for transfers between devices, permute(): return lax.ppermute(block, ('layer', 'plane'), route)  3.55 us
  transfers between devices with their start and end apart: 10, of which 4 were waited for; matrix products, arithmetic and copies ran while one was open for 0% of the time, Pallas kernels for 14%

profile of v4, /device:TPU:11, one launch (start us, length us, event | category | flops | bytes accessed | tf_op | source)
XLA Modules:
  0.0 20.4 jit_solution(16923960302666736608)
XLA Ops:
  0.0 0.0 copy-start
  0.0 1.1 %shard_map.56 = (f32[2,2,128,128]{3,2,1,0:T(8,128)S(1)}, f32[1,2,128,128]{3,2,1,0:T(8,128)S(1)}, f32[1,2,128,128]{3,2,1,0:T(8,128)S(1)}) custom-call(s32[2]{0:T(128)} %bitcast.12, bf16[2,2,128,128]{3,2,1,0:T(8,128)(2,1)} %bitcast.7), custom_call_target="tpu_custom_call" | custom-call | flops 99999997952 | bytes 100000000 | tf_op jit(solution)/shard_map/pallas_call | solution.py:300
  1.1 1.8 %collective-permute-start = (f32[2,2,128,128]{3,2,1,0:T(8,128)S(1)}, f32[2,2,128,128]{3,2,1,0:T(8,128)S(1)}, u32[]{:S(2)}, u32[]{:S(2)}) collective-permute-start(f32[2,2,128,128]{3,2,1,0:T(8,128)S(1)} %get-tuple-element.19), channel_id=1, source_target_pairs={{0,4},{1,5},{2,6},{3,7},{4,8},{5,9},{6,10},{7,11},{8,12},{9,13},{1... | collective-permute-start | bytes 786440 | tf_op jit(solution)/shard_map/ppermute | solution.py:45
  3.0 0.0 collective-permute-start.1
  3.0 0.6 %collective-permute-start.2 = (f32[1,2,128,128]{3,2,1,0:T(8,128)S(1)}, f32[1,2,128,128]{3,2,1,0:T(8,128)S(1)}, u32[]{:S(2)}, u32[]{:S(2)}) collective-permute-start(f32[1,2,128,128]{3,2,1,0:T(8,128)S(1)} %get-tuple-element.21), channel_id=1, source_target_pairs={{0,4},{1,6},{2,5},{3,7},{4,0},{5,1},{6,2},{7,3},{8,12},{9,14},{10,... | collective-permute-start | bytes 393224 | tf_op jit(solution)/shard_map/ppermute | solution.py:45
  3.5 2.1 %collective-permute-start.3 = (f32[1,2,128,128]{3,2,1,0:T(8,128)S(1)}, f32[1,2,128,128]{3,2,1,0:T(8,128)S(1)}, u32[]{:S(2)}, u32[]{:S(2)}) collective-permute-start(f32[1,2,128,128]{3,2,1,0:T(8,128)S(1)} %get-tuple-element.20), channel_id=1, source_target_pairs={{0,4},{1,5},{2,6},{3,7},{4,9},{5,8},{6,11},{7,10},{8,12},{9,13},{1... | collective-permute-start | bytes 393224 | tf_op jit(solution)/shard_map/ppermute | solution.py:45
  5.6 1.6 %collective-permute-start.4 = (f32[1,2,128,128]{3,2,1,0:T(8,128)S(1)}, f32[1,2,128,128]{3,2,1,0:T(8,128)S(1)}, u32[]{:S(2)}, u32[]{:S(2)}) collective-permute-start(f32[1,2,128,128]{3,2,1,0:T(8,128)S(1)} %get-tuple-element.21), channel_id=1, source_target_pairs={{0,4},{1,5},{2,6},{3,7},{4,8},{5,10},{6,9},{7,11},{8,12},{9,13},{1... | collective-permute-start | bytes 393224 | tf_op jit(solution)/shard_map/ppermute | solution.py:45
  7.3 0.0 copy-done
  7.3 1.6 %shard_map.55 = (bf16[512,1536]{1,0:T(8,128)(2,1)S(1)}, f32[2,2,128,128]{3,2,1,0:T(8,128)S(1)}, f32[2,1,2,8,128]{4,3,2,1,0:T(8,128)S(1)}) custom-call(s32[24]{0:T(128)} %bitcast.10, s32[24]{0:T(128)} %bitcast.11, s32[2]{0:T(128)} %bitcast.13, bf16[2,2,128,128]{3,2,1,0:T(8,128)(2,1)} %bitcast.8, f32[24,2,128,128]{3,2,1,0:T(8,128)S(1)} %bitcast.6), custom_call_target="tpu_custom_call" | custom-call | flops 201326592 | bytes 5128392 | tf_op jit(solution)/shard_map/pallas_call | solution.py:300
  8.8 0.0 collective-permute-done.1.even_ref
  8.9 0.5 %collective-permute-done.2.odd_ref = f32[1,2,128,128]{3,2,1,0:T(8,128)S(1)} collective-permute-done((f32[1,2,128,128]{3,2,1,0:T(8,128)S(1)}, f32[1,2,128,128]{3,2,1,0:T(8,128)S(1)}, u32[]{:S(2)}, u32[]{:S(2)}) %collective-permute-start.2) | collective-permute-done | bytes 131104 | tf_op jit(solution)/shard_map/ppermute | solution.py:45
  9.4 0.0 collective-permute-done.all_ref
  9.4 0.5 %shard_map.57 = (f32[2,2,128,128]{3,2,1,0:T(8,128)S(1)}, f32[1,2,128,128]{3,2,1,0:T(8,128)S(1)}) custom-call(f32[2,1,2,8,128]{4,3,2,1,0:T(8,128)S(1)} %get-tuple-element.17.mask_ref, bf16[512,1536]{1,0:T(8,128)(2,1)S(1)} %get-tuple-element.16.matrix_ref, f32[2,2,128,128]{3,2,1,0:T(8,128)S(1)} %get-tuple-element.18.own_ref, ...), custom_call_target="tpu_custom_call" | custom-call | flops 201326592 | bytes 2768896 | tf_op jit(solution)/shard_map/pallas_call | solution.py:300
  9.9 0.1 collective-permute-start.5
  9.9 0.0 copy-start.1
  9.9 0.2 %collective-permute-start.6 = (f32[1,2,128,128]{3,2,1,0:T(8,128)S(1)}, f32[1,2,128,128]{3,2,1,0:T(8,128)S(1)}, u32[]{:S(2)}, u32[]{:S(2)}) collective-permute-start(f32[1,2,128,128]{3,2,1,0:T(8,128)S(1)} %get-tuple-element.24), channel_id=1, source_target_pairs={{0,4},{1,5},{2,6},{3,7},{4,9},{5,8},{6,11},{7,10},{8,12},{9,13},{1... | collective-permute-start | bytes 393224 | tf_op jit(solution)/shard_map/ppermute | solution.py:45
  10.2 0.0 collective-permute-done.3.even_ref
  10.2 0.0 collective-permute-done.4.odd_ref
  10.2 4.7 %collective-permute-start.8 = (f32[1,2,128,128]{3,2,1,0:T(8,128)S(1)}, f32[1,2,128,128]{3,2,1,0:T(8,128)S(1)}, u32[]{:S(2)}, u32[]{:S(2)}) collective-permute-start(f32[1,2,128,128]{3,2,1,0:T(8,128)S(1)} %get-tuple-element.25), channel_id=1, source_target_pairs={{0,5},{1,4},{2,7},{3,6},{4,8},{5,10},{6,9},{7,11},{8,13},{9,12},{1... | collective-permute-start | bytes 393224 | tf_op jit(solution)/shard_map/ppermute | solution.py:45
  14.9 0.0 collective-permute-start.9
  14.9 0.6 %collective-permute-start.7 = (f32[2,2,128,128]{3,2,1,0:T(8,128)S(1)}, f32[2,2,128,128]{3,2,1,0:T(8,128)S(1)}, u32[]{:S(2)}, u32[]{:S(2)}) collective-permute-start(f32[2,2,128,128]{3,2,1,0:T(8,128)S(1)} %get-tuple-element.23.trace_ref), channel_id=1, source_target_pairs={{0,4},{1,5},{2,6},{3,7},{4,0},{5,1},{6,2},{7,3},{8,12},{9,13},{10,... | collective-permute-start | bytes 786440 | tf_op jit(solution)/shard_map/ppermute | solution.py:45
  15.5 0.0 copy-done.1
  15.5 0.4 %shard_map.59.base_ref = f32[2,2,128,128]{3,2,1,0:T(8,128)S(1)} custom-call(bf16[512,1536]{1,0:T(8,128)(2,1)S(1)} %get-tuple-element.16.matrix_ref, bf16[2,2,128,128]{3,2,1,0:T(8,128)(2,1)S(1)} %bitcast.9, f32[2,2,128,128]{3,2,1,0:T(8,128)S(1)} %get-tuple-element.23.trace_ref), custom_call_target="tpu_custom_call" | custom-call | flops 201326592 | bytes 2228224 | tf_op jit(solution)/shard_map/pallas_call | solution.py:300
  15.8 0.0 collective-permute-done.6.even_ref
  15.8 0.0 collective-permute-done.5.all_ref
  15.9 0.7 %collective-permute-done.7.all_ref = f32[2,2,128,128]{3,2,1,0:T(8,128)S(1)} collective-permute-done((f32[2,2,128,128]{3,2,1,0:T(8,128)S(1)}, f32[2,2,128,128]{3,2,1,0:T(8,128)S(1)}, u32[]{:S(2)}, u32[]{:S(2)}) %collective-permute-start.7) | collective-permute-done | bytes 262176 | tf_op jit(solution)/shard_map/ppermute | solution.py:45
  16.6 0.4 %shard_map.61.base_ref = f32[2,2,128,128]{3,2,1,0:T(8,128)S(1)} custom-call(bf16[512,1536]{1,0:T(8,128)(2,1)S(1)} %get-tuple-element.16.matrix_ref, f32[2,2,128,128]{3,2,1,0:T(8,128)S(1)} %shard_map.60.base_ref, f32[2,2,128,128]{3,2,1,0:T(8,128)S(1)} %collective-permute-done.7.all_ref), custom_call_target="tpu_custom_call" | custom-call | flops 201326592 | bytes 2359296 | tf_op jit(solution)/shard_map/pallas_call | solution.py:300
  17.0 0.5 %collective-permute-done.8.mixed_ref = f32[1,2,128,128]{3,2,1,0:T(8,128)S(1)} collective-permute-done((f32[1,2,128,128]{3,2,1,0:T(8,128)S(1)}, f32[1,2,128,128]{3,2,1,0:T(8,128)S(1)}, u32[]{:S(2)}, u32[]{:S(2)}) %collective-permute-start.8) | collective-permute-done | bytes 131104 | tf_op jit(solution)/shard_map/ppermute | solution.py:45
  17.5 1.8 %collective-permute-done.9.odd_ref = f32[1,2,128,128]{3,2,1,0:T(8,128)S(1)} collective-permute-done((f32[1,2,128,128]{3,2,1,0:T(8,128)S(1)}, f32[1,2,128,128]{3,2,1,0:T(8,128)S(1)}, u32[]{:S(2)}, u32[]{:S(2)}) %collective-permute-start.9) | collective-permute-done | bytes 131104 | tf_op jit(solution)/shard_map/ppermute | solution.py:45
  19.3 1.1 %shard_map.62 = f32[2,2,128,128]{3,2,1,0:T(8,128)} custom-call(bf16[512,1536]{1,0:T(8,128)(2,1)S(1)} %get-tuple-element.16.matrix_ref, f32[2,2,128,128]{3,2,1,0:T(8,128)S(1)} %shard_map.61.base_ref, f32[1,2,128,128]{3,2,1,0:T(8,128)S(1)} %collective-permute-done.8.mixed_ref, f32[1,2,128,128]{3,2,1,0:T(8,128)S(1)} %collective-permute-done.9.odd_ref), custom_call_target="tpu_custom_call" | custom-call | flops 201326592 | bytes 2359296 | tf_op jit(solution)/shard_map/pallas_call | solution.py:300
  (2 shorter events, 0.1 us)
Async XLA Ops:
  0.0 7.3 %copy-start = (f32[1,24,2,128,128]{4,3,2,1,0:T(8,128)S(1)}, f32[1,24,2,128,128]{4,3,2,1,0:T(8,128)}, u32[]{:S(2)}) copy-start(f32[1,24,2,128,128]{4,3,2,1,0:T(8,128)} %param.6) | copy-start | bytes 9437188
  1.1 8.3 %collective-permute-start = (f32[2,2,128,128]{3,2,1,0:T(8,128)S(1)}, f32[2,2,128,128]{3,2,1,0:T(8,128)S(1)}, u32[]{:S(2)}, u32[]{:S(2)}) collective-permute-start(f32[2,2,128,128]{3,2,1,0:T(8,128)S(1)} %get-tuple-element.19), channel_id=1, source_target_pairs={{0,4},{1,5},{2,6},{3,7},{4,8},{5,9},{6,10},{7,11},{8,12},{9,13},{1... | collective-permute-start | bytes 786440 | tf_op jit(solution)/shard_map/ppermute | solution.py:45
  3.0 5.9 %collective-permute-start.1 = (f32[1,2,128,128]{3,2,1,0:T(8,128)S(1)}, f32[1,2,128,128]{3,2,1,0:T(8,128)S(1)}, u32[]{:S(2)}, u32[]{:S(2)}) collective-permute-start(f32[1,2,128,128]{3,2,1,0:T(8,128)S(1)} %get-tuple-element.20), channel_id=1, source_target_pairs={{0,5},{1,4},{2,7},{3,6},{4,0},{5,1},{6,2},{7,3},{8,13},{9,12},{10,... | collective-permute-start | bytes 393224 | tf_op jit(solution)/shard_map/ppermute | solution.py:45
  3.0 6.4 %collective-permute-start.2 = (f32[1,2,128,128]{3,2,1,0:T(8,128)S(1)}, f32[1,2,128,128]{3,2,1,0:T(8,128)S(1)}, u32[]{:S(2)}, u32[]{:S(2)}) collective-permute-start(f32[1,2,128,128]{3,2,1,0:T(8,128)S(1)} %get-tuple-element.21), channel_id=1, source_target_pairs={{0,4},{1,6},{2,5},{3,7},{4,0},{5,1},{6,2},{7,3},{8,12},{9,14},{10,... | collective-permute-start | bytes 393224 | tf_op jit(solution)/shard_map/ppermute | solution.py:45
  3.5 6.6 %collective-permute-start.3 = (f32[1,2,128,128]{3,2,1,0:T(8,128)S(1)}, f32[1,2,128,128]{3,2,1,0:T(8,128)S(1)}, u32[]{:S(2)}, u32[]{:S(2)}) collective-permute-start(f32[1,2,128,128]{3,2,1,0:T(8,128)S(1)} %get-tuple-element.20), channel_id=1, source_target_pairs={{0,4},{1,5},{2,6},{3,7},{4,9},{5,8},{6,11},{7,10},{8,12},{9,13},{1... | collective-permute-start | bytes 393224 | tf_op jit(solution)/shard_map/ppermute | solution.py:45
  5.6 4.5 %collective-permute-start.4 = (f32[1,2,128,128]{3,2,1,0:T(8,128)S(1)}, f32[1,2,128,128]{3,2,1,0:T(8,128)S(1)}, u32[]{:S(2)}, u32[]{:S(2)}) collective-permute-start(f32[1,2,128,128]{3,2,1,0:T(8,128)S(1)} %get-tuple-element.21), channel_id=1, source_target_pairs={{0,4},{1,5},{2,6},{3,7},{4,8},{5,10},{6,9},{7,11},{8,12},{9,13},{1... | collective-permute-start | bytes 393224 | tf_op jit(solution)/shard_map/ppermute | solution.py:45
  9.9 6.0 %collective-permute-start.5 = (f32[2,2,128,128]{3,2,1,0:T(8,128)S(1)}, f32[2,2,128,128]{3,2,1,0:T(8,128)S(1)}, u32[]{:S(2)}, u32[]{:S(2)}) collective-permute-start(f32[2,2,128,128]{3,2,1,0:T(8,128)S(1)} %get-tuple-element.22.known_ref), channel_id=1, source_target_pairs={{0,4},{1,5},{2,6},{3,7},{4,8},{5,9},{6,10},{7,11},{8,12},{9,13},{1... | collective-permute-start | bytes 786440 | tf_op jit(solution)/shard_map/ppermute | solution.py:45
  9.9 5.5 %copy-start.1 = (bf16[1,2,2,128,128]{4,3,2,1,0:T(8,128)(2,1)S(1)}, bf16[1,2,2,128,128]{4,3,2,1,0:T(8,128)(2,1)}, u32[]{:S(2)}) copy-start(bf16[1,2,2,128,128]{4,3,2,1,0:T(8,128)(2,1)} %param.5) | copy-start | bytes 393220
  9.9 5.9 %collective-permute-start.6 = (f32[1,2,128,128]{3,2,1,0:T(8,128)S(1)}, f32[1,2,128,128]{3,2,1,0:T(8,128)S(1)}, u32[]{:S(2)}, u32[]{:S(2)}) collective-permute-start(f32[1,2,128,128]{3,2,1,0:T(8,128)S(1)} %get-tuple-element.24), channel_id=1, source_target_pairs={{0,4},{1,5},{2,6},{3,7},{4,9},{5,8},{6,11},{7,10},{8,12},{9,13},{1... | collective-permute-start | bytes 393224 | tf_op jit(solution)/shard_map/ppermute | solution.py:45
  10.2 7.3 %collective-permute-start.8 = (f32[1,2,128,128]{3,2,1,0:T(8,128)S(1)}, f32[1,2,128,128]{3,2,1,0:T(8,128)S(1)}, u32[]{:S(2)}, u32[]{:S(2)}) collective-permute-start(f32[1,2,128,128]{3,2,1,0:T(8,128)S(1)} %get-tuple-element.25), channel_id=1, source_target_pairs={{0,5},{1,4},{2,7},{3,6},{4,8},{5,10},{6,9},{7,11},{8,13},{9,12},{1... | collective-permute-start | bytes 393224 | tf_op jit(solution)/shard_map/ppermute | solution.py:45
  14.9 4.4 %collective-permute-start.9 = (f32[1,2,128,128]{3,2,1,0:T(8,128)S(1)}, f32[1,2,128,128]{3,2,1,0:T(8,128)S(1)}, u32[]{:S(2)}, u32[]{:S(2)}) collective-permute-start(f32[1,2,128,128]{3,2,1,0:T(8,128)S(1)} %get-tuple-element.26), channel_id=1, source_target_pairs={{0,4},{1,6},{2,5},{3,7},{4,0},{5,1},{6,2},{7,3},{8,12},{9,14},{10,... | collective-permute-start | bytes 393224 | tf_op jit(solution)/shard_map/ppermute | solution.py:45
  14.9 1.7 %collective-permute-start.7 = (f32[2,2,128,128]{3,2,1,0:T(8,128)S(1)}, f32[2,2,128,128]{3,2,1,0:T(8,128)S(1)}, u32[]{:S(2)}, u32[]{:S(2)}) collective-permute-start(f32[2,2,128,128]{3,2,1,0:T(8,128)S(1)} %get-tuple-element.23.trace_ref), channel_id=1, source_target_pairs={{0,4},{1,5},{2,6},{3,7},{4,0},{5,1},{6,2},{7,3},{8,12},{9,13},{10,... | collective-permute-start | bytes 786440 | tf_op jit(solution)/shard_map/ppermute | solution.py:45

commit v5 on v4

--- a/solution.py
+++ b/solution.py
@@ -45,14 +45,16 @@
     return lax.ppermute(block, ("layer", "plane"), route)
 
 
-def mixed(l, p, layers, planes, partner):
-    if l + 1 == layers:
-        return 0, p
-    return l + 1, partner[l % 2](p, planes)
-
-
 def onward(l, p, layers, planes, partner):
     return (l + 1) % layers, p
+
+
+def with_mate(block):
+    layers = lax.axis_size("layer")
+    if layers % 2:
+        return permute(block, inward, same)[None]
+    groups = [[l, l + 1] for l in range(0, layers, 2)]
+    return lax.all_gather(block, "layer", axis_index_groups=groups)
 
 
 def split(value):
@@ -204,7 +206,7 @@
     return lax.axis_index("layer") % 2 == 1
 
 
-def odd_kernel(mask_ref, matrix_ref, own_ref, all_ref, even_ref, odd_ref, new_ref, new_even_ref):
+def odd_kernel(mask_ref, matrix_ref, own_ref, all_ref, even_ref, odd_ref, new_ref, new_even_ref, new_odd_ref):
     @pl.when(on_odd_layer())
     def _():
         second_tick(matrix_ref, own_ref, (all_ref, even_ref, odd_ref), new_ref)
@@ -214,6 +216,7 @@
         new_ref[...] = own_ref[...]
 
     choose(mask_ref, 0, new_ref, new_even_ref)
+    choose(mask_ref, 1, new_ref, new_odd_ref)
 
 
 def on_even_layer():
@@ -221,7 +224,7 @@
     return (layer % 2 == 0) & (layer > 0)
 
 
-def even_kernel(mask_ref, matrix_ref, own_ref, known_ref, all_ref, even_ref, odd_ref, new_ref, mixed_ref, new_odd_ref):
+def even_kernel(mask_ref, matrix_ref, own_ref, known_ref, all_ref, even_ref, odd_ref, new_ref, new_even_ref, new_odd_ref):
     @pl.when(jnp.logical_not(on_even_layer()))
     def _():
         new_ref[...] = known_ref[...]
@@ -230,15 +233,8 @@
     def _():
         second_tick(matrix_ref, own_ref, (all_ref, even_ref, odd_ref), new_ref)
 
+    choose(mask_ref, 0, new_ref, new_even_ref)
     choose(mask_ref, 1, new_ref, new_odd_ref)
-
-    @pl.when(on_odd_layer())
-    def _():
-        mixed_ref[...] = new_odd_ref[...]
-
-    @pl.when(jnp.logical_not(on_odd_layer()))
-    def _():
-        choose(mask_ref, 0, new_ref, mixed_ref)
 
 
 def own_kernel(matrix_ref, source_ref, trace_ref, own_ref):
@@ -254,7 +250,17 @@
     store(three_products(matrix_ref, columns, blocks), base_ref, out_ref)
 
 
-def even_last_kernel(matrix_ref, base_ref, all_ref, even_ref, out_ref):
+def mate_kernel(matrix_ref, base_ref, pair_ref, out_ref):
+    @pl.when(jnp.logical_not(on_odd_layer()))
+    def _():
+        out_ref[...] = base_ref[...]
+
+    @pl.when(on_odd_layer())
+    def _():
+        third_tick(matrix_ref, 0, base_ref, (pair_ref.at[0],), out_ref)
+
+
+def even_part_kernel(matrix_ref, base_ref, all_ref, even_ref, out_ref):
     @pl.when(jnp.logical_not(on_even_layer()))
     def _():
         out_ref[...] = base_ref[...]
@@ -264,26 +270,16 @@
         third_tick(matrix_ref, 0, base_ref, (all_ref, even_ref), out_ref)
 
 
-def odd_whole_kernel(matrix_ref, base_ref, all_ref, out_ref):
+def last_kernel(matrix_ref, base_ref, outer_odd_ref, inner_even_ref, inner_odd_ref, out_ref):
+    blocks = base_ref.shape[0]
+
     @pl.when(on_odd_layer())
     def _():
-        third_tick(matrix_ref, 0, base_ref, (all_ref,), out_ref)
-
-    @pl.when(jnp.logical_not(on_odd_layer()))
-    def _():
-        out_ref[...] = base_ref[...]
-
-
-def last_kernel(matrix_ref, base_ref, mixed_ref, odd_ref, out_ref):
-    blocks = base_ref.shape[0]
-
-    @pl.when(on_odd_layer())
-    def _():
-        third_tick(matrix_ref, blocks, base_ref, (mixed_ref, odd_ref), out_ref)
+        third_tick(matrix_ref, blocks, base_ref, (inner_even_ref, inner_odd_ref), out_ref)
 
     @pl.when(on_even_layer())
     def _():
-        third_tick(matrix_ref, blocks + mixed_ref.shape[0], base_ref, (mixed_ref,), out_ref)
+        third_tick(matrix_ref, blocks + inner_even_ref.shape[0], base_ref, (outer_odd_ref,), out_ref)
 
     @pl.when(lax.axis_index("layer") == 0)
     def _():
@@ -353,19 +349,17 @@
         ],
         in_hbm=True,
     )
-    second, even = call(odd_kernel, (mask, matrix, own, whole, *from_even), (trace, part), flops)
-    early = permute(second, outward, same)
-    early_even = permute(even, outward, even_pair)
+    second, even, odd = call(odd_kernel, (mask, matrix, own, whole, *from_even), (trace, part, part), flops)
+    early = permute(second, outward, same), permute(even, outward, even_pair), permute(odd, outward, odd_pair)
     traces, even, odd = call(
-        even_kernel, (mask, matrix, own, second, whole, *from_odd), (trace, part, part), 2000000000, moved=0
-    )
-    late_mixed = permute(even, mixed, (even_pair, odd_pair))
+        even_kernel, (mask, matrix, own, second, whole, *from_odd), (trace, part, part), flops)
+    late_even = permute(even, inward, even_pair)
     late_odd = permute(odd, inward, odd_pair)
-    late = permute(traces, inward, same)
+    pair = with_mate(traces)
     (own,) = call(own_kernel, (matrix, source, traces), (trace,), flops)
-    (own,) = call(even_last_kernel, (matrix, own, early, early_even), (trace,), 10**11, moved=10**9)
-    (own,) = call(odd_whole_kernel, (matrix, own, late), (trace,), flops)
-    (out,) = call(last_kernel, (matrix, own, late_mixed, late_odd), (trace,), flops)
+    (own,) = call(mate_kernel, (matrix, own, pair), (trace,), flops)
+    (own,) = call(even_part_kernel, (matrix, own, *early[:2]), (trace,), 10**11, moved=10**9)
+    (out,) = call(last_kernel, (matrix, own, early[2], late_even, late_odd), (trace,), flops)
     return out[None]
 
 

time: 20.5 us -> 20.2 us (0.985)
  the two profiles are of different devices: /device:TPU:11 before, /device:TPU:0 now
where the time goes in v5:
time: 20.2 us; the launch traced here: 20 us
  starting transfers between devices  12.1 us (60%)
  Pallas kernels  3.93 us (19%)
  blocking collectives  2.32 us (11%)
  waiting for transfers between devices  1.62 us (8%)
    ppermute x10, starting transfers between devices, permute(): return lax.ppermute(block, ('layer', 'plane'), route)  12.1 us
    pallas_call x8, Pallas kernels, call(): pl.pallas_call(kernel, out_shape=outs, in_specs=[hbm if in_hbm and x.size...  3.93 us
    all_gather x1, blocking collectives, with_mate(): return lax.all_gather(block, 'layer', axis_index_groups=groups)  2.32 us
    ppermute x10, waiting for transfers between devices, permute(): return lax.ppermute(block, ('layer', 'plane'), route)  1.62 us
  transfers between devices with their start and end apart: 10, of which 2 were waited for; matrix products, arithmetic and copies ran while one was open for 0% of the time, Pallas kernels for 10%

profile of v5, /device:TPU:0, one launch (start us, length us, event | category | flops | bytes accessed | tf_op | source)
XLA Modules:
  0.0 20.0 jit_solution(15677498100369213572)
XLA Ops:
  0.0 0.0 copy-start
  0.0 1.1 %shard_map.56 = (f32[2,2,128,128]{3,2,1,0:T(8,128)S(1)}, f32[1,2,128,128]{3,2,1,0:T(8,128)S(1)}, f32[1,2,128,128]{3,2,1,0:T(8,128)S(1)}) custom-call(s32[2]{0:T(128)} %bitcast.14, bf16[2,2,128,128]{3,2,1,0:T(8,128)(2,1)} %bitcast.9), custom_call_target="tpu_custom_call" | custom-call | flops 99999997952 | bytes 100000000 | tf_op jit(solution)/shard_map/pallas_call | solution.py:296
  1.1 0.5 %collective-permute-start = (f32[2,2,128,128]{3,2,1,0:T(8,128)S(1)}, f32[2,2,128,128]{3,2,1,0:T(8,128)S(1)}, u32[]{:S(2)}, u32[]{:S(2)}) collective-permute-start(f32[2,2,128,128]{3,2,1,0:T(8,128)S(1)} %get-tuple-element.20), channel_id=1, source_target_pairs={{0,4},{1,5},{2,6},{3,7},{4,8},{5,9},{6,10},{7,11},{8,12},{9,13},{1... | collective-permute-start | bytes 786440 | tf_op jit(solution)/shard_map/ppermute | solution.py:45
  1.6 3.8 %collective-permute-start.1 = (f32[1,2,128,128]{3,2,1,0:T(8,128)S(1)}, f32[1,2,128,128]{3,2,1,0:T(8,128)S(1)}, u32[]{:S(2)}, u32[]{:S(2)}) collective-permute-start(f32[1,2,128,128]{3,2,1,0:T(8,128)S(1)} %get-tuple-element.21), channel_id=1, source_target_pairs={{0,5},{1,4},{2,7},{3,6},{4,0},{5,1},{6,2},{7,3},{8,13},{9,12},{10,... | collective-permute-start | bytes 393224 | tf_op jit(solution)/shard_map/ppermute | solution.py:45
  5.4 0.0 collective-permute-start.2
  5.4 0.5 %collective-permute-start.3 = (f32[1,2,128,128]{3,2,1,0:T(8,128)S(1)}, f32[1,2,128,128]{3,2,1,0:T(8,128)S(1)}, u32[]{:S(2)}, u32[]{:S(2)}) collective-permute-start(f32[1,2,128,128]{3,2,1,0:T(8,128)S(1)} %get-tuple-element.21), channel_id=1, source_target_pairs={{0,4},{1,5},{2,6},{3,7},{4,9},{5,8},{6,11},{7,10},{8,12},{9,13},{1... | collective-permute-start | bytes 393224 | tf_op jit(solution)/shard_map/ppermute | solution.py:45
  5.9 2.1 %collective-permute-start.4 = (f32[1,2,128,128]{3,2,1,0:T(8,128)S(1)}, f32[1,2,128,128]{3,2,1,0:T(8,128)S(1)}, u32[]{:S(2)}, u32[]{:S(2)}) collective-permute-start(f32[1,2,128,128]{3,2,1,0:T(8,128)S(1)} %get-tuple-element.22), channel_id=1, source_target_pairs={{0,4},{1,5},{2,6},{3,7},{4,8},{5,10},{6,9},{7,11},{8,12},{9,13},{1... | collective-permute-start | bytes 393224 | tf_op jit(solution)/shard_map/ppermute | solution.py:45
  8.0 0.0 copy-done
  8.0 1.6 %shard_map.55 = (bf16[512,1536]{1,0:T(8,128)(2,1)S(1)}, f32[2,2,128,128]{3,2,1,0:T(8,128)S(1)}, f32[2,1,2,8,128]{4,3,2,1,0:T(8,128)S(1)}) custom-call(s32[24]{0:T(128)} %bitcast.12, s32[24]{0:T(128)} %bitcast.13, s32[2]{0:T(128)} %bitcast.15, bf16[2,2,128,128]{3,2,1,0:T(8,128)(2,1)} %bitcast.10, f32[24,2,128,128]{3,2,1,0:T(8,128)S(1)} %bitcast.7), custom_call_target="tpu_custom_call" | custom-call | flops 201326592 | bytes 5128392 | tf_op jit(solution)/shard_map/pallas_call | solution.py:296
  9.6 0.0 copy-start.1
  9.6 0.0 collective-permute-done.1.even_ref
  9.6 0.0 collective-permute-done.2.odd_ref
  9.7 0.0 collective-permute-done.all_ref
  9.7 0.1 shard_map.57
  9.7 0.5 %collective-permute-start.5 = (f32[2,2,128,128]{3,2,1,0:T(8,128)S(1)}, f32[2,2,128,128]{3,2,1,0:T(8,128)S(1)}, u32[]{:S(2)}, u32[]{:S(2)}) collective-permute-start(f32[2,2,128,128]{3,2,1,0:T(8,128)S(1)} %get-tuple-element.23.known_ref), channel_id=1, source_target_pairs={{0,4},{1,5},{2,6},{3,7},{4,8},{5,9},{6,10},{7,11},{8,12},{9,13},{1... | collective-permute-start | bytes 786440 | tf_op jit(solution)/shard_map/ppermute | solution.py:45
  10.2 1.2 %collective-permute-start.6 = (f32[1,2,128,128]{3,2,1,0:T(8,128)S(1)}, f32[1,2,128,128]{3,2,1,0:T(8,128)S(1)}, u32[]{:S(2)}, u32[]{:S(2)}) collective-permute-start(f32[1,2,128,128]{3,2,1,0:T(8,128)S(1)} %get-tuple-element.25), channel_id=1, source_target_pairs={{0,4},{1,5},{2,6},{3,7},{4,9},{5,8},{6,11},{7,10},{8,12},{9,13},{1... | collective-permute-start | bytes 393224 | tf_op jit(solution)/shard_map/ppermute | solution.py:45
  11.4 2.4 %collective-permute-start.7 = (f32[1,2,128,128]{3,2,1,0:T(8,128)S(1)}, f32[1,2,128,128]{3,2,1,0:T(8,128)S(1)}, u32[]{:S(2)}, u32[]{:S(2)}) collective-permute-start(f32[1,2,128,128]{3,2,1,0:T(8,128)S(1)} %get-tuple-element.26), channel_id=1, source_target_pairs={{0,4},{1,5},{2,6},{3,7},{4,8},{5,10},{6,9},{7,11},{8,12},{9,13},{1... | collective-permute-start | bytes 393224 | tf_op jit(solution)/shard_map/ppermute | solution.py:45
  13.8 0.0 collective-permute-done.3.even_ref
  13.8 0.0 collective-permute-done.4.odd_ref
  13.9 1.1 %collective-permute-start.8 = (f32[1,2,128,128]{3,2,1,0:T(8,128)S(1)}, f32[1,2,128,128]{3,2,1,0:T(8,128)S(1)}, u32[]{:S(2)}, u32[]{:S(2)}) collective-permute-start(f32[1,2,128,128]{3,2,1,0:T(8,128)S(1)} %get-tuple-element.27), channel_id=1, source_target_pairs={{0,5},{1,4},{2,7},{3,6},{4,0},{5,1},{6,2},{7,3},{8,13},{9,12},{10,... | collective-permute-start | bytes 393224 | tf_op jit(solution)/shard_map/ppermute | solution.py:45
  14.9 0.0 collective-permute-start.9
  14.9 0.0 copy-done.1
  14.9 0.4 %shard_map.59.base_ref = f32[2,2,128,128]{3,2,1,0:T(8,128)S(1)} custom-call(bf16[512,1536]{1,0:T(8,128)(2,1)S(1)} %get-tuple-element.17.matrix_ref, bf16[2,2,128,128]{3,2,1,0:T(8,128)(2,1)S(1)} %bitcast.11, f32[2,2,128,128]{3,2,1,0:T(8,128)S(1)} %get-tuple-element.24.trace_ref), custom_call_target="tpu_custom_call" | custom-call | flops 201326592 | bytes 2228224 | tf_op jit(solution)/shard_map/pallas_call | solution.py:296
  15.3 2.3 %all-gather = f32[4,2,128,128]{3,2,1,0:T(8,128)S(1)} all-gather(f32[2,2,128,128]{3,2,1,0:T(8,128)S(1)} %get-tuple-element.24.trace_ref), channel_id=2, replica_groups={{0,4},{8,12},{16,20},{24,28},{1,5},{9,13},{17,21},{25,29},{2,6},{10,14}..., dimensions={0}, use_global_device_ids=true | all-gather | bytes 786432 | tf_op jit(solution)/shard_map/all_gather | solution.py:57
  17.7 0.2 %collective-permute-done.6.even_ref = f32[1,2,128,128]{3,2,1,0:T(8,128)S(1)} collective-permute-done((f32[1,2,128,128]{3,2,1,0:T(8,128)S(1)}, f32[1,2,128,128]{3,2,1,0:T(8,128)S(1)}, u32[]{:S(2)}, u32[]{:S(2)}) %collective-permute-start.6) | collective-permute-done | bytes 131104 | tf_op jit(solution)/shard_map/ppermute | solution.py:45
  17.9 0.0 collective-permute-done.5.all_ref
  17.9 1.4 %collective-permute-done.7.outer_odd_ref = f32[1,2,128,128]{3,2,1,0:T(8,128)S(1)} collective-permute-done((f32[1,2,128,128]{3,2,1,0:T(8,128)S(1)}, f32[1,2,128,128]{3,2,1,0:T(8,128)S(1)}, u32[]{:S(2)}, u32[]{:S(2)}) %collective-permute-start.7) | collective-permute-done | bytes 131104 | tf_op jit(solution)/shard_map/ppermute | solution.py:45
  19.3 0.0 collective-permute-done.8.inner_even_ref
  19.3 0.0 collective-permute-done.9.inner_odd_ref
  19.3 0.7 %shard_map.62 = f32[2,2,128,128]{3,2,1,0:T(8,128)} custom-call(bf16[512,1536]{1,0:T(8,128)(2,1)S(1)} %get-tuple-element.17.matrix_ref, f32[2,2,128,128]{3,2,1,0:T(8,128)S(1)} %shard_map.61.base_ref, f32[1,2,128,128]{3,2,1,0:T(8,128)S(1)} %collective-permute-done.7.outer_odd_ref, f32[1,2,128,128]{3,2,1,0:T(8,128)S(1)} %collective-permute-done.8.inner_even_ref, ...), custom_call_target="tpu_custom_call" | custom-call | flops 201326592 | bytes 2490368 | tf_op jit(solution)/shard_map/pallas_call | solution.py:296
  (3 shorter events, 0.1 us)
Async XLA Ops:
  0.0 8.0 %copy-start = (f32[1,24,2,128,128]{4,3,2,1,0:T(8,128)S(1)}, f32[1,24,2,128,128]{4,3,2,1,0:T(8,128)}, u32[]{:S(2)}) copy-start(f32[1,24,2,128,128]{4,3,2,1,0:T(8,128)} %param.6) | copy-start | bytes 9437188
  1.1 8.5 %collective-permute-start = (f32[2,2,128,128]{3,2,1,0:T(8,128)S(1)}, f32[2,2,128,128]{3,2,1,0:T(8,128)S(1)}, u32[]{:S(2)}, u32[]{:S(2)}) collective-permute-start(f32[2,2,128,128]{3,2,1,0:T(8,128)S(1)} %get-tuple-element.20), channel_id=1, source_target_pairs={{0,4},{1,5},{2,6},{3,7},{4,8},{5,9},{6,10},{7,11},{8,12},{9,13},{1... | collective-permute-start | bytes 786440 | tf_op jit(solution)/shard_map/ppermute | solution.py:45
  1.6 8.0 %collective-permute-start.1 = (f32[1,2,128,128]{3,2,1,0:T(8,128)S(1)}, f32[1,2,128,128]{3,2,1,0:T(8,128)S(1)}, u32[]{:S(2)}, u32[]{:S(2)}) collective-permute-start(f32[1,2,128,128]{3,2,1,0:T(8,128)S(1)} %get-tuple-element.21), channel_id=1, source_target_pairs={{0,5},{1,4},{2,7},{3,6},{4,0},{5,1},{6,2},{7,3},{8,13},{9,12},{10,... | collective-permute-start | bytes 393224 | tf_op jit(solution)/shard_map/ppermute | solution.py:45
  5.4 4.2 %collective-permute-start.2 = (f32[1,2,128,128]{3,2,1,0:T(8,128)S(1)}, f32[1,2,128,128]{3,2,1,0:T(8,128)S(1)}, u32[]{:S(2)}, u32[]{:S(2)}) collective-permute-start(f32[1,2,128,128]{3,2,1,0:T(8,128)S(1)} %get-tuple-element.22), channel_id=1, source_target_pairs={{0,4},{1,6},{2,5},{3,7},{4,0},{5,1},{6,2},{7,3},{8,12},{9,14},{10,... | collective-permute-start | bytes 393224 | tf_op jit(solution)/shard_map/ppermute | solution.py:45
  5.4 8.4 %collective-permute-start.3 = (f32[1,2,128,128]{3,2,1,0:T(8,128)S(1)}, f32[1,2,128,128]{3,2,1,0:T(8,128)S(1)}, u32[]{:S(2)}, u32[]{:S(2)}) collective-permute-start(f32[1,2,128,128]{3,2,1,0:T(8,128)S(1)} %get-tuple-element.21), channel_id=1, source_target_pairs={{0,4},{1,5},{2,6},{3,7},{4,9},{5,8},{6,11},{7,10},{8,12},{9,13},{1... | collective-permute-start | bytes 393224 | tf_op jit(solution)/shard_map/ppermute | solution.py:45
  5.9 7.9 %collective-permute-start.4 = (f32[1,2,128,128]{3,2,1,0:T(8,128)S(1)}, f32[1,2,128,128]{3,2,1,0:T(8,128)S(1)}, u32[]{:S(2)}, u32[]{:S(2)}) collective-permute-start(f32[1,2,128,128]{3,2,1,0:T(8,128)S(1)} %get-tuple-element.22), channel_id=1, source_target_pairs={{0,4},{1,5},{2,6},{3,7},{4,8},{5,10},{6,9},{7,11},{8,12},{9,13},{1... | collective-permute-start | bytes 393224 | tf_op jit(solution)/shard_map/ppermute | solution.py:45
  9.6 5.3 %copy-start.1 = (bf16[1,2,2,128,128]{4,3,2,1,0:T(8,128)(2,1)S(1)}, bf16[1,2,2,128,128]{4,3,2,1,0:T(8,128)(2,1)}, u32[]{:S(2)}) copy-start(bf16[1,2,2,128,128]{4,3,2,1,0:T(8,128)(2,1)} %param.5) | copy-start | bytes 393220
  9.7 8.2 %collective-permute-start.5 = (f32[2,2,128,128]{3,2,1,0:T(8,128)S(1)}, f32[2,2,128,128]{3,2,1,0:T(8,128)S(1)}, u32[]{:S(2)}, u32[]{:S(2)}) collective-permute-start(f32[2,2,128,128]{3,2,1,0:T(8,128)S(1)} %get-tuple-element.23.known_ref), channel_id=1, source_target_pairs={{0,4},{1,5},{2,6},{3,7},{4,8},{5,9},{6,10},{7,11},{8,12},{9,13},{1... | collective-permute-start | bytes 786440 | tf_op jit(solution)/shard_map/ppermute | solution.py:45
  10.2 7.7 %collective-permute-start.6 = (f32[1,2,128,128]{3,2,1,0:T(8,128)S(1)}, f32[1,2,128,128]{3,2,1,0:T(8,128)S(1)}, u32[]{:S(2)}, u32[]{:S(2)}) collective-permute-start(f32[1,2,128,128]{3,2,1,0:T(8,128)S(1)} %get-tuple-element.25), channel_id=1, source_target_pairs={{0,4},{1,5},{2,6},{3,7},{4,9},{5,8},{6,11},{7,10},{8,12},{9,13},{1... | collective-permute-start | bytes 393224 | tf_op jit(solution)/shard_map/ppermute | solution.py:45
  11.4 7.9 %collective-permute-start.7 = (f32[1,2,128,128]{3,2,1,0:T(8,128)S(1)}, f32[1,2,128,128]{3,2,1,0:T(8,128)S(1)}, u32[]{:S(2)}, u32[]{:S(2)}) collective-permute-start(f32[1,2,128,128]{3,2,1,0:T(8,128)S(1)} %get-tuple-element.26), channel_id=1, source_target_pairs={{0,4},{1,5},{2,6},{3,7},{4,8},{5,10},{6,9},{7,11},{8,12},{9,13},{1... | collective-permute-start | bytes 393224 | tf_op jit(solution)/shard_map/ppermute | solution.py:45
  13.9 5.4 %collective-permute-start.8 = (f32[1,2,128,128]{3,2,1,0:T(8,128)S(1)}, f32[1,2,128,128]{3,2,1,0:T(8,128)S(1)}, u32[]{:S(2)}, u32[]{:S(2)}) collective-permute-start(f32[1,2,128,128]{3,2,1,0:T(8,128)S(1)} %get-tuple-element.27), channel_id=1, source_target_pairs={{0,5},{1,4},{2,7},{3,6},{4,0},{5,1},{6,2},{7,3},{8,13},{9,12},{10,... | collective-permute-start | bytes 393224 | tf_op jit(solution)/shard_map/ppermute | solution.py:45
  14.9 4.4 %collective-permute-start.9 = (f32[1,2,128,128]{3,2,1,0:T(8,128)S(1)}, f32[1,2,128,128]{3,2,1,0:T(8,128)S(1)}, u32[]{:S(2)}, u32[]{:S(2)}) collective-permute-start(f32[1,2,128,128]{3,2,1,0:T(8,128)S(1)} %get-tuple-element.28), channel_id=1, source_target_pairs={{0,4},{1,6},{2,5},{3,7},{4,0},{5,1},{6,2},{7,3},{8,12},{9,14},{10,... | collective-permute-start | bytes 393224 | tf_op jit(solution)/shard_map/ppermute | solution.py:45

commit v6 on v5

--- a/solution.py
+++ b/solution.py
@@ -115,6 +115,10 @@
     for k in range(listed):
         even_ref[k] = source_ref[send_ref[(1 - is_odd) * listed + k]].astype(F32)
         odd_ref[k] = source_ref[send_ref[is_odd * listed + k]].astype(F32)
+
+
+def after_kernel(first_ref, payload_ref, passed_ref):
+    passed_ref[...] = payload_ref[...]
 
 
 def prepare_kernel(
@@ -260,8 +264,14 @@
         third_tick(matrix_ref, 0, base_ref, (pair_ref.at[0],), out_ref)
 
 
-def even_part_kernel(matrix_ref, base_ref, all_ref, even_ref, out_ref):
-    @pl.when(jnp.logical_not(on_even_layer()))
+def even_part_kernel(matrix_ref, base_ref, all_ref, even_ref, out_ref, final_hbm, sem):
+    @pl.when(lax.axis_index("layer") == 0)
+    def _():
+        copy = pltpu.make_async_copy(base_ref, final_hbm, sem)
+        copy.start()
+        copy.wait()
+
+    @pl.when(on_odd_layer())
     def _():
         out_ref[...] = base_ref[...]
 
@@ -270,7 +280,9 @@
         third_tick(matrix_ref, 0, base_ref, (all_ref, even_ref), out_ref)
 
 
-def last_kernel(matrix_ref, base_ref, outer_odd_ref, inner_even_ref, inner_odd_ref, out_ref):
+def last_kernel(
+    matrix_ref, base_ref, outer_odd_ref, inner_even_ref, inner_odd_ref, begun_hbm, final_hbm, out_ref, sem
+):
     blocks = base_ref.shape[0]
 
     @pl.when(on_odd_layer())
@@ -281,24 +293,33 @@
     def _():
         third_tick(matrix_ref, blocks + inner_even_ref.shape[0], base_ref, (outer_odd_ref,), out_ref)
 
-    @pl.when(lax.axis_index("layer") == 0)
-    def _():
-        out_ref[...] = base_ref[...]
-
-
-def call(kernel, ins, outs, flops, scratch=(), in_hbm=False, moved=None):
+    @pl.when(lax.axis_index("layer") > 0)
+    def _():
+        copy = pltpu.make_async_copy(out_ref, final_hbm, sem)
+        copy.start()
+        copy.wait()
+
+
+def call(kernel, ins, outs, flops, scratch=(), in_hbm=False, moved=None, last_in_hbm=False, last_out_hbm=False):
     if moved is None:
         moved = sum(x.size * x.dtype.itemsize for x in (*ins, *outs))
-    if in_hbm:
-        ins = [x if x.size > 10**6 // 2 else pltpu.with_memory_space_constraint(x, pltpu.HBM) for x in ins]
     vmem = pl.BlockSpec(memory_space=pltpu.VMEM)
     hbm = pl.BlockSpec(memory_space=pltpu.HBM)
+    held = [in_hbm and not (x.ndim == 4 and x.dtype == F32) for x in ins]
+    if last_in_hbm:
+        held[-1] = True
+    ins = [pltpu.with_memory_space_constraint(x, pltpu.HBM) if h else x for x, h in zip(ins, held)]
+    out_specs = [vmem] * len(outs)
+    if last_out_hbm:
+        out_specs[-1] = hbm
+        outs = (*outs[:-1], pltpu.HBM(outs[-1].shape, outs[-1].dtype))
     return pl.pallas_call(
         kernel,
         out_shape=outs,
-        in_specs=[hbm if in_hbm and x.size <= 10**6 // 2 else vmem for x in ins],
-        out_specs=[vmem] * len(outs),
+        in_specs=[hbm if h else vmem for h in held],
+        out_specs=out_specs,
         scratch_shapes=scratch,
+        input_output_aliases={len(ins) - 1: len(outs) - 1} if last_in_hbm else {},
         compiler_params=pltpu.CompilerParams(vmem_limit_bytes=LIMIT),
         cost_estimate=pl.CostEstimate(flops=flops, bytes_accessed=moved, transcendentals=0),
     )(*ins)
@@ -331,8 +352,10 @@
         in_hbm=True,
         moved=10**8,
     )
-    whole = permute(whole, onward, same)
-    from_odd = permute(even, outward, even_pair), permute(odd, outward, odd_pair)
+    mate = permute(whole, inward, same)
+    (later,) = call(after_kernel, (mate, odd), (part,), 0)
+    whole = permute(whole, outward, same)
+    from_odd = permute(even, outward, even_pair), permute(later, outward, odd_pair)
     from_even = permute(even, inward, even_pair), permute(odd, inward, odd_pair)
     matrix, own, mask = call(
         prepare_kernel,
@@ -349,7 +372,7 @@
         ],
         in_hbm=True,
     )
-    second, even, odd = call(odd_kernel, (mask, matrix, own, whole, *from_even), (trace, part, part), flops)
+    second, even, odd = call(odd_kernel, (mask, matrix, own, mate, *from_even), (trace, part, part), flops)
     early = permute(second, outward, same), permute(even, outward, even_pair), permute(odd, outward, odd_pair)
     traces, even, odd = call(
         even_kernel, (mask, matrix, own, second, whole, *from_odd), (trace, part, part), flops)
@@ -358,8 +381,24 @@
     pair = with_mate(traces)
     (own,) = call(own_kernel, (matrix, source, traces), (trace,), flops)
     (own,) = call(mate_kernel, (matrix, own, pair), (trace,), flops)
-    (own,) = call(even_part_kernel, (matrix, own, *early[:2]), (trace,), 10**11, moved=10**9)
-    (out,) = call(last_kernel, (matrix, own, early[2], late_even, late_odd), (trace,), flops)
+    own, begun = call(
+        even_part_kernel,
+        (matrix, own, *early[:2]),
+        (trace, trace),
+        10**11,
+        [pltpu.SemaphoreType.DMA],
+        moved=10**9,
+        last_out_hbm=True,
+    )
+    (out,) = call(
+        last_kernel,
+        (matrix, own, early[2], late_even, late_odd, begun),
+        (trace,),
+        flops,
+        [pltpu.VMEM(trace.shape, F32), pltpu.SemaphoreType.DMA],
+        last_in_hbm=True,
+        last_out_hbm=True,
+    )
     return out[None]
 
 

time: 20.2 us -> 20 us (0.990)
  the two profiles are of different devices: /device:TPU:0 before, /device:TPU:3 now
where the time goes in v6:
time: 20 us; the launch traced here: 19.8 us
  starting transfers between devices  12.3 us (62%)
  Pallas kernels  5.16 us (26%)
  blocking collectives  2.18 us (11%)
    ppermute x11, starting transfers between devices, permute(): return lax.ppermute(block, ('layer', 'plane'), route)  12.3 us
    pallas_call x9, Pallas kernels, call(): pl.pallas_call(kernel, out_shape=outs, in_specs=[hbm if h else vmem for h...  5.16 us
    all_gather x1, blocking collectives, with_mate(): return lax.all_gather(block, 'layer', axis_index_groups=groups)  2.18 us
  transfers between devices with their start and end apart: 11, of which 0 were waited for; matrix products, arithmetic and copies ran while one was open for 0% of the time, Pallas kernels for 15%

profile of v6, /device:TPU:3, one launch (start us, length us, event | category | flops | bytes accessed | tf_op | source)
XLA Modules:
  0.0 19.8 jit_solution(18264820566326343729)
XLA Ops:
  0.0 1.1 %shard_map.56 = (f32[2,2,128,128]{3,2,1,0:T(8,128)S(1)}, f32[1,2,128,128]{3,2,1,0:T(8,128)S(1)}, f32[1,2,128,128]{3,2,1,0:T(8,128)S(1)}) custom-call(s32[2]{0:T(128)} %bitcast.14, bf16[2,2,128,128]{3,2,1,0:T(8,128)(2,1)} %bitcast.9), custom_call_target="tpu_custom_call" | custom-call | flops 99999997952 | bytes 100000000 | tf_op jit(solution)/shard_map/pallas_call | solution.py:316
  1.1 0.7 %collective-permute-start = (f32[2,2,128,128]{3,2,1,0:T(8,128)S(1)}, f32[2,2,128,128]{3,2,1,0:T(8,128)S(1)}, u32[]{:S(2)}, u32[]{:S(2)}) collective-permute-start(f32[2,2,128,128]{3,2,1,0:T(8,128)S(1)} %get-tuple-element.22), channel_id=1, source_target_pairs={{0,4},{1,5},{2,6},{3,7},{4,0},{5,1},{6,2},{7,3},{8,12},{9,13},{10,... | collective-permute-start | bytes 786440 | tf_op jit(solution)/shard_map/ppermute | solution.py:45
  1.9 1.2 %collective-permute-start.3 = (f32[2,2,128,128]{3,2,1,0:T(8,128)S(1)}, f32[2,2,128,128]{3,2,1,0:T(8,128)S(1)}, u32[]{:S(2)}, u32[]{:S(2)}) collective-permute-start(f32[2,2,128,128]{3,2,1,0:T(8,128)S(1)} %get-tuple-element.22), channel_id=1, source_target_pairs={{0,4},{1,5},{2,6},{3,7},{4,8},{5,9},{6,10},{7,11},{8,12},{9,13},{1... | collective-permute-start | bytes 786440 | tf_op jit(solution)/shard_map/ppermute | solution.py:45
  3.0 0.0 collective-permute-start.1
  3.0 1.7 %collective-permute-start.2 = (f32[1,2,128,128]{3,2,1,0:T(8,128)S(1)}, f32[1,2,128,128]{3,2,1,0:T(8,128)S(1)}, u32[]{:S(2)}, u32[]{:S(2)}) collective-permute-start(f32[1,2,128,128]{3,2,1,0:T(8,128)S(1)} %get-tuple-element.24.payload_ref), channel_id=1, source_target_pairs={{0,4},{1,6},{2,5},{3,7},{4,0},{5,1},{6,2},{7,3},{8,12},{9,14},{10,... | collective-permute-start | bytes 393224 | tf_op jit(solution)/shard_map/ppermute | solution.py:45
  4.7 2.1 %collective-permute-start.4 = (f32[1,2,128,128]{3,2,1,0:T(8,128)S(1)}, f32[1,2,128,128]{3,2,1,0:T(8,128)S(1)}, u32[]{:S(2)}, u32[]{:S(2)}) collective-permute-start(f32[1,2,128,128]{3,2,1,0:T(8,128)S(1)} %get-tuple-element.23), channel_id=1, source_target_pairs={{0,4},{1,5},{2,6},{3,7},{4,9},{5,8},{6,11},{7,10},{8,12},{9,13},{1... | collective-permute-start | bytes 393224 | tf_op jit(solution)/shard_map/ppermute | solution.py:45
  6.8 0.0 collective-permute-done.all_ref.first_ref
  6.9 0.1 collective-permute-start.5
  6.9 1.6 %shard_map.55 = (bf16[512,1536]{1,0:T(8,128)(2,1)S(1)}, f32[2,2,128,128]{3,2,1,0:T(8,128)S(1)}, f32[2,1,2,8,128]{4,3,2,1,0:T(8,128)S(1)}) custom-call(s32[24]{0:T(128)} %bitcast.12, s32[24]{0:T(128)} %bitcast.13, s32[2]{0:T(128)} %bitcast.15, bf16[2,2,128,128]{3,2,1,0:T(8,128)(2,1)} %bitcast.10, f32[24,2,128,128]{3,2,1,0:T(8,128)S(1)} %bitcast.7), custom_call_target="tpu_custom_call" | custom-call | flops 201326592 | bytes 5128392 | tf_op jit(solution)/shard_map/pallas_call | solution.py:316
  8.5 0.0 copy-start.1
  8.5 0.0 collective-permute-done.1.even_ref
  8.5 0.0 collective-permute-done.2.odd_ref
  8.5 0.5 %shard_map.57 = (f32[2,2,128,128]{3,2,1,0:T(8,128)S(1)}, f32[1,2,128,128]{3,2,1,0:T(8,128)S(1)}, f32[1,2,128,128]{3,2,1,0:T(8,128)S(1)}) custom-call(f32[2,1,2,8,128]{4,3,2,1,0:T(8,128)S(1)} %get-tuple-element.20.mask_ref, bf16[512,1536]{1,0:T(8,128)(2,1)S(1)} %get-tuple-element.19.matrix_ref, f32[2,2,128,128]{3,2,1,0:T(8,128)S(1)} %get-tuple-element.21.own_ref, ...), custom_call_target="tpu_custom_call" | custom-call | flops 201326592 | bytes 2899968 | tf_op jit(solution)/shard_map/pallas_call | solution.py:316
  9.0 0.6 %collective-permute-start.6 = (f32[2,2,128,128]{3,2,1,0:T(8,128)S(1)}, f32[2,2,128,128]{3,2,1,0:T(8,128)S(1)}, u32[]{:S(2)}, u32[]{:S(2)}) collective-permute-start(f32[2,2,128,128]{3,2,1,0:T(8,128)S(1)} %get-tuple-element.25.known_ref), channel_id=1, source_target_pairs={{0,4},{1,5},{2,6},{3,7},{4,8},{5,9},{6,10},{7,11},{8,12},{9,13},{1... | collective-permute-start | bytes 786440 | tf_op jit(solution)/shard_map/ppermute | solution.py:45
  9.6 3.6 %collective-permute-start.7 = (f32[1,2,128,128]{3,2,1,0:T(8,128)S(1)}, f32[1,2,128,128]{3,2,1,0:T(8,128)S(1)}, u32[]{:S(2)}, u32[]{:S(2)}) collective-permute-start(f32[1,2,128,128]{3,2,1,0:T(8,128)S(1)} %get-tuple-element.27), channel_id=1, source_target_pairs={{0,4},{1,5},{2,6},{3,7},{4,9},{5,8},{6,11},{7,10},{8,12},{9,13},{1... | collective-permute-start | bytes 393224 | tf_op jit(solution)/shard_map/ppermute | solution.py:45
  13.2 0.0 collective-permute-done.4.even_ref
  13.2 0.0 collective-permute-start.8
  13.2 0.0 collective-permute-done.3.all_ref
  13.2 0.0 collective-permute-done.5.odd_ref
  13.2 0.1 shard_map.59
  13.3 1.0 %collective-permute-start.9 = (f32[1,2,128,128]{3,2,1,0:T(8,128)S(1)}, f32[1,2,128,128]{3,2,1,0:T(8,128)S(1)}, u32[]{:S(2)}, u32[]{:S(2)}) collective-permute-start(f32[1,2,128,128]{3,2,1,0:T(8,128)S(1)} %get-tuple-element.30), channel_id=1, source_target_pairs={{0,5},{1,4},{2,7},{3,6},{4,0},{5,1},{6,2},{7,3},{8,13},{9,12},{10,... | collective-permute-start | bytes 393224 | tf_op jit(solution)/shard_map/ppermute | solution.py:45
  14.2 1.4 %collective-permute-start.10 = (f32[1,2,128,128]{3,2,1,0:T(8,128)S(1)}, f32[1,2,128,128]{3,2,1,0:T(8,128)S(1)}, u32[]{:S(2)}, u32[]{:S(2)}) collective-permute-start(f32[1,2,128,128]{3,2,1,0:T(8,128)S(1)} %get-tuple-element.31), channel_id=1, source_target_pairs={{0,4},{1,6},{2,5},{3,7},{4,0},{5,1},{6,2},{7,3},{8,12},{9,14},{10,... | collective-permute-start | bytes 393224 | tf_op jit(solution)/shard_map/ppermute | solution.py:45
  15.7 0.4 %shard_map.60.base_ref = f32[2,2,128,128]{3,2,1,0:T(8,128)S(1)} custom-call(bf16[512,1536]{1,0:T(8,128)(2,1)S(1)} %get-tuple-element.19.matrix_ref, bf16[2,2,128,128]{3,2,1,0:T(8,128)(2,1)S(1)} %bitcast.11, f32[2,2,128,128]{3,2,1,0:T(8,128)S(1)} %get-tuple-element.26.trace_ref), custom_call_target="tpu_custom_call" | custom-call | flops 201326592 | bytes 2228224 | tf_op jit(solution)/shard_map/pallas_call | solution.py:316
  16.0 2.2 %all-gather = f32[4,2,128,128]{3,2,1,0:T(8,128)S(1)} all-gather(f32[2,2,128,128]{3,2,1,0:T(8,128)S(1)} %get-tuple-element.26.trace_ref), channel_id=2, replica_groups={{0,4},{8,12},{16,20},{24,28},{1,5},{9,13},{17,21},{25,29},{2,6},{10,14}..., dimensions={0}, use_global_device_ids=true | all-gather | bytes 786432 | tf_op jit(solution)/shard_map/all_gather | solution.py:57
  18.2 0.4 %shard_map.61.base_ref = f32[2,2,128,128]{3,2,1,0:T(8,128)S(1)} custom-call(bf16[512,1536]{1,0:T(8,128)(2,1)S(1)} %get-tuple-element.19.matrix_ref, f32[2,2,128,128]{3,2,1,0:T(8,128)S(1)} %shard_map.60.base_ref, f32[2,2,2,128,128]{4,3,2,1,0:T(8,128)S(1)} %bitcast.8), custom_call_target="tpu_custom_call" | custom-call | flops 201326592 | bytes 2621440 | tf_op jit(solution)/shard_map/pallas_call | solution.py:316
  18.6 0.0 collective-permute-done.7.even_ref
  18.6 0.0 collective-permute-done.6.all_ref
  18.6 0.1 shard_map.62
  18.7 0.0 collective-permute-done.8.outer_odd_ref
  18.7 0.0 collective-permute-done.9.inner_even_ref
  18.7 0.0 collective-permute-done.10.inner_odd_ref
  18.7 1.1 %shard_map.63 = f32[2,2,128,128]{3,2,1,0:T(8,128)} custom-call(bf16[512,1536]{1,0:T(8,128)(2,1)S(1)} %get-tuple-element.19.matrix_ref, f32[2,2,128,128]{3,2,1,0:T(8,128)S(1)} %get-tuple-element.28.base_ref, f32[1,2,128,128]{3,2,1,0:T(8,128)S(1)} %collective-permute-done.8.outer_odd_ref, ...), custom_call_target="tpu_custom_call", output_to_operand_aliasing={{}: (5, {})} | custom-call | flops 201326592 | bytes 2752512 | tf_op jit(solution)/shard_map/pallas_call | solution.py:316
  (4 shorter events, 0.0 us)
Async XLA Ops:
  0.0 6.9 %copy-start = (f32[1,24,2,128,128]{4,3,2,1,0:T(8,128)S(1)}, f32[1,24,2,128,128]{4,3,2,1,0:T(8,128)}, u32[]{:S(2)}) copy-start(f32[1,24,2,128,128]{4,3,2,1,0:T(8,128)} %param.6) | copy-start | bytes 9437188
  1.1 5.7 %collective-permute-start = (f32[2,2,128,128]{3,2,1,0:T(8,128)S(1)}, f32[2,2,128,128]{3,2,1,0:T(8,128)S(1)}, u32[]{:S(2)}, u32[]{:S(2)}) collective-permute-start(f32[2,2,128,128]{3,2,1,0:T(8,128)S(1)} %get-tuple-element.22), channel_id=1, source_target_pairs={{0,4},{1,5},{2,6},{3,7},{4,0},{5,1},{6,2},{7,3},{8,12},{9,13},{10,... | collective-permute-start | bytes 786440 | tf_op jit(solution)/shard_map/ppermute | solution.py:45
  1.9 11.3 %collective-permute-start.3 = (f32[2,2,128,128]{3,2,1,0:T(8,128)S(1)}, f32[2,2,128,128]{3,2,1,0:T(8,128)S(1)}, u32[]{:S(2)}, u32[]{:S(2)}) collective-permute-start(f32[2,2,128,128]{3,2,1,0:T(8,128)S(1)} %get-tuple-element.22), channel_id=1, source_target_pairs={{0,4},{1,5},{2,6},{3,7},{4,8},{5,9},{6,10},{7,11},{8,12},{9,13},{1... | collective-permute-start | bytes 786440 | tf_op jit(solution)/shard_map/ppermute | solution.py:45
  3.0 5.5 %collective-permute-start.1 = (f32[1,2,128,128]{3,2,1,0:T(8,128)S(1)}, f32[1,2,128,128]{3,2,1,0:T(8,128)S(1)}, u32[]{:S(2)}, u32[]{:S(2)}) collective-permute-start(f32[1,2,128,128]{3,2,1,0:T(8,128)S(1)} %get-tuple-element.23), channel_id=1, source_target_pairs={{0,5},{1,4},{2,7},{3,6},{4,0},{5,1},{6,2},{7,3},{8,13},{9,12},{10,... | collective-permute-start | bytes 393224 | tf_op jit(solution)/shard_map/ppermute | solution.py:45
  3.0 5.5 %collective-permute-start.2 = (f32[1,2,128,128]{3,2,1,0:T(8,128)S(1)}, f32[1,2,128,128]{3,2,1,0:T(8,128)S(1)}, u32[]{:S(2)}, u32[]{:S(2)}) collective-permute-start(f32[1,2,128,128]{3,2,1,0:T(8,128)S(1)} %get-tuple-element.24.payload_ref), channel_id=1, source_target_pairs={{0,4},{1,6},{2,5},{3,7},{4,0},{5,1},{6,2},{7,3},{8,12},{9,14},{10,... | collective-permute-start | bytes 393224 | tf_op jit(solution)/shard_map/ppermute | solution.py:45
  4.7 8.5 %collective-permute-start.4 = (f32[1,2,128,128]{3,2,1,0:T(8,128)S(1)}, f32[1,2,128,128]{3,2,1,0:T(8,128)S(1)}, u32[]{:S(2)}, u32[]{:S(2)}) collective-permute-start(f32[1,2,128,128]{3,2,1,0:T(8,128)S(1)} %get-tuple-element.23), channel_id=1, source_target_pairs={{0,4},{1,5},{2,6},{3,7},{4,9},{5,8},{6,11},{7,10},{8,12},{9,13},{1... | collective-permute-start | bytes 393224 | tf_op jit(solution)/shard_map/ppermute | solution.py:45
  6.9 6.3 %collective-permute-start.5 = (f32[1,2,128,128]{3,2,1,0:T(8,128)S(1)}, f32[1,2,128,128]{3,2,1,0:T(8,128)S(1)}, u32[]{:S(2)}, u32[]{:S(2)}) collective-permute-start(f32[1,2,128,128]{3,2,1,0:T(8,128)S(1)} %shard_map.58), channel_id=1, source_target_pairs={{0,4},{1,5},{2,6},{3,7},{4,8},{5,10},{6,9},{7,11},{8,12},{9,13},{1... | collective-permute-start | bytes 393224 | tf_op jit(solution)/shard_map/ppermute | solution.py:45
  8.5 7.1 %copy-start.1 = (bf16[1,2,2,128,128]{4,3,2,1,0:T(8,128)(2,1)S(1)}, bf16[1,2,2,128,128]{4,3,2,1,0:T(8,128)(2,1)}, u32[]{:S(2)}) copy-start(bf16[1,2,2,128,128]{4,3,2,1,0:T(8,128)(2,1)} %param.5) | copy-start | bytes 393220
  9.0 9.6 %collective-permute-start.6 = (f32[2,2,128,128]{3,2,1,0:T(8,128)S(1)}, f32[2,2,128,128]{3,2,1,0:T(8,128)S(1)}, u32[]{:S(2)}, u32[]{:S(2)}) collective-permute-start(f32[2,2,128,128]{3,2,1,0:T(8,128)S(1)} %get-tuple-element.25.known_ref), channel_id=1, source_target_pairs={{0,4},{1,5},{2,6},{3,7},{4,8},{5,9},{6,10},{7,11},{8,12},{9,13},{1... | collective-permute-start | bytes 786440 | tf_op jit(solution)/shard_map/ppermute | solution.py:45
  9.6 9.0 %collective-permute-start.7 = (f32[1,2,128,128]{3,2,1,0:T(8,128)S(1)}, f32[1,2,128,128]{3,2,1,0:T(8,128)S(1)}, u32[]{:S(2)}, u32[]{:S(2)}) collective-permute-start(f32[1,2,128,128]{3,2,1,0:T(8,128)S(1)} %get-tuple-element.27), channel_id=1, source_target_pairs={{0,4},{1,5},{2,6},{3,7},{4,9},{5,8},{6,11},{7,10},{8,12},{9,13},{1... | collective-permute-start | bytes 393224 | tf_op jit(solution)/shard_map/ppermute | solution.py:45
  13.2 5.5 %collective-permute-start.8 = (f32[1,2,128,128]{3,2,1,0:T(8,128)S(1)}, f32[1,2,128,128]{3,2,1,0:T(8,128)S(1)}, u32[]{:S(2)}, u32[]{:S(2)}) collective-permute-start(f32[1,2,128,128]{3,2,1,0:T(8,128)S(1)} %get-tuple-element.29), channel_id=1, source_target_pairs={{0,4},{1,5},{2,6},{3,7},{4,8},{5,10},{6,9},{7,11},{8,12},{9,13},{1... | collective-permute-start | bytes 393224 | tf_op jit(solution)/shard_map/ppermute | solution.py:45
  13.3 5.4 %collective-permute-start.9 = (f32[1,2,128,128]{3,2,1,0:T(8,128)S(1)}, f32[1,2,128,128]{3,2,1,0:T(8,128)S(1)}, u32[]{:S(2)}, u32[]{:S(2)}) collective-permute-start(f32[1,2,128,128]{3,2,1,0:T(8,128)S(1)} %get-tuple-element.30), channel_id=1, source_target_pairs={{0,5},{1,4},{2,7},{3,6},{4,0},{5,1},{6,2},{7,3},{8,13},{9,12},{10,... | collective-permute-start | bytes 393224 | tf_op jit(solution)/shard_map/ppermute | solution.py:45
  14.2 4.5 %collective-permute-start.10 = (f32[1,2,128,128]{3,2,1,0:T(8,128)S(1)}, f32[1,2,128,128]{3,2,1,0:T(8,128)S(1)}, u32[]{:S(2)}, u32[]{:S(2)}) collective-permute-start(f32[1,2,128,128]{3,2,1,0:T(8,128)S(1)} %get-tuple-element.31), channel_id=1, source_target_pairs={{0,4},{1,6},{2,5},{3,7},{4,0},{5,1},{6,2},{7,3},{8,12},{9,14},{10,... | collective-permute-start | bytes 393224 | tf_op jit(solution)/shard_map/ppermute | solution.py:45

commit v7 on v6

--- a/solution.py
+++ b/solution.py
@@ -8,6 +8,7 @@
 F32 = jnp.float32
 BF16 = jnp.bfloat16
 LIMIT = 40 * 1024 * 1024
+LONG = 10**11
 
 
 def even_pair(p, planes):
@@ -43,10 +44,6 @@
             to_layer, to_plane = way(l, p, layers, planes, partner)
             route.append((l * planes + p, to_layer * planes + to_plane))
     return lax.ppermute(block, ("layer", "plane"), route)
-
-
-def onward(l, p, layers, planes, partner):
-    return (l + 1) % layers, p
 
 
 def with_mate(block):
@@ -241,12 +238,6 @@
     choose(mask_ref, 1, new_ref, new_odd_ref)
 
 
-def own_kernel(matrix_ref, source_ref, trace_ref, own_ref):
-    blocks = gather(trace_ref)
-    depth = 2 * trace_ref.shape[2] * len(blocks)
-    store(three_products(matrix_ref, slice(matrix_ref.shape[1] - depth, None), blocks), source_ref, own_ref)
-
-
 def third_tick(matrix_ref, first, base_ref, refs, out_ref):
     blocks = gather(*refs)
     unit = 2 * base_ref.shape[2]
@@ -254,14 +245,31 @@
     store(three_products(matrix_ref, columns, blocks), base_ref, out_ref)
 
 
-def mate_kernel(matrix_ref, base_ref, pair_ref, out_ref):
+def first_own_column(matrix_ref, trace_ref):
+    blocks, _, width, _ = trace_ref.shape
+    return matrix_ref.shape[1] // (2 * width) - blocks
+
+
+def odd_own_kernel(matrix_ref, source_ref, trace_ref, payload_ref, out_ref, passed_ref):
+    passed_ref[...] = payload_ref[...]
+
+    @pl.when(on_odd_layer())
+    def _():
+        third_tick(matrix_ref, first_own_column(matrix_ref, trace_ref), source_ref, (trace_ref,), out_ref)
+
     @pl.when(jnp.logical_not(on_odd_layer()))
     def _():
-        out_ref[...] = base_ref[...]
-
+        out_ref[...] = source_ref[...].astype(F32)
+
+
+def pair_kernel(matrix_ref, base_ref, trace_ref, pair_ref, out_ref):
     @pl.when(on_odd_layer())
     def _():
         third_tick(matrix_ref, 0, base_ref, (pair_ref.at[0],), out_ref)
+
+    @pl.when(jnp.logical_not(on_odd_layer()))
+    def _():
+        third_tick(matrix_ref, first_own_column(matrix_ref, trace_ref), base_ref, (trace_ref,), out_ref)
 
 
 def even_part_kernel(matrix_ref, base_ref, all_ref, even_ref, out_ref, final_hbm, sem):
@@ -347,7 +355,7 @@
         widen_kernel,
         (send, source),
         (trace, part, part),
-        10**11,
+        LONG,
         [send_copy, source_copy, pltpu.SemaphoreType.DMA((2,))],
         in_hbm=True,
         moved=10**8,
@@ -373,19 +381,20 @@
         in_hbm=True,
     )
     second, even, odd = call(odd_kernel, (mask, matrix, own, mate, *from_even), (trace, part, part), flops)
+    third, odd = call(odd_own_kernel, (matrix, source, second, odd), (trace, part), flops)
     early = permute(second, outward, same), permute(even, outward, even_pair), permute(odd, outward, odd_pair)
     traces, even, odd = call(
-        even_kernel, (mask, matrix, own, second, whole, *from_odd), (trace, part, part), flops)
+        even_kernel, (mask, matrix, own, second, whole, *from_odd), (trace, part, part), flops
+    )
     late_even = permute(even, inward, even_pair)
     late_odd = permute(odd, inward, odd_pair)
     pair = with_mate(traces)
-    (own,) = call(own_kernel, (matrix, source, traces), (trace,), flops)
-    (own,) = call(mate_kernel, (matrix, own, pair), (trace,), flops)
+    (own,) = call(pair_kernel, (matrix, third, traces, pair), (trace,), flops)
     own, begun = call(
         even_part_kernel,
         (matrix, own, *early[:2]),
         (trace, trace),
-        10**11,
+        LONG,
         [pltpu.SemaphoreType.DMA],
         moved=10**9,
         last_out_hbm=True,

time: 20 us -> 19.9 us (level)
  the two profiles are of different devices: /device:TPU:3 before, /device:TPU:1 now
where the time goes in v7:
time: 19.9 us; the launch traced here: 19.8 us
  starting transfers between devices  11.8 us (59%)
  Pallas kernels  5.16 us (26%)
  blocking collectives  2.17 us (11%)
  waiting for transfers between devices  0.48 us (2%)
    ppermute x11, starting transfers between devices, permute(): return lax.ppermute(block, ('layer', 'plane'), route)  11.8 us
    pallas_call x9, Pallas kernels, call(): pl.pallas_call(kernel, out_shape=outs, in_specs=[hbm if h else vmem for h...  5.16 us
    all_gather x1, blocking collectives, with_mate(): return lax.all_gather(block, 'layer', axis_index_groups=groups)  2.17 us
    ppermute x11, waiting for transfers between devices, permute(): return lax.ppermute(block, ('layer', 'plane'), route)  0.48 us
  transfers between devices with their start and end apart: 11, of which 1 were waited for; matrix products, arithmetic and copies ran while one was open for 0% of the time, Pallas kernels for 15%

profile of v7, /device:TPU:1, one launch (start us, length us, event | category | flops | bytes accessed | tf_op | source)
XLA Modules:
  0.0 19.8 jit_solution(13102361250510450474)
XLA Ops:
  0.0 1.1 %shard_map.56 = (f32[2,2,128,128]{3,2,1,0:T(8,128)S(1)}, f32[1,2,128,128]{3,2,1,0:T(8,128)S(1)}, f32[1,2,128,128]{3,2,1,0:T(8,128)S(1)}) custom-call(s32[2]{0:T(128)} %bitcast.14, bf16[2,2,128,128]{3,2,1,0:T(8,128)(2,1)} %bitcast.9), custom_call_target="tpu_custom_call" | custom-call | flops 99999997952 | bytes 100000000 | tf_op jit(solution)/shard_map/pallas_call | solution.py:324
  1.1 0.0 copy-start.1
  1.1 0.1 collective-permute-start
  1.3 2.6 %collective-permute-start.3 = (f32[2,2,128,128]{3,2,1,0:T(8,128)S(1)}, f32[2,2,128,128]{3,2,1,0:T(8,128)S(1)}, u32[]{:S(2)}, u32[]{:S(2)}) collective-permute-start(f32[2,2,128,128]{3,2,1,0:T(8,128)S(1)} %get-tuple-element.24), channel_id=1, source_target_pairs={{0,4},{1,5},{2,6},{3,7},{4,8},{5,9},{6,10},{7,11},{8,12},{9,13},{1... | collective-permute-start | bytes 786440 | tf_op jit(solution)/shard_map/ppermute | solution.py:46
  3.9 0.0 collective-permute-start.1
  3.9 1.7 %collective-permute-start.2 = (f32[1,2,128,128]{3,2,1,0:T(8,128)S(1)}, f32[1,2,128,128]{3,2,1,0:T(8,128)S(1)}, u32[]{:S(2)}, u32[]{:S(2)}) collective-permute-start(f32[1,2,128,128]{3,2,1,0:T(8,128)S(1)} %get-tuple-element.26.payload_ref), channel_id=1, source_target_pairs={{0,4},{1,6},{2,5},{3,7},{4,0},{5,1},{6,2},{7,3},{8,12},{9,14},{10,... | collective-permute-start | bytes 393224 | tf_op jit(solution)/shard_map/ppermute | solution.py:46
  5.6 2.1 %collective-permute-start.4 = (f32[1,2,128,128]{3,2,1,0:T(8,128)S(1)}, f32[1,2,128,128]{3,2,1,0:T(8,128)S(1)}, u32[]{:S(2)}, u32[]{:S(2)}) collective-permute-start(f32[1,2,128,128]{3,2,1,0:T(8,128)S(1)} %get-tuple-element.25), channel_id=1, source_target_pairs={{0,4},{1,5},{2,6},{3,7},{4,9},{5,8},{6,11},{7,10},{8,12},{9,13},{1... | collective-permute-start | bytes 393224 | tf_op jit(solution)/shard_map/ppermute | solution.py:46
  7.7 0.0 collective-permute-done.all_ref.first_ref
  7.7 0.1 collective-permute-start.5
  7.8 1.6 %shard_map.55 = (bf16[512,1536]{1,0:T(8,128)(2,1)S(1)}, f32[2,2,128,128]{3,2,1,0:T(8,128)S(1)}, f32[2,1,2,8,128]{4,3,2,1,0:T(8,128)S(1)}) custom-call(s32[24]{0:T(128)} %bitcast.12, s32[24]{0:T(128)} %bitcast.13, s32[2]{0:T(128)} %bitcast.15, bf16[2,2,128,128]{3,2,1,0:T(8,128)(2,1)} %bitcast.10, f32[24,2,128,128]{3,2,1,0:T(8,128)S(1)} %bitcast.7), custom_call_target="tpu_custom_call" | custom-call | flops 201326592 | bytes 5128392 | tf_op jit(solution)/shard_map/pallas_call | solution.py:324
  9.4 0.0 collective-permute-done.1.even_ref
  9.4 0.0 collective-permute-done.2.odd_ref
  9.4 0.5 %shard_map.57 = (f32[2,2,128,128]{3,2,1,0:T(8,128)S(1)}, f32[1,2,128,128]{3,2,1,0:T(8,128)S(1)}, f32[1,2,128,128]{3,2,1,0:T(8,128)S(1)}) custom-call(f32[2,1,2,8,128]{4,3,2,1,0:T(8,128)S(1)} %get-tuple-element.22.mask_ref, bf16[512,1536]{1,0:T(8,128)(2,1)S(1)} %get-tuple-element.21.matrix_ref, f32[2,2,128,128]{3,2,1,0:T(8,128)S(1)} %get-tuple-element.23.own_ref, ...), custom_call_target="tpu_custom_call" | custom-call | flops 201326592 | bytes 2899968 | tf_op jit(solution)/shard_map/pallas_call | solution.py:324
  9.9 1.2 %collective-permute-start.6 = (f32[2,2,128,128]{3,2,1,0:T(8,128)S(1)}, f32[2,2,128,128]{3,2,1,0:T(8,128)S(1)}, u32[]{:S(2)}, u32[]{:S(2)}) collective-permute-start(f32[2,2,128,128]{3,2,1,0:T(8,128)S(1)} %get-tuple-element.27.trace_ref.known_ref), channel_id=1, source_target_pairs={{0,4},{1,5},{2,6},{3,7},{4,8},{5,9},{6,10},{7,11},{8,12},{9,13},{1... | collective-permute-start | bytes 786440 | tf_op jit(solution)/shard_map/ppermute | solution.py:46
  11.1 2.3 %collective-permute-start.7 = (f32[1,2,128,128]{3,2,1,0:T(8,128)S(1)}, f32[1,2,128,128]{3,2,1,0:T(8,128)S(1)}, u32[]{:S(2)}, u32[]{:S(2)}) collective-permute-start(f32[1,2,128,128]{3,2,1,0:T(8,128)S(1)} %get-tuple-element.31), channel_id=1, source_target_pairs={{0,4},{1,5},{2,6},{3,7},{4,9},{5,8},{6,11},{7,10},{8,12},{9,13},{1... | collective-permute-start | bytes 393224 | tf_op jit(solution)/shard_map/ppermute | solution.py:46
  13.4 0.4 %shard_map.58 = (f32[2,2,128,128]{3,2,1,0:T(8,128)S(1)}, f32[1,2,128,128]{3,2,1,0:T(8,128)S(1)}) custom-call(bf16[512,1536]{1,0:T(8,128)(2,1)S(1)} %get-tuple-element.21.matrix_ref, bf16[2,2,128,128]{3,2,1,0:T(8,128)(2,1)S(1)} %bitcast.11, f32[2,2,128,128]{3,2,1,0:T(8,128)S(1)} %get-tuple-element.27.trace_ref.known_ref, ...), custom_call_target="tpu_custom_call" | custom-call | flops 201326592 | bytes 2490368 | tf_op jit(solution)/shard_map/pallas_call | solution.py:324
  13.8 0.0 collective-permute-done.4.even_ref
  13.8 0.1 collective-permute-start.8
  13.9 0.0 collective-permute-done.3.all_ref
  13.9 0.0 collective-permute-done.5.odd_ref
  13.9 0.1 shard_map.60
  14.0 0.5 %collective-permute-start.9 = (f32[1,2,128,128]{3,2,1,0:T(8,128)S(1)}, f32[1,2,128,128]{3,2,1,0:T(8,128)S(1)}, u32[]{:S(2)}, u32[]{:S(2)}) collective-permute-start(f32[1,2,128,128]{3,2,1,0:T(8,128)S(1)} %get-tuple-element.34), channel_id=1, source_target_pairs={{0,5},{1,4},{2,7},{3,6},{4,0},{5,1},{6,2},{7,3},{8,13},{9,12},{10,... | collective-permute-start | bytes 393224 | tf_op jit(solution)/shard_map/ppermute | solution.py:46
  14.5 1.1 %collective-permute-start.10 = (f32[1,2,128,128]{3,2,1,0:T(8,128)S(1)}, f32[1,2,128,128]{3,2,1,0:T(8,128)S(1)}, u32[]{:S(2)}, u32[]{:S(2)}) collective-permute-start(f32[1,2,128,128]{3,2,1,0:T(8,128)S(1)} %get-tuple-element.35), channel_id=1, source_target_pairs={{0,4},{1,6},{2,5},{3,7},{4,0},{5,1},{6,2},{7,3},{8,12},{9,14},{10,... | collective-permute-start | bytes 393224 | tf_op jit(solution)/shard_map/ppermute | solution.py:46
  15.6 2.2 %all-gather = f32[4,2,128,128]{3,2,1,0:T(8,128)S(1)} all-gather(f32[2,2,128,128]{3,2,1,0:T(8,128)S(1)} %get-tuple-element.30.trace_ref), channel_id=2, replica_groups={{0,4},{8,12},{16,20},{24,28},{1,5},{9,13},{17,21},{25,29},{2,6},{10,14}..., dimensions={0}, use_global_device_ids=true | all-gather | bytes 786432 | tf_op jit(solution)/shard_map/all_gather | solution.py:54
  17.8 0.4 %shard_map.61.base_ref = f32[2,2,128,128]{3,2,1,0:T(8,128)S(1)} custom-call(bf16[512,1536]{1,0:T(8,128)(2,1)S(1)} %get-tuple-element.21.matrix_ref, f32[2,2,128,128]{3,2,1,0:T(8,128)S(1)} %get-tuple-element.29.base_ref, f32[2,2,128,128]{3,2,1,0:T(8,128)S(1)} %get-tuple-element.30.trace_ref, f32[2,2,2,128,128]{4,3,2,1,0:T(8,128)S(1)} %bitcast.8), custom_call_target="tpu_custom_call" | custom-call | flops 201326592 | bytes 2883584 | tf_op jit(solution)/shard_map/pallas_call | solution.py:324
  18.1 0.0 collective-permute-done.7.even_ref
  18.2 0.0 collective-permute-done.6.all_ref
  18.2 0.1 shard_map.62
  18.2 0.0 collective-permute-done.8.outer_odd_ref
  18.2 0.5 %collective-permute-done.9.inner_even_ref = f32[1,2,128,128]{3,2,1,0:T(8,128)S(1)} collective-permute-done((f32[1,2,128,128]{3,2,1,0:T(8,128)S(1)}, f32[1,2,128,128]{3,2,1,0:T(8,128)S(1)}, u32[]{:S(2)}, u32[]{:S(2)}) %collective-permute-start.9) | collective-permute-done | bytes 131104 | tf_op jit(solution)/shard_map/ppermute | solution.py:46
  18.7 0.0 collective-permute-done.10.inner_odd_ref
  18.7 1.1 %shard_map.63 = f32[2,2,128,128]{3,2,1,0:T(8,128)} custom-call(bf16[512,1536]{1,0:T(8,128)(2,1)S(1)} %get-tuple-element.21.matrix_ref, f32[2,2,128,128]{3,2,1,0:T(8,128)S(1)} %get-tuple-element.32.base_ref, f32[1,2,128,128]{3,2,1,0:T(8,128)S(1)} %collective-permute-done.8.outer_odd_ref, ...), custom_call_target="tpu_custom_call", output_to_operand_aliasing={{}: (5, {})} | custom-call | flops 201326592 | bytes 2752512 | tf_op jit(solution)/shard_map/pallas_call | solution.py:324
  (4 shorter events, 0.0 us)
Async XLA Ops:
  0.0 7.8 %copy-start = (f32[1,24,2,128,128]{4,3,2,1,0:T(8,128)S(1)}, f32[1,24,2,128,128]{4,3,2,1,0:T(8,128)}, u32[]{:S(2)}) copy-start(f32[1,24,2,128,128]{4,3,2,1,0:T(8,128)} %param.6) | copy-start | bytes 9437188
  1.1 12.3 %copy-start.1 = (bf16[1,2,2,128,128]{4,3,2,1,0:T(8,128)(2,1)S(1)}, bf16[1,2,2,128,128]{4,3,2,1,0:T(8,128)(2,1)}, u32[]{:S(2)}) copy-start(bf16[1,2,2,128,128]{4,3,2,1,0:T(8,128)(2,1)} %param.5) | copy-start | bytes 393220
  1.1 6.5 %collective-permute-start = (f32[2,2,128,128]{3,2,1,0:T(8,128)S(1)}, f32[2,2,128,128]{3,2,1,0:T(8,128)S(1)}, u32[]{:S(2)}, u32[]{:S(2)}) collective-permute-start(f32[2,2,128,128]{3,2,1,0:T(8,128)S(1)} %get-tuple-element.24), channel_id=1, source_target_pairs={{0,4},{1,5},{2,6},{3,7},{4,0},{5,1},{6,2},{7,3},{8,12},{9,13},{10,... | collective-permute-start | bytes 786440 | tf_op jit(solution)/shard_map/ppermute | solution.py:46
  1.3 12.6 %collective-permute-start.3 = (f32[2,2,128,128]{3,2,1,0:T(8,128)S(1)}, f32[2,2,128,128]{3,2,1,0:T(8,128)S(1)}, u32[]{:S(2)}, u32[]{:S(2)}) collective-permute-start(f32[2,2,128,128]{3,2,1,0:T(8,128)S(1)} %get-tuple-element.24), channel_id=1, source_target_pairs={{0,4},{1,5},{2,6},{3,7},{4,8},{5,9},{6,10},{7,11},{8,12},{9,13},{1... | collective-permute-start | bytes 786440 | tf_op jit(solution)/shard_map/ppermute | solution.py:46
  3.9 5.5 %collective-permute-start.1 = (f32[1,2,128,128]{3,2,1,0:T(8,128)S(1)}, f32[1,2,128,128]{3,2,1,0:T(8,128)S(1)}, u32[]{:S(2)}, u32[]{:S(2)}) collective-permute-start(f32[1,2,128,128]{3,2,1,0:T(8,128)S(1)} %get-tuple-element.25), channel_id=1, source_target_pairs={{0,5},{1,4},{2,7},{3,6},{4,0},{5,1},{6,2},{7,3},{8,13},{9,12},{10,... | collective-permute-start | bytes 393224 | tf_op jit(solution)/shard_map/ppermute | solution.py:46
  3.9 5.5 %collective-permute-start.2 = (f32[1,2,128,128]{3,2,1,0:T(8,128)S(1)}, f32[1,2,128,128]{3,2,1,0:T(8,128)S(1)}, u32[]{:S(2)}, u32[]{:S(2)}) collective-permute-start(f32[1,2,128,128]{3,2,1,0:T(8,128)S(1)} %get-tuple-element.26.payload_ref), channel_id=1, source_target_pairs={{0,4},{1,6},{2,5},{3,7},{4,0},{5,1},{6,2},{7,3},{8,12},{9,14},{10,... | collective-permute-start | bytes 393224 | tf_op jit(solution)/shard_map/ppermute | solution.py:46
  5.6 8.2 %collective-permute-start.4 = (f32[1,2,128,128]{3,2,1,0:T(8,128)S(1)}, f32[1,2,128,128]{3,2,1,0:T(8,128)S(1)}, u32[]{:S(2)}, u32[]{:S(2)}) collective-permute-start(f32[1,2,128,128]{3,2,1,0:T(8,128)S(1)} %get-tuple-element.25), channel_id=1, source_target_pairs={{0,4},{1,5},{2,6},{3,7},{4,9},{5,8},{6,11},{7,10},{8,12},{9,13},{1... | collective-permute-start | bytes 393224 | tf_op jit(solution)/shard_map/ppermute | solution.py:46
  7.7 6.2 %collective-permute-start.5 = (f32[1,2,128,128]{3,2,1,0:T(8,128)S(1)}, f32[1,2,128,128]{3,2,1,0:T(8,128)S(1)}, u32[]{:S(2)}, u32[]{:S(2)}) collective-permute-start(f32[1,2,128,128]{3,2,1,0:T(8,128)S(1)} %shard_map.59), channel_id=1, source_target_pairs={{0,4},{1,5},{2,6},{3,7},{4,8},{5,10},{6,9},{7,11},{8,12},{9,13},{1... | collective-permute-start | bytes 393224 | tf_op jit(solution)/shard_map/ppermute | solution.py:46
  9.9 8.3 %collective-permute-start.6 = (f32[2,2,128,128]{3,2,1,0:T(8,128)S(1)}, f32[2,2,128,128]{3,2,1,0:T(8,128)S(1)}, u32[]{:S(2)}, u32[]{:S(2)}) collective-permute-start(f32[2,2,128,128]{3,2,1,0:T(8,128)S(1)} %get-tuple-element.27.trace_ref.known_ref), channel_id=1, source_target_pairs={{0,4},{1,5},{2,6},{3,7},{4,8},{5,9},{6,10},{7,11},{8,12},{9,13},{1... | collective-permute-start | bytes 786440 | tf_op jit(solution)/shard_map/ppermute | solution.py:46
  11.1 7.1 %collective-permute-start.7 = (f32[1,2,128,128]{3,2,1,0:T(8,128)S(1)}, f32[1,2,128,128]{3,2,1,0:T(8,128)S(1)}, u32[]{:S(2)}, u32[]{:S(2)}) collective-permute-start(f32[1,2,128,128]{3,2,1,0:T(8,128)S(1)} %get-tuple-element.31), channel_id=1, source_target_pairs={{0,4},{1,5},{2,6},{3,7},{4,9},{5,8},{6,11},{7,10},{8,12},{9,13},{1... | collective-permute-start | bytes 393224 | tf_op jit(solution)/shard_map/ppermute | solution.py:46
  13.8 4.4 %collective-permute-start.8 = (f32[1,2,128,128]{3,2,1,0:T(8,128)S(1)}, f32[1,2,128,128]{3,2,1,0:T(8,128)S(1)}, u32[]{:S(2)}, u32[]{:S(2)}) collective-permute-start(f32[1,2,128,128]{3,2,1,0:T(8,128)S(1)} %get-tuple-element.33), channel_id=1, source_target_pairs={{0,4},{1,5},{2,6},{3,7},{4,8},{5,10},{6,9},{7,11},{8,12},{9,13},{1... | collective-permute-start | bytes 393224 | tf_op jit(solution)/shard_map/ppermute | solution.py:46
  14.0 4.7 %collective-permute-start.9 = (f32[1,2,128,128]{3,2,1,0:T(8,128)S(1)}, f32[1,2,128,128]{3,2,1,0:T(8,128)S(1)}, u32[]{:S(2)}, u32[]{:S(2)}) collective-permute-start(f32[1,2,128,128]{3,2,1,0:T(8,128)S(1)} %get-tuple-element.34), channel_id=1, source_target_pairs={{0,5},{1,4},{2,7},{3,6},{4,0},{5,1},{6,2},{7,3},{8,13},{9,12},{10,... | collective-permute-start | bytes 393224 | tf_op jit(solution)/shard_map/ppermute | solution.py:46
  14.5 4.2 %collective-permute-start.10 = (f32[1,2,128,128]{3,2,1,0:T(8,128)S(1)}, f32[1,2,128,128]{3,2,1,0:T(8,128)S(1)}, u32[]{:S(2)}, u32[]{:S(2)}) collective-permute-start(f32[1,2,128,128]{3,2,1,0:T(8,128)S(1)} %get-tuple-element.35), channel_id=1, source_target_pairs={{0,4},{1,6},{2,5},{3,7},{4,0},{5,1},{6,2},{7,3},{8,12},{9,14},{10,... | collective-permute-start | bytes 393224 | tf_op jit(solution)/shard_map/ppermute | solution.py:46

commit v8 on v7

--- a/solution.py
+++ b/solution.py
@@ -361,9 +361,9 @@
         moved=10**8,
     )
     mate = permute(whole, inward, same)
-    (later,) = call(after_kernel, (mate, odd), (part,), 0)
+    (later,) = call(after_kernel, (mate, even), (part,), 0)
     whole = permute(whole, outward, same)
-    from_odd = permute(even, outward, even_pair), permute(later, outward, odd_pair)
+    from_odd = permute(later, outward, even_pair), permute(odd, outward, odd_pair)
     from_even = permute(even, inward, even_pair), permute(odd, inward, odd_pair)
     matrix, own, mask = call(
         prepare_kernel,

time: 19.9 us -> 19.8 us (level)
  the two profiles are of different devices: /device:TPU:1 before, /device:TPU:3 now
where the time goes in v8:
time: 19.8 us; the launch traced here: 19.4 us
  starting transfers between devices  11.9 us (60%)
  Pallas kernels  5.18 us (26%)
  blocking collectives  2.17 us (11%)
    ppermute x11, starting transfers between devices, permute(): return lax.ppermute(block, ('layer', 'plane'), route)  11.9 us
    pallas_call x9, Pallas kernels, call(): pl.pallas_call(kernel, out_shape=outs, in_specs=[hbm if h else vmem for h...  5.18 us
    all_gather x1, blocking collectives, with_mate(): return lax.all_gather(block, 'layer', axis_index_groups=groups)  2.17 us
  transfers between devices with their start and end apart: 11, of which 0 were waited for; matrix products, arithmetic and copies ran while one was open for 0% of the time, Pallas kernels for 15%

profile of v8, /device:TPU:3, one launch (start us, length us, event | category | flops | bytes accessed | tf_op | source)
XLA Modules:
  0.0 19.4 jit_solution(2724426039205836087)
XLA Ops:
  0.0 1.1 %shard_map.56 = (f32[2,2,128,128]{3,2,1,0:T(8,128)S(1)}, f32[1,2,128,128]{3,2,1,0:T(8,128)S(1)}, f32[1,2,128,128]{3,2,1,0:T(8,128)S(1)}) custom-call(s32[2]{0:T(128)} %bitcast.14, bf16[2,2,128,128]{3,2,1,0:T(8,128)(2,1)} %bitcast.9), custom_call_target="tpu_custom_call" | custom-call | flops 99999997952 | bytes 100000000 | tf_op jit(solution)/shard_map/pallas_call | solution.py:324
  1.1 0.0 copy-start.1
  1.1 0.7 %collective-permute-start = (f32[2,2,128,128]{3,2,1,0:T(8,128)S(1)}, f32[2,2,128,128]{3,2,1,0:T(8,128)S(1)}, u32[]{:S(2)}, u32[]{:S(2)}) collective-permute-start(f32[2,2,128,128]{3,2,1,0:T(8,128)S(1)} %get-tuple-element.24), channel_id=1, source_target_pairs={{0,4},{1,5},{2,6},{3,7},{4,0},{5,1},{6,2},{7,3},{8,12},{9,13},{10,... | collective-permute-start | bytes 786440 | tf_op jit(solution)/shard_map/ppermute | solution.py:46
  1.9 1.2 %collective-permute-start.3 = (f32[2,2,128,128]{3,2,1,0:T(8,128)S(1)}, f32[2,2,128,128]{3,2,1,0:T(8,128)S(1)}, u32[]{:S(2)}, u32[]{:S(2)}) collective-permute-start(f32[2,2,128,128]{3,2,1,0:T(8,128)S(1)} %get-tuple-element.24), channel_id=1, source_target_pairs={{0,4},{1,5},{2,6},{3,7},{4,8},{5,9},{6,10},{7,11},{8,12},{9,13},{1... | collective-permute-start | bytes 786440 | tf_op jit(solution)/shard_map/ppermute | solution.py:46
  3.0 0.0 collective-permute-start.1
  3.0 1.7 %collective-permute-start.2 = (f32[1,2,128,128]{3,2,1,0:T(8,128)S(1)}, f32[1,2,128,128]{3,2,1,0:T(8,128)S(1)}, u32[]{:S(2)}, u32[]{:S(2)}) collective-permute-start(f32[1,2,128,128]{3,2,1,0:T(8,128)S(1)} %get-tuple-element.26), channel_id=1, source_target_pairs={{0,4},{1,6},{2,5},{3,7},{4,0},{5,1},{6,2},{7,3},{8,12},{9,14},{10,... | collective-permute-start | bytes 393224 | tf_op jit(solution)/shard_map/ppermute | solution.py:46
  4.7 1.1 %collective-permute-start.5 = (f32[1,2,128,128]{3,2,1,0:T(8,128)S(1)}, f32[1,2,128,128]{3,2,1,0:T(8,128)S(1)}, u32[]{:S(2)}, u32[]{:S(2)}) collective-permute-start(f32[1,2,128,128]{3,2,1,0:T(8,128)S(1)} %get-tuple-element.26), channel_id=1, source_target_pairs={{0,4},{1,5},{2,6},{3,7},{4,8},{5,10},{6,9},{7,11},{8,12},{9,13},{1... | collective-permute-start | bytes 393224 | tf_op jit(solution)/shard_map/ppermute | solution.py:46
  5.8 0.0 collective-permute-done.all_ref.first_ref
  5.9 1.1 %collective-permute-start.4 = (f32[1,2,128,128]{3,2,1,0:T(8,128)S(1)}, f32[1,2,128,128]{3,2,1,0:T(8,128)S(1)}, u32[]{:S(2)}, u32[]{:S(2)}) collective-permute-start(f32[1,2,128,128]{3,2,1,0:T(8,128)S(1)} %shard_map.59), channel_id=1, source_target_pairs={{0,4},{1,5},{2,6},{3,7},{4,9},{5,8},{6,11},{7,10},{8,12},{9,13},{1... | collective-permute-start | bytes 393224 | tf_op jit(solution)/shard_map/ppermute | solution.py:46
  6.9 1.6 %shard_map.55 = (bf16[512,1536]{1,0:T(8,128)(2,1)S(1)}, f32[2,2,128,128]{3,2,1,0:T(8,128)S(1)}, f32[2,1,2,8,128]{4,3,2,1,0:T(8,128)S(1)}) custom-call(s32[24]{0:T(128)} %bitcast.12, s32[24]{0:T(128)} %bitcast.13, s32[2]{0:T(128)} %bitcast.15, bf16[2,2,128,128]{3,2,1,0:T(8,128)(2,1)} %bitcast.10, f32[24,2,128,128]{3,2,1,0:T(8,128)S(1)} %bitcast.7), custom_call_target="tpu_custom_call" | custom-call | flops 201326592 | bytes 5128392 | tf_op jit(solution)/shard_map/pallas_call | solution.py:324
  8.5 0.0 collective-permute-done.1.even_ref
  8.5 0.0 collective-permute-done.2.odd_ref
  8.5 0.5 %shard_map.57 = (f32[2,2,128,128]{3,2,1,0:T(8,128)S(1)}, f32[1,2,128,128]{3,2,1,0:T(8,128)S(1)}, f32[1,2,128,128]{3,2,1,0:T(8,128)S(1)}) custom-call(f32[2,1,2,8,128]{4,3,2,1,0:T(8,128)S(1)} %get-tuple-element.22.mask_ref, bf16[512,1536]{1,0:T(8,128)(2,1)S(1)} %get-tuple-element.21.matrix_ref, f32[2,2,128,128]{3,2,1,0:T(8,128)S(1)} %get-tuple-element.23.own_ref, ...), custom_call_target="tpu_custom_call" | custom-call | flops 201326592 | bytes 2899968 | tf_op jit(solution)/shard_map/pallas_call | solution.py:324
  9.0 0.1 collective-permute-start.6
  9.1 4.2 %collective-permute-start.7 = (f32[1,2,128,128]{3,2,1,0:T(8,128)S(1)}, f32[1,2,128,128]{3,2,1,0:T(8,128)S(1)}, u32[]{:S(2)}, u32[]{:S(2)}) collective-permute-start(f32[1,2,128,128]{3,2,1,0:T(8,128)S(1)} %get-tuple-element.31), channel_id=1, source_target_pairs={{0,4},{1,5},{2,6},{3,7},{4,9},{5,8},{6,11},{7,10},{8,12},{9,13},{1... | collective-permute-start | bytes 393224 | tf_op jit(solution)/shard_map/ppermute | solution.py:46
  13.3 0.4 %shard_map.58 = (f32[2,2,128,128]{3,2,1,0:T(8,128)S(1)}, f32[1,2,128,128]{3,2,1,0:T(8,128)S(1)}) custom-call(bf16[512,1536]{1,0:T(8,128)(2,1)S(1)} %get-tuple-element.21.matrix_ref, bf16[2,2,128,128]{3,2,1,0:T(8,128)(2,1)S(1)} %bitcast.11, f32[2,2,128,128]{3,2,1,0:T(8,128)S(1)} %get-tuple-element.27.trace_ref.known_ref, ...), custom_call_target="tpu_custom_call" | custom-call | flops 201326592 | bytes 2490368 | tf_op jit(solution)/shard_map/pallas_call | solution.py:324
  13.7 0.0 collective-permute-done.5.odd_ref
  13.7 0.1 collective-permute-start.8
  13.7 0.0 collective-permute-done.3.all_ref
  13.8 0.0 collective-permute-done.4.even_ref
  13.8 0.1 shard_map.60
  13.8 0.9 %collective-permute-start.9 = (f32[1,2,128,128]{3,2,1,0:T(8,128)S(1)}, f32[1,2,128,128]{3,2,1,0:T(8,128)S(1)}, u32[]{:S(2)}, u32[]{:S(2)}) collective-permute-start(f32[1,2,128,128]{3,2,1,0:T(8,128)S(1)} %get-tuple-element.34), channel_id=1, source_target_pairs={{0,5},{1,4},{2,7},{3,6},{4,0},{5,1},{6,2},{7,3},{8,13},{9,12},{10,... | collective-permute-start | bytes 393224 | tf_op jit(solution)/shard_map/ppermute | solution.py:46
  14.8 0.9 %collective-permute-start.10 = (f32[1,2,128,128]{3,2,1,0:T(8,128)S(1)}, f32[1,2,128,128]{3,2,1,0:T(8,128)S(1)}, u32[]{:S(2)}, u32[]{:S(2)}) collective-permute-start(f32[1,2,128,128]{3,2,1,0:T(8,128)S(1)} %get-tuple-element.35), channel_id=1, source_target_pairs={{0,4},{1,6},{2,5},{3,7},{4,0},{5,1},{6,2},{7,3},{8,12},{9,14},{10,... | collective-permute-start | bytes 393224 | tf_op jit(solution)/shard_map/ppermute | solution.py:46
  15.7 2.2 %all-gather = f32[4,2,128,128]{3,2,1,0:T(8,128)S(1)} all-gather(f32[2,2,128,128]{3,2,1,0:T(8,128)S(1)} %get-tuple-element.30.trace_ref), channel_id=2, replica_groups={{0,4},{8,12},{16,20},{24,28},{1,5},{9,13},{17,21},{25,29},{2,6},{10,14}..., dimensions={0}, use_global_device_ids=true | all-gather | bytes 786432 | tf_op jit(solution)/shard_map/all_gather | solution.py:54
  17.8 0.4 %shard_map.61.base_ref = f32[2,2,128,128]{3,2,1,0:T(8,128)S(1)} custom-call(bf16[512,1536]{1,0:T(8,128)(2,1)S(1)} %get-tuple-element.21.matrix_ref, f32[2,2,128,128]{3,2,1,0:T(8,128)S(1)} %get-tuple-element.29.base_ref, f32[2,2,128,128]{3,2,1,0:T(8,128)S(1)} %get-tuple-element.30.trace_ref, f32[2,2,2,128,128]{4,3,2,1,0:T(8,128)S(1)} %bitcast.8), custom_call_target="tpu_custom_call" | custom-call | flops 201326592 | bytes 2883584 | tf_op jit(solution)/shard_map/pallas_call | solution.py:324
  18.2 0.0 collective-permute-done.7.even_ref
  18.2 0.0 collective-permute-done.6.all_ref
  18.2 0.1 shard_map.62
  18.3 0.0 collective-permute-done.8.outer_odd_ref
  18.3 0.0 collective-permute-done.9.inner_even_ref
  18.3 0.0 collective-permute-done.10.inner_odd_ref
  18.3 1.1 %shard_map.63 = f32[2,2,128,128]{3,2,1,0:T(8,128)} custom-call(bf16[512,1536]{1,0:T(8,128)(2,1)S(1)} %get-tuple-element.21.matrix_ref, f32[2,2,128,128]{3,2,1,0:T(8,128)S(1)} %get-tuple-element.32.base_ref, f32[1,2,128,128]{3,2,1,0:T(8,128)S(1)} %collective-permute-done.8.outer_odd_ref, ...), custom_call_target="tpu_custom_call", output_to_operand_aliasing={{}: (5, {})} | custom-call | flops 201326592 | bytes 2752512 | tf_op jit(solution)/shard_map/pallas_call | solution.py:324
  (4 shorter events, 0.0 us)
Async XLA Ops:
  0.0 6.9 %copy-start = (f32[1,24,2,128,128]{4,3,2,1,0:T(8,128)S(1)}, f32[1,24,2,128,128]{4,3,2,1,0:T(8,128)}, u32[]{:S(2)}) copy-start(f32[1,24,2,128,128]{4,3,2,1,0:T(8,128)} %param.6) | copy-start | bytes 9437188
  1.1 12.1 %copy-start.1 = (bf16[1,2,2,128,128]{4,3,2,1,0:T(8,128)(2,1)S(1)}, bf16[1,2,2,128,128]{4,3,2,1,0:T(8,128)(2,1)}, u32[]{:S(2)}) copy-start(bf16[1,2,2,128,128]{4,3,2,1,0:T(8,128)(2,1)} %param.5) | copy-start | bytes 393220
  1.1 4.7 %collective-permute-start = (f32[2,2,128,128]{3,2,1,0:T(8,128)S(1)}, f32[2,2,128,128]{3,2,1,0:T(8,128)S(1)}, u32[]{:S(2)}, u32[]{:S(2)}) collective-permute-start(f32[2,2,128,128]{3,2,1,0:T(8,128)S(1)} %get-tuple-element.24), channel_id=1, source_target_pairs={{0,4},{1,5},{2,6},{3,7},{4,0},{5,1},{6,2},{7,3},{8,12},{9,13},{10,... | collective-permute-start | bytes 786440 | tf_op jit(solution)/shard_map/ppermute | solution.py:46
  1.9 11.9 %collective-permute-start.3 = (f32[2,2,128,128]{3,2,1,0:T(8,128)S(1)}, f32[2,2,128,128]{3,2,1,0:T(8,128)S(1)}, u32[]{:S(2)}, u32[]{:S(2)}) collective-permute-start(f32[2,2,128,128]{3,2,1,0:T(8,128)S(1)} %get-tuple-element.24), channel_id=1, source_target_pairs={{0,4},{1,5},{2,6},{3,7},{4,8},{5,9},{6,10},{7,11},{8,12},{9,13},{1... | collective-permute-start | bytes 786440 | tf_op jit(solution)/shard_map/ppermute | solution.py:46
  3.0 5.5 %collective-permute-start.1 = (f32[1,2,128,128]{3,2,1,0:T(8,128)S(1)}, f32[1,2,128,128]{3,2,1,0:T(8,128)S(1)}, u32[]{:S(2)}, u32[]{:S(2)}) collective-permute-start(f32[1,2,128,128]{3,2,1,0:T(8,128)S(1)} %get-tuple-element.25.payload_ref), channel_id=1, source_target_pairs={{0,5},{1,4},{2,7},{3,6},{4,0},{5,1},{6,2},{7,3},{8,13},{9,12},{10,... | collective-permute-start | bytes 393224 | tf_op jit(solution)/shard_map/ppermute | solution.py:46
  3.0 5.5 %collective-permute-start.2 = (f32[1,2,128,128]{3,2,1,0:T(8,128)S(1)}, f32[1,2,128,128]{3,2,1,0:T(8,128)S(1)}, u32[]{:S(2)}, u32[]{:S(2)}) collective-permute-start(f32[1,2,128,128]{3,2,1,0:T(8,128)S(1)} %get-tuple-element.26), channel_id=1, source_target_pairs={{0,4},{1,6},{2,5},{3,7},{4,0},{5,1},{6,2},{7,3},{8,12},{9,14},{10,... | collective-permute-start | bytes 393224 | tf_op jit(solution)/shard_map/ppermute | solution.py:46
  4.7 8.9 %collective-permute-start.5 = (f32[1,2,128,128]{3,2,1,0:T(8,128)S(1)}, f32[1,2,128,128]{3,2,1,0:T(8,128)S(1)}, u32[]{:S(2)}, u32[]{:S(2)}) collective-permute-start(f32[1,2,128,128]{3,2,1,0:T(8,128)S(1)} %get-tuple-element.26), channel_id=1, source_target_pairs={{0,4},{1,5},{2,6},{3,7},{4,8},{5,10},{6,9},{7,11},{8,12},{9,13},{1... | collective-permute-start | bytes 393224 | tf_op jit(solution)/shard_map/ppermute | solution.py:46
  5.9 7.9 %collective-permute-start.4 = (f32[1,2,128,128]{3,2,1,0:T(8,128)S(1)}, f32[1,2,128,128]{3,2,1,0:T(8,128)S(1)}, u32[]{:S(2)}, u32[]{:S(2)}) collective-permute-start(f32[1,2,128,128]{3,2,1,0:T(8,128)S(1)} %shard_map.59), channel_id=1, source_target_pairs={{0,4},{1,5},{2,6},{3,7},{4,9},{5,8},{6,11},{7,10},{8,12},{9,13},{1... | collective-permute-start | bytes 393224 | tf_op jit(solution)/shard_map/ppermute | solution.py:46
  9.0 9.2 %collective-permute-start.6 = (f32[2,2,128,128]{3,2,1,0:T(8,128)S(1)}, f32[2,2,128,128]{3,2,1,0:T(8,128)S(1)}, u32[]{:S(2)}, u32[]{:S(2)}) collective-permute-start(f32[2,2,128,128]{3,2,1,0:T(8,128)S(1)} %get-tuple-element.27.trace_ref.known_ref), channel_id=1, source_target_pairs={{0,4},{1,5},{2,6},{3,7},{4,8},{5,9},{6,10},{7,11},{8,12},{9,13},{1... | collective-permute-start | bytes 786440 | tf_op jit(solution)/shard_map/ppermute | solution.py:46
  9.1 9.1 %collective-permute-start.7 = (f32[1,2,128,128]{3,2,1,0:T(8,128)S(1)}, f32[1,2,128,128]{3,2,1,0:T(8,128)S(1)}, u32[]{:S(2)}, u32[]{:S(2)}) collective-permute-start(f32[1,2,128,128]{3,2,1,0:T(8,128)S(1)} %get-tuple-element.31), channel_id=1, source_target_pairs={{0,4},{1,5},{2,6},{3,7},{4,9},{5,8},{6,11},{7,10},{8,12},{9,13},{1... | collective-permute-start | bytes 393224 | tf_op jit(solution)/shard_map/ppermute | solution.py:46
  13.7 4.6 %collective-permute-start.8 = (f32[1,2,128,128]{3,2,1,0:T(8,128)S(1)}, f32[1,2,128,128]{3,2,1,0:T(8,128)S(1)}, u32[]{:S(2)}, u32[]{:S(2)}) collective-permute-start(f32[1,2,128,128]{3,2,1,0:T(8,128)S(1)} %get-tuple-element.33), channel_id=1, source_target_pairs={{0,4},{1,5},{2,6},{3,7},{4,8},{5,10},{6,9},{7,11},{8,12},{9,13},{1... | collective-permute-start | bytes 393224 | tf_op jit(solution)/shard_map/ppermute | solution.py:46
  13.8 4.5 %collective-permute-start.9 = (f32[1,2,128,128]{3,2,1,0:T(8,128)S(1)}, f32[1,2,128,128]{3,2,1,0:T(8,128)S(1)}, u32[]{:S(2)}, u32[]{:S(2)}) collective-permute-start(f32[1,2,128,128]{3,2,1,0:T(8,128)S(1)} %get-tuple-element.34), channel_id=1, source_target_pairs={{0,5},{1,4},{2,7},{3,6},{4,0},{5,1},{6,2},{7,3},{8,13},{9,12},{10,... | collective-permute-start | bytes 393224 | tf_op jit(solution)/shard_map/ppermute | solution.py:46
  14.8 3.5 %collective-permute-start.10 = (f32[1,2,128,128]{3,2,1,0:T(8,128)S(1)}, f32[1,2,128,128]{3,2,1,0:T(8,128)S(1)}, u32[]{:S(2)}, u32[]{:S(2)}) collective-permute-start(f32[1,2,128,128]{3,2,1,0:T(8,128)S(1)} %get-tuple-element.35), channel_id=1, source_target_pairs={{0,4},{1,6},{2,5},{3,7},{4,0},{5,1},{6,2},{7,3},{8,12},{9,14},{10,... | collective-permute-start | bytes 393224 | tf_op jit(solution)/shard_map/ppermute | solution.py:46

commit v9 on v8

--- a/solution.py
+++ b/solution.py
@@ -8,7 +8,6 @@
 F32 = jnp.float32
 BF16 = jnp.bfloat16
 LIMIT = 40 * 1024 * 1024
-LONG = 10**11
 
 
 def even_pair(p, planes):
@@ -44,6 +43,10 @@
             to_layer, to_plane = way(l, p, layers, planes, partner)
             route.append((l * planes + p, to_layer * planes + to_plane))
     return lax.ppermute(block, ("layer", "plane"), route)
+
+
+def onward(l, p, layers, planes, partner):
+    return (l + 1) % layers, p
 
 
 def with_mate(block):
@@ -119,16 +122,15 @@
 
 
 def prepare_kernel(
-    rows_hbm, cols_hbm, send_hbm, source_hbm, tiles_ref,
+    rows_in, cols_in, send_in, source_ref, tiles_ref,
     matrix_ref, own_ref, mask_ref,
-    rows_ref, cols_ref, send_ref, source_ref, total, sems,
+    rows_ref, cols_ref, send_ref, total, sems,
 ):
     tile_count, _, width, _ = tiles_ref.shape
     blocks_here = source_ref.shape[0]
     extended = total.shape[0] // blocks_here
     listed = (extended - 2 * blocks_here) // 2
-    small = [(rows_hbm, rows_ref), (cols_hbm, cols_ref), (send_hbm, send_ref)]
-    copies = fetch(small + [(source_hbm, source_ref)], sems)
+    copies = fetch([(rows_in, rows_ref), (cols_in, cols_ref), (send_in, send_ref)], sems)
     layer = lax.axis_index("layer")
     plane = lax.axis_index("plane")
     planes = lax.axis_size("plane")
@@ -146,7 +148,7 @@
         total[slot, :, width:] += tiles_ref[t, 1]
         return carry
 
-    for copy in copies[:3]:
+    for copy in copies:
         copy.wait()
     for k in range(listed):
         to_even = send_ref[(1 - is_odd) * listed + k]
@@ -176,7 +178,6 @@
             here = slice(c * 2 * width, (c + 1) * 2 * width)
             matrix_ref[r * width : (r + 1) * width, here] = high
             matrix_ref[height + r * width : height + (r + 1) * width, here] = low
-    copies[-1].wait()
     own = operand([(source_ref[b, 0], source_ref[b, 1]) for b in range(blocks_here)])
     columns = slice((extended - blocks_here) * 2 * width, None)
     store(two_products(matrix_ref, columns, own), source_ref, own_ref)
@@ -289,23 +290,35 @@
 
 
 def last_kernel(
-    matrix_ref, base_ref, outer_odd_ref, inner_even_ref, inner_odd_ref, begun_hbm, final_hbm, out_ref, sem
+    matrix_ref, base_ref, outer_odd_ref, inner_even_ref, inner_odd_ref, begun_hbm, final_hbm, out_ref, sems
 ):
-    blocks = base_ref.shape[0]
+    blocks, _, width, shots = base_ref.shape
+
+    def finish(first, refs):
+        received = gather(*refs)
+        halves = [(split(x), split(y)) for x, y in received]
+        high = operand([(x[0], y[0]) for x, y in halves])
+        low = operand([(x[1], y[1]) for x, y in halves])
+        columns = slice(first * 2 * width, (first + len(received)) * 2 * width)
+        copies = []
+        for b in range(blocks):
+            upper = matrix_ref[b * width : (b + 1) * width, columns]
+            under = matrix_ref[(blocks + b) * width : (blocks + b + 1) * width, columns]
+            result = product(upper, high) + product(under, high) + product(upper, low)
+            for part in range(2):
+                out_ref[b, part] = result[:, part * shots : (part + 1) * shots] + base_ref[b, part]
+            copies.append(pltpu.make_async_copy(out_ref.at[b], final_hbm.at[b], sems.at[b]))
+            copies[-1].start()
+        for copy in copies:
+            copy.wait()
 
     @pl.when(on_odd_layer())
     def _():
-        third_tick(matrix_ref, blocks, base_ref, (inner_even_ref, inner_odd_ref), out_ref)
+        finish(blocks, (inner_even_ref, inner_odd_ref))
 
     @pl.when(on_even_layer())
     def _():
-        third_tick(matrix_ref, blocks + inner_even_ref.shape[0], base_ref, (outer_odd_ref,), out_ref)
-
-    @pl.when(lax.axis_index("layer") > 0)
-    def _():
-        copy = pltpu.make_async_copy(out_ref, final_hbm, sem)
-        copy.start()
-        copy.wait()
+        finish(blocks + inner_even_ref.shape[0], (outer_odd_ref,))
 
 
 def call(kernel, ins, outs, flops, scratch=(), in_hbm=False, moved=None, last_in_hbm=False, last_out_hbm=False):
@@ -355,7 +368,7 @@
         widen_kernel,
         (send, source),
         (trace, part, part),
-        LONG,
+        10**11,
         [send_copy, source_copy, pltpu.SemaphoreType.DMA((2,))],
         in_hbm=True,
         moved=10**8,
@@ -374,18 +387,15 @@
             pltpu.SMEM(rows.shape, rows.dtype),
             pltpu.SMEM(cols.shape, cols.dtype),
             send_copy,
-            source_copy,
             pltpu.VMEM((blocks * extended, width, 2 * width), F32),
-            pltpu.SemaphoreType.DMA((4,)),
+            pltpu.SemaphoreType.DMA((3,)),
         ],
-        in_hbm=True,
     )
     second, even, odd = call(odd_kernel, (mask, matrix, own, mate, *from_even), (trace, part, part), flops)
     third, odd = call(odd_own_kernel, (matrix, source, second, odd), (trace, part), flops)
     early = permute(second, outward, same), permute(even, outward, even_pair), permute(odd, outward, odd_pair)
     traces, even, odd = call(
-        even_kernel, (mask, matrix, own, second, whole, *from_odd), (trace, part, part), flops
-    )
+        even_kernel, (mask, matrix, own, second, whole, *from_odd), (trace, part, part), flops)
     late_even = permute(even, inward, even_pair)
     late_odd = permute(odd, inward, odd_pair)
     pair = with_mate(traces)
@@ -394,7 +404,7 @@
         even_part_kernel,
         (matrix, own, *early[:2]),
         (trace, trace),
-        LONG,
+        10**11,
         [pltpu.SemaphoreType.DMA],
         moved=10**9,
         last_out_hbm=True,
@@ -404,7 +414,7 @@
         (matrix, own, early[2], late_even, late_odd, begun),
         (trace,),
         flops,
-        [pltpu.VMEM(trace.shape, F32), pltpu.SemaphoreType.DMA],
+        [pltpu.VMEM(trace.shape, F32), pltpu.SemaphoreType.DMA((blocks,))],
         last_in_hbm=True,
         last_out_hbm=True,
     )

time: 19.8 us -> 19.8 us (level)
  Pallas kernels: 5.18 us -> 4.96 us
  starting transfers between devices: 11.9 us -> 12.1 us
    pallas_call x9, Pallas kernels: 5.18 us -> 4.96 us  [call(): pl.pallas_call(kernel, out_shape=outs, in_specs=[hbm if h else vmem for h...]
    ppermute x11, starting transfers between devices: 11.9 us -> 12.1 us  [permute(): return lax.ppermute(block, ('layer', 'plane'), route)]
  transfers between devices with their start and end apart: 11 -> 11, of which waited for: 0 -> 0; matrix products, arithmetic and copies ran while one was open for 0% -> 0% of each run, Pallas kernels for 15% -> 14%
where the time goes in v9:
time: 19.8 us; the launch traced here: 19.5 us
  starting transfers between devices  12.1 us (61%)
  Pallas kernels  4.96 us (25%)
  blocking collectives  2.17 us (11%)
    ppermute x11, starting transfers between devices, permute(): return lax.ppermute(block, ('layer', 'plane'), route)  12.1 us
    pallas_call x9, Pallas kernels, call(): pl.pallas_call(kernel, out_shape=outs, in_specs=[hbm if h else vmem for h...  4.96 us
    all_gather x1, blocking collectives, with_mate(): return lax.all_gather(block, 'layer', axis_index_groups=groups)  2.17 us
  transfers between devices with their start and end apart: 11, of which 0 were waited for; matrix products, arithmetic and copies ran while one was open for 0% of the time, Pallas kernels for 14%

profile of v9, /device:TPU:3, one launch (start us, length us, event | category | flops | bytes accessed | tf_op | source)
XLA Modules:
  0.0 19.5 jit_solution(1363820455834579759)
XLA Ops:
  0.0 1.1 %shard_map.56 = (f32[2,2,128,128]{3,2,1,0:T(8,128)S(1)}, f32[1,2,128,128]{3,2,1,0:T(8,128)S(1)}, f32[1,2,128,128]{3,2,1,0:T(8,128)S(1)}) custom-call(s32[2]{0:T(128)} %bitcast.14, bf16[2,2,128,128]{3,2,1,0:T(8,128)(2,1)} %bitcast.9), custom_call_target="tpu_custom_call" | custom-call | flops 99999997952 | bytes 100000000 | tf_op jit(solution)/shard_map/pallas_call | solution.py:337
  1.2 0.7 %collective-permute-start = (f32[2,2,128,128]{3,2,1,0:T(8,128)S(1)}, f32[2,2,128,128]{3,2,1,0:T(8,128)S(1)}, u32[]{:S(2)}, u32[]{:S(2)}) collective-permute-start(f32[2,2,128,128]{3,2,1,0:T(8,128)S(1)} %get-tuple-element.24), channel_id=1, source_target_pairs={{0,4},{1,5},{2,6},{3,7},{4,0},{5,1},{6,2},{7,3},{8,12},{9,13},{10,... | collective-permute-start | bytes 786440 | tf_op jit(solution)/shard_map/ppermute | solution.py:45
  1.9 1.2 %collective-permute-start.3 = (f32[2,2,128,128]{3,2,1,0:T(8,128)S(1)}, f32[2,2,128,128]{3,2,1,0:T(8,128)S(1)}, u32[]{:S(2)}, u32[]{:S(2)}) collective-permute-start(f32[2,2,128,128]{3,2,1,0:T(8,128)S(1)} %get-tuple-element.24), channel_id=1, source_target_pairs={{0,4},{1,5},{2,6},{3,7},{4,8},{5,9},{6,10},{7,11},{8,12},{9,13},{1... | collective-permute-start | bytes 786440 | tf_op jit(solution)/shard_map/ppermute | solution.py:45
  3.1 0.0 collective-permute-start.1
  3.1 1.7 %collective-permute-start.2 = (f32[1,2,128,128]{3,2,1,0:T(8,128)S(1)}, f32[1,2,128,128]{3,2,1,0:T(8,128)S(1)}, u32[]{:S(2)}, u32[]{:S(2)}) collective-permute-start(f32[1,2,128,128]{3,2,1,0:T(8,128)S(1)} %get-tuple-element.26), channel_id=1, source_target_pairs={{0,4},{1,6},{2,5},{3,7},{4,0},{5,1},{6,2},{7,3},{8,12},{9,14},{10,... | collective-permute-start | bytes 393224 | tf_op jit(solution)/shard_map/ppermute | solution.py:45
  4.8 1.1 %collective-permute-start.5 = (f32[1,2,128,128]{3,2,1,0:T(8,128)S(1)}, f32[1,2,128,128]{3,2,1,0:T(8,128)S(1)}, u32[]{:S(2)}, u32[]{:S(2)}) collective-permute-start(f32[1,2,128,128]{3,2,1,0:T(8,128)S(1)} %get-tuple-element.26), channel_id=1, source_target_pairs={{0,4},{1,5},{2,6},{3,7},{4,8},{5,10},{6,9},{7,11},{8,12},{9,13},{1... | collective-permute-start | bytes 393224 | tf_op jit(solution)/shard_map/ppermute | solution.py:45
  5.9 0.0 collective-permute-done.all_ref.first_ref
  5.9 1.1 %collective-permute-start.4 = (f32[1,2,128,128]{3,2,1,0:T(8,128)S(1)}, f32[1,2,128,128]{3,2,1,0:T(8,128)S(1)}, u32[]{:S(2)}, u32[]{:S(2)}) collective-permute-start(f32[1,2,128,128]{3,2,1,0:T(8,128)S(1)} %shard_map.59), channel_id=1, source_target_pairs={{0,4},{1,5},{2,6},{3,7},{4,9},{5,8},{6,11},{7,10},{8,12},{9,13},{1... | collective-permute-start | bytes 393224 | tf_op jit(solution)/shard_map/ppermute | solution.py:45
  6.9 0.0 copy-done.1
  7.0 1.3 %shard_map.55 = (bf16[512,1536]{1,0:T(8,128)(2,1)S(1)}, f32[2,2,128,128]{3,2,1,0:T(8,128)S(1)}, f32[2,1,2,8,128]{4,3,2,1,0:T(8,128)S(1)}) custom-call(s32[24]{0:T(128)S(1)} %bitcast.12, s32[24]{0:T(128)S(1)} %bitcast.13, s32[2]{0:T(128)S(1)} %bitcast.15, bf16[2,2,128,128]{3,2,1,0:T(8,128)(2,1)S(1)} %bitcast.10, f32[24,2,128,128]{3,2,1,0:T(8,128)S(1)} %bitcast.7), custom_call_target="tpu_custom_call" | custom-call | flops 201326592 | bytes 5128392 | tf_op jit(solution)/shard_map/pallas_call | solution.py:337
  8.3 0.0 collective-permute-done.1.even_ref
  8.3 0.0 collective-permute-done.2.odd_ref
  8.3 0.5 %shard_map.57 = (f32[2,2,128,128]{3,2,1,0:T(8,128)S(1)}, f32[1,2,128,128]{3,2,1,0:T(8,128)S(1)}, f32[1,2,128,128]{3,2,1,0:T(8,128)S(1)}) custom-call(f32[2,1,2,8,128]{4,3,2,1,0:T(8,128)S(1)} %get-tuple-element.22.mask_ref, bf16[512,1536]{1,0:T(8,128)(2,1)S(1)} %get-tuple-element.21.matrix_ref, f32[2,2,128,128]{3,2,1,0:T(8,128)S(1)} %get-tuple-element.23.own_ref, ...), custom_call_target="tpu_custom_call" | custom-call | flops 201326592 | bytes 2899968 | tf_op jit(solution)/shard_map/pallas_call | solution.py:337
  8.8 0.1 collective-permute-start.6
  8.9 4.4 %collective-permute-start.7 = (f32[1,2,128,128]{3,2,1,0:T(8,128)S(1)}, f32[1,2,128,128]{3,2,1,0:T(8,128)S(1)}, u32[]{:S(2)}, u32[]{:S(2)}) collective-permute-start(f32[1,2,128,128]{3,2,1,0:T(8,128)S(1)} %get-tuple-element.31), channel_id=1, source_target_pairs={{0,4},{1,5},{2,6},{3,7},{4,9},{5,8},{6,11},{7,10},{8,12},{9,13},{1... | collective-permute-start | bytes 393224 | tf_op jit(solution)/shard_map/ppermute | solution.py:45
  13.3 0.4 %shard_map.58 = (f32[2,2,128,128]{3,2,1,0:T(8,128)S(1)}, f32[1,2,128,128]{3,2,1,0:T(8,128)S(1)}) custom-call(bf16[512,1536]{1,0:T(8,128)(2,1)S(1)} %get-tuple-element.21.matrix_ref, bf16[2,2,128,128]{3,2,1,0:T(8,128)(2,1)S(1)} %bitcast.11, f32[2,2,128,128]{3,2,1,0:T(8,128)S(1)} %get-tuple-element.27.trace_ref.known_ref, ...), custom_call_target="tpu_custom_call" | custom-call | flops 201326592 | bytes 2490368 | tf_op jit(solution)/shard_map/pallas_call | solution.py:337
  13.7 0.0 collective-permute-done.5.odd_ref
  13.7 0.1 collective-permute-start.8
  13.8 0.0 collective-permute-done.3.all_ref
  13.8 0.0 collective-permute-done.4.even_ref
  13.8 0.1 shard_map.60
  13.9 0.9 %collective-permute-start.9 = (f32[1,2,128,128]{3,2,1,0:T(8,128)S(1)}, f32[1,2,128,128]{3,2,1,0:T(8,128)S(1)}, u32[]{:S(2)}, u32[]{:S(2)}) collective-permute-start(f32[1,2,128,128]{3,2,1,0:T(8,128)S(1)} %get-tuple-element.34), channel_id=1, source_target_pairs={{0,5},{1,4},{2,7},{3,6},{4,0},{5,1},{6,2},{7,3},{8,13},{9,12},{10,... | collective-permute-start | bytes 393224 | tf_op jit(solution)/shard_map/ppermute | solution.py:45
  14.8 0.9 %collective-permute-start.10 = (f32[1,2,128,128]{3,2,1,0:T(8,128)S(1)}, f32[1,2,128,128]{3,2,1,0:T(8,128)S(1)}, u32[]{:S(2)}, u32[]{:S(2)}) collective-permute-start(f32[1,2,128,128]{3,2,1,0:T(8,128)S(1)} %get-tuple-element.35), channel_id=1, source_target_pairs={{0,4},{1,6},{2,5},{3,7},{4,0},{5,1},{6,2},{7,3},{8,12},{9,14},{10,... | collective-permute-start | bytes 393224 | tf_op jit(solution)/shard_map/ppermute | solution.py:45
  15.7 2.2 %all-gather = f32[4,2,128,128]{3,2,1,0:T(8,128)S(1)} all-gather(f32[2,2,128,128]{3,2,1,0:T(8,128)S(1)} %get-tuple-element.30.trace_ref), channel_id=2, replica_groups={{0,4},{8,12},{16,20},{24,28},{1,5},{9,13},{17,21},{25,29},{2,6},{10,14}..., dimensions={0}, use_global_device_ids=true | all-gather | bytes 786432 | tf_op jit(solution)/shard_map/all_gather | solution.py:57
  17.9 0.4 %shard_map.61.base_ref = f32[2,2,128,128]{3,2,1,0:T(8,128)S(1)} custom-call(bf16[512,1536]{1,0:T(8,128)(2,1)S(1)} %get-tuple-element.21.matrix_ref, f32[2,2,128,128]{3,2,1,0:T(8,128)S(1)} %get-tuple-element.29.base_ref, f32[2,2,128,128]{3,2,1,0:T(8,128)S(1)} %get-tuple-element.30.trace_ref, f32[2,2,2,128,128]{4,3,2,1,0:T(8,128)S(1)} %bitcast.8), custom_call_target="tpu_custom_call" | custom-call | flops 201326592 | bytes 2883584 | tf_op jit(solution)/shard_map/pallas_call | solution.py:337
  18.2 0.0 collective-permute-done.7.even_ref
  18.2 0.0 collective-permute-done.6.all_ref
  18.3 0.1 shard_map.62
  18.3 0.0 collective-permute-done.8.outer_odd_ref
  18.3 0.0 collective-permute-done.9.inner_even_ref
  18.3 0.0 collective-permute-done.10.inner_odd_ref
  18.4 1.1 %shard_map.63 = f32[2,2,128,128]{3,2,1,0:T(8,128)} custom-call(bf16[512,1536]{1,0:T(8,128)(2,1)S(1)} %get-tuple-element.21.matrix_ref, f32[2,2,128,128]{3,2,1,0:T(8,128)S(1)} %get-tuple-element.32.base_ref, f32[1,2,128,128]{3,2,1,0:T(8,128)S(1)} %collective-permute-done.8.outer_odd_ref, ...), custom_call_target="tpu_custom_call", output_to_operand_aliasing={{}: (5, {})} | custom-call | flops 201326592 | bytes 2752512 | tf_op jit(solution)/shard_map/pallas_call | solution.py:337
  (10 shorter events, 0.0 us)
Async XLA Ops:
  0.0 6.9 %copy-start = (f32[1,24,2,128,128]{4,3,2,1,0:T(8,128)S(1)}, f32[1,24,2,128,128]{4,3,2,1,0:T(8,128)}, u32[]{:S(2)}) copy-start(f32[1,24,2,128,128]{4,3,2,1,0:T(8,128)} %param.6) | copy-start | bytes 9437188
  0.0 6.9 %copy-start.1 = (bf16[1,2,2,128,128]{4,3,2,1,0:T(8,128)(2,1)S(1)}, bf16[1,2,2,128,128]{4,3,2,1,0:T(8,128)(2,1)}, u32[]{:S(2)}) copy-start(bf16[1,2,2,128,128]{4,3,2,1,0:T(8,128)(2,1)} %param.5) | copy-start | bytes 393220
  0.0 6.9 %copy-start.2 = (s32[1,24]{1,0:T(1,128)S(1)}, s32[1,24]{1,0:T(1,128)}, u32[]{:S(2)}) copy-start(s32[1,24]{1,0:T(1,128)} %param.7) | copy-start | bytes 292
  0.0 6.9 %copy-start.3 = (s32[1,24]{1,0:T(1,128)S(1)}, s32[1,24]{1,0:T(1,128)}, u32[]{:S(2)}) copy-start(s32[1,24]{1,0:T(1,128)} %param.8) | copy-start | bytes 292
  0.0 6.9 %copy-start.4 = (s32[1,2,1]{1,2,0:T(1,128)S(1)}, s32[1,2,1]{1,2,0:T(1,128)}, u32[]{:S(2)}) copy-start(s32[1,2,1]{1,2,0:T(1,128)} %param.9) | copy-start | bytes 28
  1.2 4.7 %collective-permute-start = (f32[2,2,128,128]{3,2,1,0:T(8,128)S(1)}, f32[2,2,128,128]{3,2,1,0:T(8,128)S(1)}, u32[]{:S(2)}, u32[]{:S(2)}) collective-permute-start(f32[2,2,128,128]{3,2,1,0:T(8,128)S(1)} %get-tuple-element.24), channel_id=1, source_target_pairs={{0,4},{1,5},{2,6},{3,7},{4,0},{5,1},{6,2},{7,3},{8,12},{9,13},{10,... | collective-permute-start | bytes 786440 | tf_op jit(solution)/shard_map/ppermute | solution.py:45
  1.9 11.9 %collective-permute-start.3 = (f32[2,2,128,128]{3,2,1,0:T(8,128)S(1)}, f32[2,2,128,128]{3,2,1,0:T(8,128)S(1)}, u32[]{:S(2)}, u32[]{:S(2)}) collective-permute-start(f32[2,2,128,128]{3,2,1,0:T(8,128)S(1)} %get-tuple-element.24), channel_id=1, source_target_pairs={{0,4},{1,5},{2,6},{3,7},{4,8},{5,9},{6,10},{7,11},{8,12},{9,13},{1... | collective-permute-start | bytes 786440 | tf_op jit(solution)/shard_map/ppermute | solution.py:45
  3.1 5.2 %collective-permute-start.1 = (f32[1,2,128,128]{3,2,1,0:T(8,128)S(1)}, f32[1,2,128,128]{3,2,1,0:T(8,128)S(1)}, u32[]{:S(2)}, u32[]{:S(2)}) collective-permute-start(f32[1,2,128,128]{3,2,1,0:T(8,128)S(1)} %get-tuple-element.25.payload_ref), channel_id=1, source_target_pairs={{0,5},{1,4},{2,7},{3,6},{4,0},{5,1},{6,2},{7,3},{8,13},{9,12},{10,... | collective-permute-start | bytes 393224 | tf_op jit(solution)/shard_map/ppermute | solution.py:45
  3.1 5.2 %collective-permute-start.2 = (f32[1,2,128,128]{3,2,1,0:T(8,128)S(1)}, f32[1,2,128,128]{3,2,1,0:T(8,128)S(1)}, u32[]{:S(2)}, u32[]{:S(2)}) collective-permute-start(f32[1,2,128,128]{3,2,1,0:T(8,128)S(1)} %get-tuple-element.26), channel_id=1, source_target_pairs={{0,4},{1,6},{2,5},{3,7},{4,0},{5,1},{6,2},{7,3},{8,12},{9,14},{10,... | collective-permute-start | bytes 393224 | tf_op jit(solution)/shard_map/ppermute | solution.py:45
  4.8 8.9 %collective-permute-start.5 = (f32[1,2,128,128]{3,2,1,0:T(8,128)S(1)}, f32[1,2,128,128]{3,2,1,0:T(8,128)S(1)}, u32[]{:S(2)}, u32[]{:S(2)}) collective-permute-start(f32[1,2,128,128]{3,2,1,0:T(8,128)S(1)} %get-tuple-element.26), channel_id=1, source_target_pairs={{0,4},{1,5},{2,6},{3,7},{4,8},{5,10},{6,9},{7,11},{8,12},{9,13},{1... | collective-permute-start | bytes 393224 | tf_op jit(solution)/shard_map/ppermute | solution.py:45
  5.9 7.9 %collective-permute-start.4 = (f32[1,2,128,128]{3,2,1,0:T(8,128)S(1)}, f32[1,2,128,128]{3,2,1,0:T(8,128)S(1)}, u32[]{:S(2)}, u32[]{:S(2)}) collective-permute-start(f32[1,2,128,128]{3,2,1,0:T(8,128)S(1)} %shard_map.59), channel_id=1, source_target_pairs={{0,4},{1,5},{2,6},{3,7},{4,9},{5,8},{6,11},{7,10},{8,12},{9,13},{1... | collective-permute-start | bytes 393224 | tf_op jit(solution)/shard_map/ppermute | solution.py:45
  8.8 9.4 %collective-permute-start.6 = (f32[2,2,128,128]{3,2,1,0:T(8,128)S(1)}, f32[2,2,128,128]{3,2,1,0:T(8,128)S(1)}, u32[]{:S(2)}, u32[]{:S(2)}) collective-permute-start(f32[2,2,128,128]{3,2,1,0:T(8,128)S(1)} %get-tuple-element.27.trace_ref.known_ref), channel_id=1, source_target_pairs={{0,4},{1,5},{2,6},{3,7},{4,8},{5,9},{6,10},{7,11},{8,12},{9,13},{1... | collective-permute-start | bytes 786440 | tf_op jit(solution)/shard_map/ppermute | solution.py:45
  8.9 9.4 %collective-permute-start.7 = (f32[1,2,128,128]{3,2,1,0:T(8,128)S(1)}, f32[1,2,128,128]{3,2,1,0:T(8,128)S(1)}, u32[]{:S(2)}, u32[]{:S(2)}) collective-permute-start(f32[1,2,128,128]{3,2,1,0:T(8,128)S(1)} %get-tuple-element.31), channel_id=1, source_target_pairs={{0,4},{1,5},{2,6},{3,7},{4,9},{5,8},{6,11},{7,10},{8,12},{9,13},{1... | collective-permute-start | bytes 393224 | tf_op jit(solution)/shard_map/ppermute | solution.py:45
  13.7 4.6 %collective-permute-start.8 = (f32[1,2,128,128]{3,2,1,0:T(8,128)S(1)}, f32[1,2,128,128]{3,2,1,0:T(8,128)S(1)}, u32[]{:S(2)}, u32[]{:S(2)}) collective-permute-start(f32[1,2,128,128]{3,2,1,0:T(8,128)S(1)} %get-tuple-element.33), channel_id=1, source_target_pairs={{0,4},{1,5},{2,6},{3,7},{4,8},{5,10},{6,9},{7,11},{8,12},{9,13},{1... | collective-permute-start | bytes 393224 | tf_op jit(solution)/shard_map/ppermute | solution.py:45
  13.9 4.5 %collective-permute-start.9 = (f32[1,2,128,128]{3,2,1,0:T(8,128)S(1)}, f32[1,2,128,128]{3,2,1,0:T(8,128)S(1)}, u32[]{:S(2)}, u32[]{:S(2)}) collective-permute-start(f32[1,2,128,128]{3,2,1,0:T(8,128)S(1)} %get-tuple-element.34), channel_id=1, source_target_pairs={{0,5},{1,4},{2,7},{3,6},{4,0},{5,1},{6,2},{7,3},{8,13},{9,12},{10,... | collective-permute-start | bytes 393224 | tf_op jit(solution)/shard_map/ppermute | solution.py:45
  14.8 3.5 %collective-permute-start.10 = (f32[1,2,128,128]{3,2,1,0:T(8,128)S(1)}, f32[1,2,128,128]{3,2,1,0:T(8,128)S(1)}, u32[]{:S(2)}, u32[]{:S(2)}) collective-permute-start(f32[1,2,128,128]{3,2,1,0:T(8,128)S(1)} %get-tuple-element.35), channel_id=1, source_target_pairs={{0,4},{1,6},{2,5},{3,7},{4,0},{5,1},{6,2},{7,3},{8,12},{9,14},{10,... | collective-permute-start | bytes 393224 | tf_op jit(solution)/shard_map/ppermute | solution.py:45

commit v10 on v9

--- a/solution.py
+++ b/solution.py
@@ -8,6 +8,7 @@
 F32 = jnp.float32
 BF16 = jnp.bfloat16
 LIMIT = 40 * 1024 * 1024
+LONG = 10**11
 
 
 def even_pair(p, planes):
@@ -43,10 +44,6 @@
             to_layer, to_plane = way(l, p, layers, planes, partner)
             route.append((l * planes + p, to_layer * planes + to_plane))
     return lax.ppermute(block, ("layer", "plane"), route)
-
-
-def onward(l, p, layers, planes, partner):
-    return (l + 1) % layers, p
 
 
 def with_mate(block):
@@ -122,15 +119,16 @@
 
 
 def prepare_kernel(
-    rows_in, cols_in, send_in, source_ref, tiles_ref,
+    rows_hbm, cols_hbm, send_hbm, source_hbm, tiles_ref,
     matrix_ref, own_ref, mask_ref,
-    rows_ref, cols_ref, send_ref, total, sems,
+    rows_ref, cols_ref, send_ref, source_ref, total, sems,
 ):
     tile_count, _, width, _ = tiles_ref.shape
     blocks_here = source_ref.shape[0]
     extended = total.shape[0] // blocks_here
     listed = (extended - 2 * blocks_here) // 2
-    copies = fetch([(rows_in, rows_ref), (cols_in, cols_ref), (send_in, send_ref)], sems)
+    small = [(rows_hbm, rows_ref), (cols_hbm, cols_ref), (send_hbm, send_ref)]
+    copies = fetch(small + [(source_hbm, source_ref)], sems)
     layer = lax.axis_index("layer")
     plane = lax.axis_index("plane")
     planes = lax.axis_size("plane")
@@ -148,7 +146,7 @@
         total[slot, :, width:] += tiles_ref[t, 1]
         return carry
 
-    for copy in copies:
+    for copy in copies[:3]:
         copy.wait()
     for k in range(listed):
         to_even = send_ref[(1 - is_odd) * listed + k]
@@ -178,6 +176,7 @@
             here = slice(c * 2 * width, (c + 1) * 2 * width)
             matrix_ref[r * width : (r + 1) * width, here] = high
             matrix_ref[height + r * width : height + (r + 1) * width, here] = low
+    copies[-1].wait()
     own = operand([(source_ref[b, 0], source_ref[b, 1]) for b in range(blocks_here)])
     columns = slice((extended - blocks_here) * 2 * width, None)
     store(two_products(matrix_ref, columns, own), source_ref, own_ref)
@@ -368,7 +367,7 @@
         widen_kernel,
         (send, source),
         (trace, part, part),
-        10**11,
+        LONG,
         [send_copy, source_copy, pltpu.SemaphoreType.DMA((2,))],
         in_hbm=True,
         moved=10**8,
@@ -387,15 +386,18 @@
             pltpu.SMEM(rows.shape, rows.dtype),
             pltpu.SMEM(cols.shape, cols.dtype),
             send_copy,
+            source_copy,
             pltpu.VMEM((blocks * extended, width, 2 * width), F32),
-            pltpu.SemaphoreType.DMA((3,)),
+            pltpu.SemaphoreType.DMA((4,)),
         ],
+        in_hbm=True,
     )
     second, even, odd = call(odd_kernel, (mask, matrix, own, mate, *from_even), (trace, part, part), flops)
     third, odd = call(odd_own_kernel, (matrix, source, second, odd), (trace, part), flops)
     early = permute(second, outward, same), permute(even, outward, even_pair), permute(odd, outward, odd_pair)
     traces, even, odd = call(
-        even_kernel, (mask, matrix, own, second, whole, *from_odd), (trace, part, part), flops)
+        even_kernel, (mask, matrix, own, second, whole, *from_odd), (trace, part, part), flops
+    )
     late_even = permute(even, inward, even_pair)
     late_odd = permute(odd, inward, odd_pair)
     pair = with_mate(traces)
@@ -404,7 +406,7 @@
         even_part_kernel,
         (matrix, own, *early[:2]),
         (trace, trace),
-        10**11,
+        LONG,
         [pltpu.SemaphoreType.DMA],
         moved=10**9,
         last_out_hbm=True,

time: 19.8 us -> 19.8 us (level)
  Pallas kernels: 4.96 us -> 5.19 us
  starting transfers between devices: 12.1 us -> 11.9 us
    pallas_call x9, Pallas kernels: 4.96 us -> 5.19 us  [call(): pl.pallas_call(kernel, out_shape=outs, in_specs=[hbm if h else vmem for h...]
    ppermute x11, starting transfers between devices: 12.1 us -> 11.9 us  [permute(): return lax.ppermute(block, ('layer', 'plane'), route)]
  transfers between devices with their start and end apart: 11 -> 11, of which waited for: 0 -> 0; matrix products, arithmetic and copies ran while one was open for 0% -> 0% of each run, Pallas kernels for 14% -> 15%
where the time goes in v10:
time: 19.8 us; the launch traced here: 19.4 us
  starting transfers between devices  11.9 us (60%)
  Pallas kernels  5.19 us (26%)
  blocking collectives  2.17 us (11%)
    ppermute x11, starting transfers between devices, permute(): return lax.ppermute(block, ('layer', 'plane'), route)  11.9 us
    pallas_call x9, Pallas kernels, call(): pl.pallas_call(kernel, out_shape=outs, in_specs=[hbm if h else vmem for h...  5.19 us
    all_gather x1, blocking collectives, with_mate(): return lax.all_gather(block, 'layer', axis_index_groups=groups)  2.17 us
  transfers between devices with their start and end apart: 11, of which 0 were waited for; matrix products, arithmetic and copies ran while one was open for 0% of the time, Pallas kernels for 15%

profile of v10, /device:TPU:3, one launch (start us, length us, event | category | flops | bytes accessed | tf_op | source)
XLA Modules:
  0.0 19.4 jit_solution(16175326664880744010)
XLA Ops:
  0.0 1.1 %shard_map.56 = (f32[2,2,128,128]{3,2,1,0:T(8,128)S(1)}, f32[1,2,128,128]{3,2,1,0:T(8,128)S(1)}, f32[1,2,128,128]{3,2,1,0:T(8,128)S(1)}) custom-call(s32[2]{0:T(128)} %bitcast.14, bf16[2,2,128,128]{3,2,1,0:T(8,128)(2,1)} %bitcast.9), custom_call_target="tpu_custom_call" | custom-call | flops 99999997952 | bytes 100000000 | tf_op jit(solution)/shard_map/pallas_call | solution.py:336
  1.1 0.0 copy-start.1
  1.1 0.7 %collective-permute-start = (f32[2,2,128,128]{3,2,1,0:T(8,128)S(1)}, f32[2,2,128,128]{3,2,1,0:T(8,128)S(1)}, u32[]{:S(2)}, u32[]{:S(2)}) collective-permute-start(f32[2,2,128,128]{3,2,1,0:T(8,128)S(1)} %get-tuple-element.24), channel_id=1, source_target_pairs={{0,4},{1,5},{2,6},{3,7},{4,0},{5,1},{6,2},{7,3},{8,12},{9,13},{10,... | collective-permute-start | bytes 786440 | tf_op jit(solution)/shard_map/ppermute | solution.py:46
  1.9 1.2 %collective-permute-start.3 = (f32[2,2,128,128]{3,2,1,0:T(8,128)S(1)}, f32[2,2,128,128]{3,2,1,0:T(8,128)S(1)}, u32[]{:S(2)}, u32[]{:S(2)}) collective-permute-start(f32[2,2,128,128]{3,2,1,0:T(8,128)S(1)} %get-tuple-element.24), channel_id=1, source_target_pairs={{0,4},{1,5},{2,6},{3,7},{4,8},{5,9},{6,10},{7,11},{8,12},{9,13},{1... | collective-permute-start | bytes 786440 | tf_op jit(solution)/shard_map/ppermute | solution.py:46
  3.0 0.0 collective-permute-start.1
  3.0 1.7 %collective-permute-start.2 = (f32[1,2,128,128]{3,2,1,0:T(8,128)S(1)}, f32[1,2,128,128]{3,2,1,0:T(8,128)S(1)}, u32[]{:S(2)}, u32[]{:S(2)}) collective-permute-start(f32[1,2,128,128]{3,2,1,0:T(8,128)S(1)} %get-tuple-element.26), channel_id=1, source_target_pairs={{0,4},{1,6},{2,5},{3,7},{4,0},{5,1},{6,2},{7,3},{8,12},{9,14},{10,... | collective-permute-start | bytes 393224 | tf_op jit(solution)/shard_map/ppermute | solution.py:46
  4.7 1.1 %collective-permute-start.5 = (f32[1,2,128,128]{3,2,1,0:T(8,128)S(1)}, f32[1,2,128,128]{3,2,1,0:T(8,128)S(1)}, u32[]{:S(2)}, u32[]{:S(2)}) collective-permute-start(f32[1,2,128,128]{3,2,1,0:T(8,128)S(1)} %get-tuple-element.26), channel_id=1, source_target_pairs={{0,4},{1,5},{2,6},{3,7},{4,8},{5,10},{6,9},{7,11},{8,12},{9,13},{1... | collective-permute-start | bytes 393224 | tf_op jit(solution)/shard_map/ppermute | solution.py:46
  5.8 0.0 collective-permute-done.all_ref.first_ref
  5.9 1.1 %collective-permute-start.4 = (f32[1,2,128,128]{3,2,1,0:T(8,128)S(1)}, f32[1,2,128,128]{3,2,1,0:T(8,128)S(1)}, u32[]{:S(2)}, u32[]{:S(2)}) collective-permute-start(f32[1,2,128,128]{3,2,1,0:T(8,128)S(1)} %shard_map.59), channel_id=1, source_target_pairs={{0,4},{1,5},{2,6},{3,7},{4,9},{5,8},{6,11},{7,10},{8,12},{9,13},{1... | collective-permute-start | bytes 393224 | tf_op jit(solution)/shard_map/ppermute | solution.py:46
  6.9 1.6 %shard_map.55 = (bf16[512,1536]{1,0:T(8,128)(2,1)S(1)}, f32[2,2,128,128]{3,2,1,0:T(8,128)S(1)}, f32[2,1,2,8,128]{4,3,2,1,0:T(8,128)S(1)}) custom-call(s32[24]{0:T(128)} %bitcast.12, s32[24]{0:T(128)} %bitcast.13, s32[2]{0:T(128)} %bitcast.15, bf16[2,2,128,128]{3,2,1,0:T(8,128)(2,1)} %bitcast.10, f32[24,2,128,128]{3,2,1,0:T(8,128)S(1)} %bitcast.7), custom_call_target="tpu_custom_call" | custom-call | flops 201326592 | bytes 5128392 | tf_op jit(solution)/shard_map/pallas_call | solution.py:336
  8.5 0.0 collective-permute-done.1.even_ref
  8.5 0.0 collective-permute-done.2.odd_ref
  8.5 0.5 %shard_map.57 = (f32[2,2,128,128]{3,2,1,0:T(8,128)S(1)}, f32[1,2,128,128]{3,2,1,0:T(8,128)S(1)}, f32[1,2,128,128]{3,2,1,0:T(8,128)S(1)}) custom-call(f32[2,1,2,8,128]{4,3,2,1,0:T(8,128)S(1)} %get-tuple-element.22.mask_ref, bf16[512,1536]{1,0:T(8,128)(2,1)S(1)} %get-tuple-element.21.matrix_ref, f32[2,2,128,128]{3,2,1,0:T(8,128)S(1)} %get-tuple-element.23.own_ref, ...), custom_call_target="tpu_custom_call" | custom-call | flops 201326592 | bytes 2899968 | tf_op jit(solution)/shard_map/pallas_call | solution.py:336
  9.0 0.1 collective-permute-start.6
  9.1 4.2 %collective-permute-start.7 = (f32[1,2,128,128]{3,2,1,0:T(8,128)S(1)}, f32[1,2,128,128]{3,2,1,0:T(8,128)S(1)}, u32[]{:S(2)}, u32[]{:S(2)}) collective-permute-start(f32[1,2,128,128]{3,2,1,0:T(8,128)S(1)} %get-tuple-element.31), channel_id=1, source_target_pairs={{0,4},{1,5},{2,6},{3,7},{4,9},{5,8},{6,11},{7,10},{8,12},{9,13},{1... | collective-permute-start | bytes 393224 | tf_op jit(solution)/shard_map/ppermute | solution.py:46
  13.3 0.4 %shard_map.58 = (f32[2,2,128,128]{3,2,1,0:T(8,128)S(1)}, f32[1,2,128,128]{3,2,1,0:T(8,128)S(1)}) custom-call(bf16[512,1536]{1,0:T(8,128)(2,1)S(1)} %get-tuple-element.21.matrix_ref, bf16[2,2,128,128]{3,2,1,0:T(8,128)(2,1)S(1)} %bitcast.11, f32[2,2,128,128]{3,2,1,0:T(8,128)S(1)} %get-tuple-element.27.trace_ref.known_ref, ...), custom_call_target="tpu_custom_call" | custom-call | flops 201326592 | bytes 2490368 | tf_op jit(solution)/shard_map/pallas_call | solution.py:336
  13.7 0.0 collective-permute-done.5.odd_ref
  13.7 0.1 collective-permute-start.8
  13.7 0.0 collective-permute-done.3.all_ref
  13.8 0.0 collective-permute-done.4.even_ref
  13.8 0.1 shard_map.60
  13.8 0.9 %collective-permute-start.9 = (f32[1,2,128,128]{3,2,1,0:T(8,128)S(1)}, f32[1,2,128,128]{3,2,1,0:T(8,128)S(1)}, u32[]{:S(2)}, u32[]{:S(2)}) collective-permute-start(f32[1,2,128,128]{3,2,1,0:T(8,128)S(1)} %get-tuple-element.34), channel_id=1, source_target_pairs={{0,5},{1,4},{2,7},{3,6},{4,0},{5,1},{6,2},{7,3},{8,13},{9,12},{10,... | collective-permute-start | bytes 393224 | tf_op jit(solution)/shard_map/ppermute | solution.py:46
  14.8 0.9 %collective-permute-start.10 = (f32[1,2,128,128]{3,2,1,0:T(8,128)S(1)}, f32[1,2,128,128]{3,2,1,0:T(8,128)S(1)}, u32[]{:S(2)}, u32[]{:S(2)}) collective-permute-start(f32[1,2,128,128]{3,2,1,0:T(8,128)S(1)} %get-tuple-element.35), channel_id=1, source_target_pairs={{0,4},{1,6},{2,5},{3,7},{4,0},{5,1},{6,2},{7,3},{8,12},{9,14},{10,... | collective-permute-start | bytes 393224 | tf_op jit(solution)/shard_map/ppermute | solution.py:46
  15.7 2.2 %all-gather = f32[4,2,128,128]{3,2,1,0:T(8,128)S(1)} all-gather(f32[2,2,128,128]{3,2,1,0:T(8,128)S(1)} %get-tuple-element.30.trace_ref), channel_id=2, replica_groups={{0,4},{8,12},{16,20},{24,28},{1,5},{9,13},{17,21},{25,29},{2,6},{10,14}..., dimensions={0}, use_global_device_ids=true | all-gather | bytes 786432 | tf_op jit(solution)/shard_map/all_gather | solution.py:54
  17.8 0.4 %shard_map.61.base_ref = f32[2,2,128,128]{3,2,1,0:T(8,128)S(1)} custom-call(bf16[512,1536]{1,0:T(8,128)(2,1)S(1)} %get-tuple-element.21.matrix_ref, f32[2,2,128,128]{3,2,1,0:T(8,128)S(1)} %get-tuple-element.29.base_ref, f32[2,2,128,128]{3,2,1,0:T(8,128)S(1)} %get-tuple-element.30.trace_ref, f32[2,2,2,128,128]{4,3,2,1,0:T(8,128)S(1)} %bitcast.8), custom_call_target="tpu_custom_call" | custom-call | flops 201326592 | bytes 2883584 | tf_op jit(solution)/shard_map/pallas_call | solution.py:336
  18.2 0.0 collective-permute-done.7.even_ref
  18.2 0.0 collective-permute-done.6.all_ref
  18.2 0.1 shard_map.62
  18.3 0.0 collective-permute-done.8.outer_odd_ref
  18.3 0.0 collective-permute-done.9.inner_even_ref
  18.3 0.0 collective-permute-done.10.inner_odd_ref
  18.3 1.1 %shard_map.63 = f32[2,2,128,128]{3,2,1,0:T(8,128)} custom-call(bf16[512,1536]{1,0:T(8,128)(2,1)S(1)} %get-tuple-element.21.matrix_ref, f32[2,2,128,128]{3,2,1,0:T(8,128)S(1)} %get-tuple-element.32.base_ref, f32[1,2,128,128]{3,2,1,0:T(8,128)S(1)} %collective-permute-done.8.outer_odd_ref, ...), custom_call_target="tpu_custom_call", output_to_operand_aliasing={{}: (5, {})} | custom-call | flops 201326592 | bytes 2752512 | tf_op jit(solution)/shard_map/pallas_call | solution.py:336
  (4 shorter events, 0.0 us)
Async XLA Ops:
  0.0 6.9 %copy-start = (f32[1,24,2,128,128]{4,3,2,1,0:T(8,128)S(1)}, f32[1,24,2,128,128]{4,3,2,1,0:T(8,128)}, u32[]{:S(2)}) copy-start(f32[1,24,2,128,128]{4,3,2,1,0:T(8,128)} %param.6) | copy-start | bytes 9437188
  1.1 12.1 %copy-start.1 = (bf16[1,2,2,128,128]{4,3,2,1,0:T(8,128)(2,1)S(1)}, bf16[1,2,2,128,128]{4,3,2,1,0:T(8,128)(2,1)}, u32[]{:S(2)}) copy-start(bf16[1,2,2,128,128]{4,3,2,1,0:T(8,128)(2,1)} %param.5) | copy-start | bytes 393220
  1.1 4.7 %collective-permute-start = (f32[2,2,128,128]{3,2,1,0:T(8,128)S(1)}, f32[2,2,128,128]{3,2,1,0:T(8,128)S(1)}, u32[]{:S(2)}, u32[]{:S(2)}) collective-permute-start(f32[2,2,128,128]{3,2,1,0:T(8,128)S(1)} %get-tuple-element.24), channel_id=1, source_target_pairs={{0,4},{1,5},{2,6},{3,7},{4,0},{5,1},{6,2},{7,3},{8,12},{9,13},{10,... | collective-permute-start | bytes 786440 | tf_op jit(solution)/shard_map/ppermute | solution.py:46
  1.9 11.9 %collective-permute-start.3 = (f32[2,2,128,128]{3,2,1,0:T(8,128)S(1)}, f32[2,2,128,128]{3,2,1,0:T(8,128)S(1)}, u32[]{:S(2)}, u32[]{:S(2)}) collective-permute-start(f32[2,2,128,128]{3,2,1,0:T(8,128)S(1)} %get-tuple-element.24), channel_id=1, source_target_pairs={{0,4},{1,5},{2,6},{3,7},{4,8},{5,9},{6,10},{7,11},{8,12},{9,13},{1... | collective-permute-start | bytes 786440 | tf_op jit(solution)/shard_map/ppermute | solution.py:46
  3.0 5.5 %collective-permute-start.1 = (f32[1,2,128,128]{3,2,1,0:T(8,128)S(1)}, f32[1,2,128,128]{3,2,1,0:T(8,128)S(1)}, u32[]{:S(2)}, u32[]{:S(2)}) collective-permute-start(f32[1,2,128,128]{3,2,1,0:T(8,128)S(1)} %get-tuple-element.25.payload_ref), channel_id=1, source_target_pairs={{0,5},{1,4},{2,7},{3,6},{4,0},{5,1},{6,2},{7,3},{8,13},{9,12},{10,... | collective-permute-start | bytes 393224 | tf_op jit(solution)/shard_map/ppermute | solution.py:46
  3.0 5.5 %collective-permute-start.2 = (f32[1,2,128,128]{3,2,1,0:T(8,128)S(1)}, f32[1,2,128,128]{3,2,1,0:T(8,128)S(1)}, u32[]{:S(2)}, u32[]{:S(2)}) collective-permute-start(f32[1,2,128,128]{3,2,1,0:T(8,128)S(1)} %get-tuple-element.26), channel_id=1, source_target_pairs={{0,4},{1,6},{2,5},{3,7},{4,0},{5,1},{6,2},{7,3},{8,12},{9,14},{10,... | collective-permute-start | bytes 393224 | tf_op jit(solution)/shard_map/ppermute | solution.py:46
  4.7 8.9 %collective-permute-start.5 = (f32[1,2,128,128]{3,2,1,0:T(8,128)S(1)}, f32[1,2,128,128]{3,2,1,0:T(8,128)S(1)}, u32[]{:S(2)}, u32[]{:S(2)}) collective-permute-start(f32[1,2,128,128]{3,2,1,0:T(8,128)S(1)} %get-tuple-element.26), channel_id=1, source_target_pairs={{0,4},{1,5},{2,6},{3,7},{4,8},{5,10},{6,9},{7,11},{8,12},{9,13},{1... | collective-permute-start | bytes 393224 | tf_op jit(solution)/shard_map/ppermute | solution.py:46
  5.9 7.9 %collective-permute-start.4 = (f32[1,2,128,128]{3,2,1,0:T(8,128)S(1)}, f32[1,2,128,128]{3,2,1,0:T(8,128)S(1)}, u32[]{:S(2)}, u32[]{:S(2)}) collective-permute-start(f32[1,2,128,128]{3,2,1,0:T(8,128)S(1)} %shard_map.59), channel_id=1, source_target_pairs={{0,4},{1,5},{2,6},{3,7},{4,9},{5,8},{6,11},{7,10},{8,12},{9,13},{1... | collective-permute-start | bytes 393224 | tf_op jit(solution)/shard_map/ppermute | solution.py:46
  9.0 9.2 %collective-permute-start.6 = (f32[2,2,128,128]{3,2,1,0:T(8,128)S(1)}, f32[2,2,128,128]{3,2,1,0:T(8,128)S(1)}, u32[]{:S(2)}, u32[]{:S(2)}) collective-permute-start(f32[2,2,128,128]{3,2,1,0:T(8,128)S(1)} %get-tuple-element.27.trace_ref.known_ref), channel_id=1, source_target_pairs={{0,4},{1,5},{2,6},{3,7},{4,8},{5,9},{6,10},{7,11},{8,12},{9,13},{1... | collective-permute-start | bytes 786440 | tf_op jit(solution)/shard_map/ppermute | solution.py:46
  9.1 9.1 %collective-permute-start.7 = (f32[1,2,128,128]{3,2,1,0:T(8,128)S(1)}, f32[1,2,128,128]{3,2,1,0:T(8,128)S(1)}, u32[]{:S(2)}, u32[]{:S(2)}) collective-permute-start(f32[1,2,128,128]{3,2,1,0:T(8,128)S(1)} %get-tuple-element.31), channel_id=1, source_target_pairs={{0,4},{1,5},{2,6},{3,7},{4,9},{5,8},{6,11},{7,10},{8,12},{9,13},{1... | collective-permute-start | bytes 393224 | tf_op jit(solution)/shard_map/ppermute | solution.py:46
  13.7 4.6 %collective-permute-start.8 = (f32[1,2,128,128]{3,2,1,0:T(8,128)S(1)}, f32[1,2,128,128]{3,2,1,0:T(8,128)S(1)}, u32[]{:S(2)}, u32[]{:S(2)}) collective-permute-start(f32[1,2,128,128]{3,2,1,0:T(8,128)S(1)} %get-tuple-element.33), channel_id=1, source_target_pairs={{0,4},{1,5},{2,6},{3,7},{4,8},{5,10},{6,9},{7,11},{8,12},{9,13},{1... | collective-permute-start | bytes 393224 | tf_op jit(solution)/shard_map/ppermute | solution.py:46
  13.8 4.5 %collective-permute-start.9 = (f32[1,2,128,128]{3,2,1,0:T(8,128)S(1)}, f32[1,2,128,128]{3,2,1,0:T(8,128)S(1)}, u32[]{:S(2)}, u32[]{:S(2)}) collective-permute-start(f32[1,2,128,128]{3,2,1,0:T(8,128)S(1)} %get-tuple-element.34), channel_id=1, source_target_pairs={{0,5},{1,4},{2,7},{3,6},{4,0},{5,1},{6,2},{7,3},{8,13},{9,12},{10,... | collective-permute-start | bytes 393224 | tf_op jit(solution)/shard_map/ppermute | solution.py:46
  14.8 3.5 %collective-permute-start.10 = (f32[1,2,128,128]{3,2,1,0:T(8,128)S(1)}, f32[1,2,128,128]{3,2,1,0:T(8,128)S(1)}, u32[]{:S(2)}, u32[]{:S(2)}) collective-permute-start(f32[1,2,128,128]{3,2,1,0:T(8,128)S(1)} %get-tuple-element.35), channel_id=1, source_target_pairs={{0,4},{1,6},{2,5},{3,7},{4,0},{5,1},{6,2},{7,3},{8,12},{9,14},{10,... | collective-permute-start | bytes 393224 | tf_op jit(solution)/shard_map/ppermute | solution.py:46
